TPU v7x, 512 devices: a whole 4x4x16 slice. The times are simulated.
512 devices in a mesh: gx: 8 (over z_lo, core), gy: 4 (over z_hi), gz: 16 (over x, y).
Axes of the slice: x: 4, y: 4, z: 16 (z_hi: 4, z_lo: 4; z = z_hi * 4 + z_lo), core: 2. Of those that a mesh axis runs over, the one named last changes fastest.
Arguments:
- particles: float32 [28, 1048576], P(None, ('gx', 'gy', 'gz')), may hold values from -3 to 3, as said below
- stencil_base: int32 [3, 1048576], P(None, ('gx', 'gy', 'gz')), may hold values from 0 to 32, as said below
- weights: float32 [8, 1048576], P(None, ('gx', 'gy', 'gz')), may hold values from 0.02 to 0.25
- gradients: float32 [3, 8, 1048576], P(None, None, ('gx', 'gy', 'gz')), may hold values from -4 to 4
- counts: int32 [512], P(('gx', 'gy', 'gz')), may hold values from 0 to 8, as said below
Outputs:
- migrated: float32 [28, 1572864], P(None, ('gx', 'gy', 'gz'))
- damage: float32 [64, 64, 512], P('gx', 'gy', 'gz')
Inputs may be any that keep to these rules, and one draw needn't show every extreme that they name: `particles`: mass and volume in 0.5 to 2, deformation gradient entries within 0.1 of the identity's, damage in 0 to 0.5, history in 0.05 to 1. `stencil_base`: row 0 lies in 0 to 8, row 1 in 0 to 16, row 2 in 0 to 32. `counts`: some device hands exactly 8 bins.
All inputs are finite; a program needn't handle non-finite values.
Results may differ from a plain program's by a relative error of at most 0.0003.
Values sent between devices are 32-bit elements; how exact they have to be, the bound alone decides.
No kernel may reach another device: no remote copies, remote signals or barrier semaphores. Data moves between devices by JAX's collectives and lax.ppermute only.
A program may use at most 64 MiB of HBM per device.

v0:
```python
import jax
import jax.numpy as jnp
from jax import lax
from jax.sharding import PartitionSpec as P

CX = 8
CY = 16
CZ = 32
NBIN = 16
BIN = 128
SUBSTEPS = 4
MOST = 8


time_step = 0.1
relax_rate = 0.2
length_sq = 0.6
shear_mod = 1.0
bulk_coef = 1.5
mass_floor = 0.5


def with_halo(value, sides, width):
    for axis, dim in sides:
        count, length = (lax.axis_size(axis), value.shape[dim])
        up = [(i, (i + 1) % count) for i in range(count - 1)]
        down = [(j, i) for i, j in up]
        last = lax.slice_in_dim(value, length - width, length, axis=dim)
        leading = lax.slice_in_dim(value, 0, width, axis=dim)
        before = lax.ppermute(last, axis, up)
        after = lax.ppermute(leading, axis, down)
        value = jnp.concatenate([before, value, after], axis=dim)
    return value


def passed_along(value, axis, by):
    count = lax.axis_size(axis)
    return lax.ppermute(value, axis, [(i, (i + by) % count) for i in range(count)])


def corner_offsets(corner):
    return (corner >> 2 & 1, corner >> 1 & 1, corner & 1)


def node_terms(particles, weights, gradients, corner):
    volume = particles[1]
    velocity = particles[2:5]
    stress = particles[14:23].reshape(3, 3, -1)
    share = particles[0] * weights[corner]
    slope = gradients[:, corner]
    force = -volume[None] * jnp.sum(stress * slope[None], axis=1)
    return jnp.concatenate(
        [
            share[None],
            share[None] * velocity,
            force,
            (share * particles[23])[None],
            (share * particles[24])[None],
        ],
        axis=0,
    )


def relax(padded, drive):
    centre = padded[1:-1, 1:-1, 1:-1]
    laplace = (
        padded[2:, 1:-1, 1:-1]
        + padded[:-2, 1:-1, 1:-1]
        + padded[1:-1, 2:, 1:-1]
        + padded[1:-1, :-2, 1:-1]
        + padded[1:-1, 1:-1, 2:]
        + padded[1:-1, 1:-1, :-2]
        - 6.0 * centre
    )
    return centre + relax_rate * (length_sq * laplace - centre + 2.0 * (1.0 - centre) * drive)


def advance(particles, near_velocity, near_damage, weights, gradients):
    moved = [jnp.sum(weights * near_velocity[i], axis=0) for i in range(3)]
    velgrad = [
        [jnp.sum(near_velocity[i] * gradients[j], axis=0) for j in range(3)] for i in range(3)
    ]
    damage_node = jnp.sum(weights * near_damage, axis=0)
    deform = [[particles[5 + 3 * i + j] for j in range(3)] for i in range(3)]
    stretch = [
        [(1.0 if i == j else 0.0) + time_step * velgrad[i][j] for j in range(3)] for i in range(3)
    ]
    mapped = [
        [
            stretch[i][0] * deform[0][j]
            + stretch[i][1] * deform[1][j]
            + stretch[i][2] * deform[2][j]
            for j in range(3)
        ]
        for i in range(3)
    ]
    jacobian = (
        mapped[0][0] * (mapped[1][1] * mapped[2][2] - mapped[1][2] * mapped[2][1])
        - mapped[0][1] * (mapped[1][0] * mapped[2][2] - mapped[1][2] * mapped[2][0])
        + mapped[0][2] * (mapped[1][0] * mapped[2][1] - mapped[1][1] * mapped[2][0])
    )
    left = [
        [
            mapped[i][0] * mapped[j][0] + mapped[i][1] * mapped[j][1] + mapped[i][2] * mapped[j][2]
            for j in range(3)
        ]
        for i in range(3)
    ]
    damaged = jnp.maximum(particles[23], damage_node)
    degrade = (1.0 - damaged) ** 2
    rows_out = []
    for i in range(3):
        for j in range(3):
            term = shear_mod * (left[i][j] - (1.0 if i == j else 0.0))
            if i == j:
                term = term + bulk_coef * (jacobian - 1.0)
            rows_out.append(degrade * term)
    energy = (
        0.5 * shear_mod * (left[0][0] + left[1][1] + left[2][2] - 3.0)
        + 0.5 * bulk_coef * (jacobian - 1.0) ** 2
    )
    history = jnp.maximum(particles[24], energy)
    position = particles[25:28] + time_step * jnp.stack(moved)
    flat_mapped = jnp.stack([mapped[i][j] for i in range(3) for j in range(3)])
    return jnp.concatenate(
        [
            particles[0:2],
            jnp.stack(moved),
            flat_mapped,
            jnp.stack(rows_out),
            damaged[None],
            history[None],
            position,
        ],
        axis=0,
    )


def fold_rims(array, dim):
    size = array.shape[dim]
    inner = lax.slice_in_dim(array, 2, size - 2, axis=dim)
    lower = lax.slice_in_dim(array, 0, 1, axis=dim)
    upper = lax.slice_in_dim(array, size - 1, size, axis=dim)
    widths_low = [(0, 0)] * array.ndim
    widths_high = [(0, 0)] * array.ndim
    widths_low[dim] = (0, size - 5)
    widths_high[dim] = (size - 5, 0)
    return inner + jnp.pad(lower, widths_low) + jnp.pad(upper, widths_high)


def inside_line(index, devices, cells, margin):
    position = index * cells + jnp.arange(cells + 2 * margin, dtype=jnp.int32) - margin
    return ((position >= 0) & (position < devices * cells)).astype(jnp.float32)


def per_device(particles, stencil_base, weights, gradients, counts):
    span_x = CX + 2
    span_y = CY + 2
    span_z = CZ + 2
    count = particles.shape[1]
    flats = []
    terms = []
    for corner in range(8):
        offset_x, offset_y, offset_z = corner_offsets(corner)
        flat_index = (
            ((stencil_base[0] + offset_x) * span_y + stencil_base[1] + offset_y) * span_z
            + stencil_base[2]
            + offset_z
        )
        flats.append(flat_index)
        terms.append(node_terms(particles, weights, gradients, corner))
    all_index = jnp.concatenate(flats)
    grid_sum = (
        jnp.zeros((9, span_x * span_y * span_z), jnp.float32)
        .at[:, all_index]
        .add(jnp.concatenate(terms, axis=1))
    )
    extended = grid_sum.reshape(9, span_x, span_y, span_z)
    owned = fold_rims(with_halo(extended, (("gx", 1),), 1), 1)
    owned = fold_rims(with_halo(owned, (("gy", 2),), 1), 2)
    owned = fold_rims(with_halo(owned, (("gz", 3),), 1), 3)
    masses = jnp.maximum(owned[0], mass_floor)
    velocity = (owned[1:4] + time_step * owned[4:7]) / masses[None]
    damage = owned[7] / masses
    drive = owned[8] / masses
    deep = with_halo(jnp.stack([damage, drive]), (("gx", 1), ("gy", 2), ("gz", 3)), SUBSTEPS)
    line_x = inside_line(lax.axis_index("gx"), lax.axis_size("gx"), CX, SUBSTEPS)
    line_y = inside_line(lax.axis_index("gy"), lax.axis_size("gy"), CY, SUBSTEPS)
    line_z = inside_line(lax.axis_index("gz"), lax.axis_size("gz"), CZ, SUBSTEPS)
    inside = line_x[:, None, None] * line_y[None, :, None] * line_z[None, None, :]
    current = deep[0]
    for step in range(SUBSTEPS):
        trim = step + 1
        local_drive = deep[1][trim:-trim, trim:-trim, trim:-trim]
        current = relax(current, local_drive) * inside[trim:-trim, trim:-trim, trim:-trim]
    damage = current
    fields = jnp.concatenate([velocity, damage[None]], axis=0)
    near_all = with_halo(fields, (("gx", 1), ("gy", 2), ("gz", 3)), 1).reshape(4, -1)
    near = near_all[:, all_index].reshape(4, 8, count)
    updated = advance(particles, near[0:3], near[3], weights, gradients)
    tail = updated[:, (NBIN - MOST) * BIN :]
    sent_count = counts.astype(jnp.float32)
    recv_tail, recv_count = passed_along((tail, sent_count), "gz", 1)
    prior = recv_count[0].astype(jnp.int32)
    own_count = counts[0]
    buffer_all = jnp.concatenate(
        [recv_tail, updated, jnp.zeros((updated.shape[0], MOST * BIN), updated.dtype)], axis=1
    )
    start = (MOST - prior) * BIN
    window = lax.dynamic_slice_in_dim(buffer_all, start, (NBIN + MOST) * BIN, 1)
    live = (NBIN - own_count + prior) * BIN
    slot = jnp.arange((NBIN + MOST) * BIN, dtype=jnp.int32)
    migrated = jnp.where(slot[None, :] < live, window, jnp.zeros_like(window))
    return (migrated, damage)


def solution(mesh):
    return jax.shard_map(
        per_device,
        mesh=mesh,
        in_specs=(
            P(None, ("gx", "gy", "gz")),
            P(None, ("gx", "gy", "gz")),
            P(None, ("gx", "gy", "gz")),
            P(None, None, ("gx", "gy", "gz")),
            P(("gx", "gy", "gz")),
        ),
        out_specs=(P(None, ("gx", "gy", "gz")), P("gx", "gy", "gz")),
        check_vma=False,
    )
```

profile of v0, /device:TPU:1, one launch (start us, length us, event | category | flops | bytes accessed | tf_op | source)
XLA Modules:
  0.0 327.6 jit_solution(2704971420648264009)
XLA Ops:
  3.8 2.0 fusion.51
  9.2 4.7 %copy.15 = f32[16384,9]{1,0:T(8,128)} copy(f32[16384,9]{0,1:T(8,128)S(1)} %bitcast.101) | data formatting | bytes 1179648 | tf_op jit(solution)/shard_map/concatenate | solution.py:176
  14.8 88.4 %scatter_custom_fusion = f32[9,6120]{0,1:T(8,128)S(1)} fusion(s32[16384]{0:T(1024)S(1)} %bitcast.102, f32[16384,9]{1,0:T(8,128)} %copy.15, f32[]{:T(128)} %constant.34.clone.1), kind=kCustom, calls=%fused_computation.6 | custom fusion | flops 147456 | bytes 220832 | tf_op jit(solution)/shard_map/scatter-add | solution.py:176
  103.2 1.5 copy.16
  105.3 4.9 %collective-permute-start.1 = (f32[9,1,18,34]{3,2,1,0:T(8,128)S(1)}, f32[9,1,18,34]{3,2,1,0:T(8,128)S(1)}, u32[]{:S(2)}, u32[]{:S(2)}) collective-permute-start(f32[9,1,18,34]{3,2,1,0:T(8,128)S(1)} %get-tuple-element.64), channel_id=1, source_target_pairs={{0,64},{64,128},{128,192},{192,256},{256,320},{320,384},{384,448},... | collective-permute-start | bytes 66104 | tf_op jit(solution)/shard_map/ppermute | solution.py:30
  110.2 5.1 %collective-permute-start.2 = (f32[9,1,18,34]{3,2,1,0:T(8,128)S(1)}, f32[9,1,18,34]{3,2,1,0:T(8,128)S(1)}, u32[]{:S(2)}, u32[]{:S(2)}) collective-permute-start(f32[9,1,18,34]{3,2,1,0:T(8,128)S(1)} %get-tuple-element.65), channel_id=1, source_target_pairs={{64,0},{128,64},{192,128},{256,192},{320,256},{384,320},{448,384},... | collective-permute-start | bytes 66104 | tf_op jit(solution)/shard_map/ppermute | solution.py:31
  116.5 8.8 %collective-permute-start.3 = (f32[9,8,1,34]{3,2,1,0:T(1,128)S(1)}, f32[9,8,1,34]{3,2,1,0:T(1,128)S(1)}, u32[]{:S(2)}, u32[]{:S(2)}) collective-permute-start(f32[9,8,1,34]{3,2,1,0:T(1,128)S(1)} %get-tuple-element.66), channel_id=1, source_target_pairs={{0,16},{16,32},{32,48},{1,17},{17,33},{33,49},{2,18},{18,34},{34,5... | collective-permute-start | bytes 29384 | tf_op jit(solution)/shard_map/ppermute | solution.py:30
  126.6 9.1 %collective-permute-done.4 = f32[9,8,1,34]{3,2,1,0:T(1,128)S(1)} collective-permute-done((f32[9,8,1,34]{3,2,1,0:T(1,128)S(1)}, f32[9,8,1,34]{3,2,1,0:T(1,128)S(1)}, u32[]{:S(2)}, u32[]{:S(2)}) %collective-permute-start.4) | collective-permute-done | bytes 9824 | tf_op jit(solution)/shard_map/ppermute | solution.py:31
  136.6 3.2 collective-permute-start.5
  142.2 2.8 collective-permute-done.6
  145.9 3.3 %collective-permute-start.7 = (f32[2,4,16,32]{3,2,1,0:T(8,128)S(1)}, f32[2,4,16,32]{3,2,1,0:T(8,128)S(1)}, u32[]{:S(2)}, u32[]{:S(2)}) collective-permute-start(f32[2,4,16,32]{3,2,1,0:T(8,128)S(1)} %get-tuple-element.122), channel_id=1, source_target_pairs={{0,64},{64,128},{128,192},{192,256},{256,320},{320,384},{384,448},... | collective-permute-start | bytes 49160 | tf_op jit(solution)/shard_map/ppermute | solution.py:30
  149.2 1.9 collective-permute-start.8
  151.2 3.6 %collective-permute-done.8 = f32[2,4,16,32]{3,2,1,0:T(8,128)S(1)} collective-permute-done((f32[2,4,16,32]{3,2,1,0:T(8,128)S(1)}, f32[2,4,16,32]{3,2,1,0:T(8,128)S(1)}, u32[]{:S(2)}, u32[]{:S(2)}) %collective-permute-start.8) | collective-permute-done | bytes 16416 | tf_op jit(solution)/shard_map/ppermute | solution.py:31
  156.1 9.8 %collective-permute-start.9 = (f32[2,16,4,32]{3,2,1,0:T(4,128)S(1)}, f32[2,16,4,32]{3,2,1,0:T(4,128)S(1)}, u32[]{:S(2)}, u32[]{:S(2)}) collective-permute-start(f32[2,16,4,32]{3,2,1,0:T(4,128)S(1)} %get-tuple-element.95), channel_id=1, source_target_pairs={{0,16},{16,32},{32,48},{1,17},{17,33},{33,49},{2,18},{18,34},{34,5... | collective-permute-start | bytes 49160 | tf_op jit(solution)/shard_map/ppermute | solution.py:30
  166.1 2.8 collective-permute-done.10
  169.1 3.2 collective-permute-start.11
  173.7 4.9 %collective-permute-done.11 = f32[2,16,24,4]{3,2,1,0:T(8,128)S(1)} collective-permute-done((f32[2,16,24,4]{3,2,1,0:T(8,128)S(1)}, f32[2,16,24,4]{3,2,1,0:T(8,128)S(1)}, u32[]{:S(2)}, u32[]{:S(2)}) %collective-permute-start.11) | collective-permute-done | bytes 12320 | tf_op jit(solution)/shard_map/ppermute | solution.py:30
  178.6 4.1 %collective-permute-done.12 = f32[2,16,24,4]{3,2,1,0:T(8,128)S(1)} collective-permute-done((f32[2,16,24,4]{3,2,1,0:T(8,128)S(1)}, f32[2,16,24,4]{3,2,1,0:T(8,128)S(1)}, u32[]{:S(2)}, u32[]{:S(2)}) %collective-permute-start.12) | collective-permute-done | bytes 12320 | tf_op jit(solution)/shard_map/ppermute | solution.py:31
  184.4 5.5 %collective-permute-start.13 = (f32[4,1,16,32]{3,2,1,0:T(8,128)S(1)}, f32[4,1,16,32]{3,2,1,0:T(8,128)S(1)}, u32[]{:S(2)}, u32[]{:S(2)}) collective-permute-start(f32[4,1,16,32]{3,2,1,0:T(8,128)S(1)} %get-tuple-element.93), channel_id=1, source_target_pairs={{0,64},{64,128},{128,192},{192,256},{256,320},{320,384},{384,448},... | collective-permute-start | bytes 24584 | tf_op jit(solution)/shard_map/ppermute | solution.py:30
  190.0 1.9 collective-permute-start.14
  191.9 3.3 %collective-permute-done.14 = f32[4,1,16,32]{3,2,1,0:T(8,128)S(1)} collective-permute-done((f32[4,1,16,32]{3,2,1,0:T(8,128)S(1)}, f32[4,1,16,32]{3,2,1,0:T(8,128)S(1)}, u32[]{:S(2)}, u32[]{:S(2)}) %collective-permute-start.14) | collective-permute-done | bytes 8224 | tf_op jit(solution)/shard_map/ppermute | solution.py:31
  195.3 7.6 %collective-permute-start.15 = (f32[4,10,1,32]{3,2,1,0:T(1,128)S(1)}, f32[4,10,1,32]{3,2,1,0:T(1,128)S(1)}, u32[]{:S(2)}, u32[]{:S(2)}) collective-permute-start(f32[4,10,1,32]{3,2,1,0:T(1,128)S(1)} %get-tuple-element.79), channel_id=1, source_target_pairs={{0,16},{16,32},{32,48},{1,17},{17,33},{33,49},{2,18},{18,34},{34,5... | collective-permute-start | bytes 15368 | tf_op jit(solution)/shard_map/ppermute | solution.py:30
  204.8 5.1 %collective-permute-start = (f32[1]{0:T(128)}, f32[1]{0:T(128)}, u32[]{:S(2)}, u32[]{:S(2)}) collective-permute-start(f32[1]{0:T(128)} %convert_element_type.40), channel_id=1, source_target_pairs={{0,1},{1,2},{2,3},{3,4},{4,5},{5,6},{6,7},{7,8},{8,9},{9,10},{10,1... | collective-permute-start | bytes 20 | tf_op jit(solution)/shard_map/ppermute | solution.py:38
  210.0 3.7 %collective-permute-done.16 = f32[4,10,1,32]{3,2,1,0:T(1,128)S(1)} collective-permute-done((f32[4,10,1,32]{3,2,1,0:T(1,128)S(1)}, f32[4,10,1,32]{3,2,1,0:T(1,128)S(1)}, u32[]{:S(2)}, u32[]{:S(2)}) %collective-permute-start.16) | collective-permute-done | bytes 5152 | tf_op jit(solution)/shard_map/ppermute | solution.py:31
  214.0 4.4 %collective-permute-start.17 = (f32[4,10,18,1]{3,2,1,0:T(8,128)S(1)}, f32[4,10,18,1]{3,2,1,0:T(8,128)S(1)}, u32[]{:S(2)}, u32[]{:S(2)}) collective-permute-start(f32[4,10,18,1]{3,2,1,0:T(8,128)S(1)} %get-tuple-element.73), channel_id=1, source_target_pairs={{0,1},{1,2},{2,3},{3,4},{4,5},{5,6},{6,7},{7,8},{8,9},{9,10},{10,1... | collective-permute-start | bytes 8648 | tf_op jit(solution)/shard_map/ppermute | solution.py:30
  220.5 8.1 %collective-permute-done.17 = f32[4,10,18,1]{3,2,1,0:T(8,128)S(1)} collective-permute-done((f32[4,10,18,1]{3,2,1,0:T(8,128)S(1)}, f32[4,10,18,1]{3,2,1,0:T(8,128)S(1)}, u32[]{:S(2)}, u32[]{:S(2)}) %collective-permute-start.17) | collective-permute-done | bytes 2912 | tf_op jit(solution)/shard_map/ppermute | solution.py:30
  228.6 4.1 %collective-permute-done.18 = f32[4,10,18,1]{3,2,1,0:T(8,128)S(1)} collective-permute-done((f32[4,10,18,1]{3,2,1,0:T(8,128)S(1)}, f32[4,10,18,1]{3,2,1,0:T(8,128)S(1)}, u32[]{:S(2)}, u32[]{:S(2)}) %collective-permute-start.18) | collective-permute-done | bytes 2912 | tf_op jit(solution)/shard_map/ppermute | solution.py:31
  233.3 1.6 copy.21
  234.9 54.4 %gather_fusion = f32[16384,4]{1,0:T(8,128)} fusion(f32[4,6120]{0,1:T(8,128)S(1)} %copy.21, s32[16384]{0:T(1024)S(1)} %broadcast_clamp_fusion), kind=kCustom, calls=%fused_computation | custom fusion | bytes 589824 | tf_op jit(solution)/shard_map/gather | solution.py:199
  289.4 26.0 %slice_reduce_fusion = (f32[16384]{0:T(1024)S(1)}, f32[16384]{0:T(1024)S(1)}, f32[16384]{0:T(1024)S(1)}, f32[16384]{0:T(1024)S(1)}) fusion(f32[4,16384]{0,1:T(8,128)} %bitcast.96), kind=kLoop, calls=%fused_computation.2 | loop fusion | bytes 524288 | tf_op jit(solution)/shard_map/slice | solution.py:200
  316.6 3.7 %collective-permute-start.19 = (f32[28,1024]{1,0:T(8,128)S(1)}, f32[28,1024]{1,0:T(8,128)S(1)}, u32[]{:S(2)}, u32[]{:S(2)}) collective-permute-start(f32[28,1024]{1,0:T(8,128)S(1)} %slice.588), channel_id=1, source_target_pairs={{0,1},{1,2},{2,3},{3,4},{4,5},{5,6},{6,7},{7,8},{8,9},{9,10},{10,1... | collective-permute-start | bytes 344072 | tf_op jit(solution)/shard_map/ppermute | solution.py:38
  320.5 6.3 %collective-permute-done.19 = f32[28,1024]{1,0:T(8,128)S(1)} collective-permute-done((f32[28,1024]{1,0:T(8,128)S(1)}, f32[28,1024]{1,0:T(8,128)S(1)}, u32[]{:S(2)}, u32[]{:S(2)}) %collective-permute-start.19) | collective-permute-done | bytes 114720 | tf_op jit(solution)/shard_map/ppermute | solution.py:38
  (127 shorter events, 24.9 us)
Async XLA Ops:
  0.6 13.2 %copy-start.2 = (s32[3,2048]{1,0:T(4,128)S(1)}, s32[3,2048]{1,0:T(4,128)}, u32[]{:S(2)}) copy-start(s32[3,2048]{1,0:T(4,128)} %param.6) | copy-start | bytes 73732
  14.2 0.6 copy-start.5
  105.3 10.1 %collective-permute-start.1 = (f32[9,1,18,34]{3,2,1,0:T(8,128)S(1)}, f32[9,1,18,34]{3,2,1,0:T(8,128)S(1)}, u32[]{:S(2)}, u32[]{:S(2)}) collective-permute-start(f32[9,1,18,34]{3,2,1,0:T(8,128)S(1)} %get-tuple-element.64), channel_id=1, source_target_pairs={{0,64},{64,128},{128,192},{192,256},{256,320},{320,384},{384,448},... | collective-permute-start | bytes 66104 | tf_op jit(solution)/shard_map/ppermute | solution.py:30
  110.2 6.1 %collective-permute-start.2 = (f32[9,1,18,34]{3,2,1,0:T(8,128)S(1)}, f32[9,1,18,34]{3,2,1,0:T(8,128)S(1)}, u32[]{:S(2)}, u32[]{:S(2)}) collective-permute-start(f32[9,1,18,34]{3,2,1,0:T(8,128)S(1)} %get-tuple-element.65), channel_id=1, source_target_pairs={{64,0},{128,64},{192,128},{256,192},{320,256},{384,320},{448,384},... | collective-permute-start | bytes 66104 | tf_op jit(solution)/shard_map/ppermute | solution.py:31
  116.5 10.1 %collective-permute-start.3 = (f32[9,8,1,34]{3,2,1,0:T(1,128)S(1)}, f32[9,8,1,34]{3,2,1,0:T(1,128)S(1)}, u32[]{:S(2)}, u32[]{:S(2)}) collective-permute-start(f32[9,8,1,34]{3,2,1,0:T(1,128)S(1)} %get-tuple-element.66), channel_id=1, source_target_pairs={{0,16},{16,32},{32,48},{1,17},{17,33},{33,49},{2,18},{18,34},{34,5... | collective-permute-start | bytes 29384 | tf_op jit(solution)/shard_map/ppermute | solution.py:30
  125.3 10.4 %collective-permute-start.4 = (f32[9,8,1,34]{3,2,1,0:T(1,128)S(1)}, f32[9,8,1,34]{3,2,1,0:T(1,128)S(1)}, u32[]{:S(2)}, u32[]{:S(2)}) collective-permute-start(f32[9,8,1,34]{3,2,1,0:T(1,128)S(1)} %get-tuple-element.67), channel_id=1, source_target_pairs={{16,0},{32,16},{48,32},{17,1},{33,17},{49,33},{18,2},{34,18},{50,3... | collective-permute-start | bytes 29384 | tf_op jit(solution)/shard_map/ppermute | solution.py:31
  136.6 5.1 %collective-permute-start.5 = (f32[9,8,16,1]{2,1,3,0:T(8,128)S(1)}, f32[9,8,16,1]{2,1,3,0:T(8,128)S(1)}, u32[]{:S(2)}, u32[]{:S(2)}) collective-permute-start(f32[9,8,16,1]{2,1,3,0:T(8,128)S(1)} %copy.17), channel_id=1, source_target_pairs={{0,1},{1,2},{2,3},{3,4},{4,5},{5,6},{6,7},{7,8},{8,9},{9,10},{10,1... | collective-permute-start | bytes 13832 | tf_op jit(solution)/shard_map/ppermute | solution.py:30
  140.3 4.7 %collective-permute-start.6 = (f32[9,8,16,1]{2,1,3,0:T(8,128)S(1)}, f32[9,8,16,1]{2,1,3,0:T(8,128)S(1)}, u32[]{:S(2)}, u32[]{:S(2)}) collective-permute-start(f32[9,8,16,1]{2,1,3,0:T(8,128)S(1)} %copy.19), channel_id=1, source_target_pairs={{1,0},{2,1},{3,2},{4,3},{5,4},{6,5},{7,6},{8,7},{9,8},{10,9},{11,1... | collective-permute-start | bytes 13832 | tf_op jit(solution)/shard_map/ppermute | solution.py:31
  145.5 74.4 %copy-start.6 = (s32[16384,1]{0,1:T(1,128)S(1)}, s32[16384,1]{0,1:T(1,128)}, u32[]{:S(2)}) copy-start(s32[16384,1]{0,1:T(1,128)} %copy-done.5) | copy-start | bytes 196612
  145.9 5.3 %collective-permute-start.7 = (f32[2,4,16,32]{3,2,1,0:T(8,128)S(1)}, f32[2,4,16,32]{3,2,1,0:T(8,128)S(1)}, u32[]{:S(2)}, u32[]{:S(2)}) collective-permute-start(f32[2,4,16,32]{3,2,1,0:T(8,128)S(1)} %get-tuple-element.122), channel_id=1, source_target_pairs={{0,64},{64,128},{128,192},{192,256},{256,320},{320,384},{384,448},... | collective-permute-start | bytes 49160 | tf_op jit(solution)/shard_map/ppermute | solution.py:30
  149.2 5.6 %collective-permute-start.8 = (f32[2,4,16,32]{3,2,1,0:T(8,128)S(1)}, f32[2,4,16,32]{3,2,1,0:T(8,128)S(1)}, u32[]{:S(2)}, u32[]{:S(2)}) collective-permute-start(f32[2,4,16,32]{3,2,1,0:T(8,128)S(1)} %get-tuple-element.123), channel_id=1, source_target_pairs={{64,0},{128,64},{192,128},{256,192},{320,256},{384,320},{448,384},... | collective-permute-start | bytes 49160 | tf_op jit(solution)/shard_map/ppermute | solution.py:31
  154.8 14.0 %collective-permute-start.10 = (f32[2,16,4,32]{3,2,1,0:T(4,128)S(1)}, f32[2,16,4,32]{3,2,1,0:T(4,128)S(1)}, u32[]{:S(2)}, u32[]{:S(2)}) collective-permute-start(f32[2,16,4,32]{3,2,1,0:T(4,128)S(1)} %get-tuple-element.96), channel_id=1, source_target_pairs={{16,0},{32,16},{48,32},{17,1},{33,17},{49,33},{18,2},{34,18},{50,3... | collective-permute-start | bytes 49160 | tf_op jit(solution)/shard_map/ppermute | solution.py:31
  156.1 12.7 %collective-permute-start.9 = (f32[2,16,4,32]{3,2,1,0:T(4,128)S(1)}, f32[2,16,4,32]{3,2,1,0:T(4,128)S(1)}, u32[]{:S(2)}, u32[]{:S(2)}) collective-permute-start(f32[2,16,4,32]{3,2,1,0:T(4,128)S(1)} %get-tuple-element.95), channel_id=1, source_target_pairs={{0,16},{16,32},{32,48},{1,17},{17,33},{33,49},{2,18},{18,34},{34,5... | collective-permute-start | bytes 49160 | tf_op jit(solution)/shard_map/ppermute | solution.py:30
  169.1 9.4 %collective-permute-start.11 = (f32[2,16,24,4]{3,2,1,0:T(8,128)S(1)}, f32[2,16,24,4]{3,2,1,0:T(8,128)S(1)}, u32[]{:S(2)}, u32[]{:S(2)}) collective-permute-start(f32[2,16,24,4]{3,2,1,0:T(8,128)S(1)} %get-tuple-element.77), channel_id=1, source_target_pairs={{0,1},{1,2},{2,3},{3,4},{4,5},{5,6},{6,7},{7,8},{8,9},{9,10},{10,1... | collective-permute-start | bytes 36872 | tf_op jit(solution)/shard_map/ppermute | solution.py:30
  172.3 10.3 %collective-permute-start.12 = (f32[2,16,24,4]{3,2,1,0:T(8,128)S(1)}, f32[2,16,24,4]{3,2,1,0:T(8,128)S(1)}, u32[]{:S(2)}, u32[]{:S(2)}) collective-permute-start(f32[2,16,24,4]{3,2,1,0:T(8,128)S(1)} %get-tuple-element.78), channel_id=1, source_target_pairs={{1,0},{2,1},{3,2},{4,3},{5,4},{6,5},{7,6},{8,7},{9,8},{10,9},{11,1... | collective-permute-start | bytes 36872 | tf_op jit(solution)/shard_map/ppermute | solution.py:31
  184.4 130.9 %copy-start = (f32[8,16,32]{2,1,0:T(8,128)}, f32[8,16,32]{2,1,0:T(8,128)S(1)}, u32[]{:S(2)}) copy-start(f32[8,16,32]{2,1,0:T(8,128)S(1)} %slice_multiply_fusion.7) | copy-start | bytes 49156
  184.4 7.5 %collective-permute-start.13 = (f32[4,1,16,32]{3,2,1,0:T(8,128)S(1)}, f32[4,1,16,32]{3,2,1,0:T(8,128)S(1)}, u32[]{:S(2)}, u32[]{:S(2)}) collective-permute-start(f32[4,1,16,32]{3,2,1,0:T(8,128)S(1)} %get-tuple-element.93), channel_id=1, source_target_pairs={{0,64},{64,128},{128,192},{192,256},{256,320},{320,384},{384,448},... | collective-permute-start | bytes 24584 | tf_op jit(solution)/shard_map/ppermute | solution.py:30
  190.0 5.2 %collective-permute-start.14 = (f32[4,1,16,32]{3,2,1,0:T(8,128)S(1)}, f32[4,1,16,32]{3,2,1,0:T(8,128)S(1)}, u32[]{:S(2)}, u32[]{:S(2)}) collective-permute-start(f32[4,1,16,32]{3,2,1,0:T(8,128)S(1)} %get-tuple-element.94), channel_id=1, source_target_pairs={{64,0},{128,64},{192,128},{256,192},{320,256},{384,320},{448,384},... | collective-permute-start | bytes 24584 | tf_op jit(solution)/shard_map/ppermute | solution.py:31
  195.3 14.7 %collective-permute-start.15 = (f32[4,10,1,32]{3,2,1,0:T(1,128)S(1)}, f32[4,10,1,32]{3,2,1,0:T(1,128)S(1)}, u32[]{:S(2)}, u32[]{:S(2)}) collective-permute-start(f32[4,10,1,32]{3,2,1,0:T(1,128)S(1)} %get-tuple-element.79), channel_id=1, source_target_pairs={{0,16},{16,32},{32,48},{1,17},{17,33},{33,49},{2,18},{18,34},{34,5... | collective-permute-start | bytes 15368 | tf_op jit(solution)/shard_map/ppermute | solution.py:30
  202.9 10.8 %collective-permute-start.16 = (f32[4,10,1,32]{3,2,1,0:T(1,128)S(1)}, f32[4,10,1,32]{3,2,1,0:T(1,128)S(1)}, u32[]{:S(2)}, u32[]{:S(2)}) collective-permute-start(f32[4,10,1,32]{3,2,1,0:T(1,128)S(1)} %get-tuple-element.80), channel_id=1, source_target_pairs={{16,0},{32,16},{48,32},{17,1},{33,17},{49,33},{18,2},{34,18},{50,3... | collective-permute-start | bytes 15368 | tf_op jit(solution)/shard_map/ppermute | solution.py:31
  204.8 15.1 %collective-permute-start = (f32[1]{0:T(128)}, f32[1]{0:T(128)}, u32[]{:S(2)}, u32[]{:S(2)}) collective-permute-start(f32[1]{0:T(128)} %convert_element_type.40), channel_id=1, source_target_pairs={{0,1},{1,2},{2,3},{3,4},{4,5},{5,6},{6,7},{7,8},{8,9},{9,10},{10,1... | collective-permute-start | bytes 20 | tf_op jit(solution)/shard_map/ppermute | solution.py:38
  214.0 14.6 %collective-permute-start.17 = (f32[4,10,18,1]{3,2,1,0:T(8,128)S(1)}, f32[4,10,18,1]{3,2,1,0:T(8,128)S(1)}, u32[]{:S(2)}, u32[]{:S(2)}) collective-permute-start(f32[4,10,18,1]{3,2,1,0:T(8,128)S(1)} %get-tuple-element.73), channel_id=1, source_target_pairs={{0,1},{1,2},{2,3},{3,4},{4,5},{5,6},{6,7},{7,8},{8,9},{9,10},{10,1... | collective-permute-start | bytes 8648 | tf_op jit(solution)/shard_map/ppermute | solution.py:30
  218.4 14.3 %collective-permute-start.18 = (f32[4,10,18,1]{3,2,1,0:T(8,128)S(1)}, f32[4,10,18,1]{3,2,1,0:T(8,128)S(1)}, u32[]{:S(2)}, u32[]{:S(2)}) collective-permute-start(f32[4,10,18,1]{3,2,1,0:T(8,128)S(1)} %get-tuple-element.74), channel_id=1, source_target_pairs={{1,0},{2,1},{3,2},{4,3},{5,4},{6,5},{7,6},{8,7},{9,8},{10,9},{11,1... | collective-permute-start | bytes 8648 | tf_op jit(solution)/shard_map/ppermute | solution.py:31
  289.4 26.1 %copy-start.1 = (f32[3,8,2048]{2,1,0:T(8,128)S(1)}, f32[3,8,2048]{2,1,0:T(8,128)}, u32[]{:S(2)}) copy-start(f32[3,8,2048]{2,1,0:T(8,128)} %param.8) | copy-start | bytes 589828
  289.4 26.1 %copy-start.4 = (f32[8,2048]{1,0:T(8,128)S(1)}, f32[8,2048]{1,0:T(8,128)}, u32[]{:S(2)}) copy-start(f32[8,2048]{1,0:T(8,128)} %param.7) | copy-start | bytes 196612
  289.4 26.5 %copy-start.3 = (f32[28,2048]{1,0:T(8,128)S(1)}, f32[28,2048]{1,0:T(8,128)}, u32[]{:S(2)}) copy-start(f32[28,2048]{1,0:T(8,128)} %param.5) | copy-start | bytes 688132
  289.4 26.9 %slice-start = ((f32[28,2048]{1,0:T(8,128)}), f32[2,2048]{1,0:T(2,128)S(1)}, s32[]{:S(2)}) async-start(f32[28,2048]{1,0:T(8,128)} %param.5), calls=%async_computation | async-start | bytes 32768 | tf_op jit(solution)/shard_map/slice | solution.py:127
  316.6 10.1 %collective-permute-start.19 = (f32[28,1024]{1,0:T(8,128)S(1)}, f32[28,1024]{1,0:T(8,128)S(1)}, u32[]{:S(2)}, u32[]{:S(2)}) collective-permute-start(f32[28,1024]{1,0:T(8,128)S(1)} %slice.588), channel_id=1, source_target_pairs={{0,1},{1,2},{2,3},{3,4},{4,5},{5,6},{6,7},{7,8},{8,9},{9,10},{10,1... | collective-permute-start | bytes 344072 | tf_op jit(solution)/shard_map/ppermute | solution.py:38
where the time goes:
time: 329 us; the launch traced here: 328 us
  other arithmetic  98 us (30%)
  local copies, waits for them, and re-layouts  96.6 us (29%)
  starting transfers between devices  76.7 us (23%)
  waiting for transfers between devices  53.7 us (16%)
    scatter-add x1, other arithmetic, per_device(): grid_sum = jnp.zeros((9, span_x * span_y * span_z), jnp.float32).at[:, al...  88.4 us
    gather x1, local copies, waits for them, and re-layouts, per_device(): near = near_all[:, all_index].reshape(4, 8, count)  54.4 us
    ppermute x9, starting transfers between devices, with_halo(): before = lax.ppermute(last, axis, up)  50.9 us
    ppermute x9, waiting for transfers between devices, with_halo(): after = lax.ppermute(leading, axis, down)  34.5 us
    slice x1, local copies, waits for them, and re-layouts, per_device(): updated = advance(particles, near[0:3], near[3], weights, gradients)  26 us
    ppermute x9, starting transfers between devices, with_halo(): after = lax.ppermute(leading, axis, down)  16.9 us
    ppermute x9, waiting for transfers between devices, with_halo(): before = lax.ppermute(last, axis, up)  12.9 us
    ppermute x2, starting transfers between devices, passed_along(): lax.ppermute(value, axis, [(i, (i + by) % count) for i in range(count)])  8.85 us
  transfers between devices with their start and end apart: 20, of which 12 were waited for; matrix products, arithmetic and copies ran while one was open for 0% of the time, Pallas kernels for 0%

commit v1 on v0

v1 whole, which is shorter than its diff:
```python
import jax
import jax.numpy as jnp
from jax import lax
from jax.experimental import pallas as pl
from jax.experimental.pallas import tpu as pltpu
from jax.sharding import PartitionSpec as P

CX = 8
CY = 16
CZ = 32
NBIN = 16
BIN = 128
SUBSTEPS = 4
FIELDS = 28
MOST = 8
COUNT = NBIN * BIN
TAIL = MOST * BIN
SLOTS = (NBIN + MOST) * BIN

time_step = 0.1
relax_rate = 0.2
length_sq = 0.6
shear_mod = 1.0
bulk_coef = 1.5
mass_floor = 0.5

EX = CX + 2
EY = CY + 2
WIDE = SUBSTEPS + 1
LAYERS = WIDE + 1
SX = CX + 2 * WIDE
SY = CY + 2 * WIDE
SZ = CZ + 2 * WIDE
OFF = WIDE - 1
PITCH = 32
AROWS = 176
GROWS = 200
GROUP = 40
ZROWS = 40
CHUNK = 256
F32 = jnp.float32
BF16 = jnp.bfloat16
VMEM = pltpu.VMEM
VMEM_LIMIT = 48 * 1024 * 1024


def shift_lanes(value, by):
    by = by % 128
    return value if by == 0 else pltpu.roll(value, by, 1)


def lane_index(rows):
    return lax.broadcasted_iota(jnp.int32, (rows, 128), 1)


def onehot_rows(base_ref, lanes):
    xy = base_ref[0:1, lanes] * EY + base_ref[1:2, lanes]
    rows = lax.broadcasted_iota(jnp.int32, (AROWS, CHUNK), 0)
    return jnp.where(rows == xy, 1.0, 0.0).astype(BF16)


def scatter_kernel(counts_ref, part_ref, base_ref, w_ref, g_ref, deep_ref, vel_ref, low_ref, high_ref, acc_ref, sum_ref):
    acc_ref[...] = jnp.zeros_like(acc_ref)

    def step(index, carry):
        lanes = pl.ds(pl.multiple_of(index * CHUNK, CHUNK), CHUNK)
        mass = part_ref[0:1, lanes]
        minus_vol = -time_step * part_ref[1:2, lanes]
        share = mass * w_ref[:, lanes]
        slope = [g_ref[j, :, lanes] for j in range(3)]
        terms = [share, share * part_ref[23:24, lanes], share * part_ref[24:25, lanes]]
        for i in range(3):
            row = 14 + 3 * i
            pull = (
                part_ref[row : row + 1, lanes] * slope[0]
                + part_ref[row + 1 : row + 2, lanes] * slope[1]
                + part_ref[row + 2 : row + 3, lanes] * slope[2]
            )
            terms.append(share * part_ref[2 + i : 3 + i, lanes] + minus_vol * pull)
        high = [t.astype(BF16).astype(F32) for t in terms]
        low = [t - h for t, h in zip(terms, high)]
        base_z = base_ref[2:3, lanes]
        sub = lax.broadcasted_iota(jnp.int32, (8, CHUNK), 0) - base_z
        blocks = {}
        for tile in range(16):
            masks = []
            for ch in range(3):
                first, last = SZ * ch + OFF, SZ * ch + OFF + CZ + 1
                if first <= 8 * tile + 7 and last >= 8 * tile:
                    masks.append((ch, sub == first - 8 * tile, sub == first + 1 - 8 * tile))
            for corner in range(4):
                for half in range(2):
                    for part, source in enumerate((high, low)):
                        value = jnp.zeros((8, CHUNK), F32)
                        for ch, at, after in masks:
                            rows = source[3 * half + ch]
                            value = jnp.where(at, rows[2 * corner : 2 * corner + 1], value)
                            value = jnp.where(after, rows[2 * corner + 1 : 2 * corner + 2], value)
                        blocks[corner, half, part, tile] = value
        onehot = onehot_rows(base_ref, lanes)
        for corner in range(4):
            for half in range(2):
                total = None
                for part in range(2):
                    rhs = jnp.concatenate([blocks[corner, half, part, t] for t in range(16)], axis=0).astype(BF16)
                    piece = lax.dot_general(onehot, rhs, (((1,), (1,)), ((), ())), preferred_element_type=F32)
                    total = piece if total is None else total + piece
                at = 128 * (2 * corner + half)
                acc_ref[:, at : at + 128] += total
        return carry

    lax.fori_loop(0, COUNT // CHUNK, step, 0)
    sum_ref[...] = jnp.zeros_like(sum_ref)
    for corner in range(4):
        shift = (corner >> 1) * EY + (corner & 1)
        sum_ref[shift : shift + AROWS, :] += acc_ref[:, 256 * corner : 256 * corner + 256]
    deep_ref[...] = sum_ref[:, 0:128]
    vel_ref[...] = sum_ref[:, 128:256]
    lane = lane_index(GROUP)
    low_msg = jnp.zeros((GROUP, 128), F32)
    high_msg = jnp.zeros((GROUP, 128), F32)
    for j in range(5):
        deep = sum_ref[GROUP * j : GROUP * (j + 1), 0:128]
        vel = sum_ref[GROUP * j : GROUP * (j + 1), 128:256]
        for ch in range(3):
            to = 24 * j + LAYERS * ch
            inside = (lane >= to) & (lane < to + LAYERS)
            low_msg = jnp.where(inside, shift_lanes(deep, to - (SZ * ch + OFF)), low_msg)
            high_msg = jnp.where(inside, shift_lanes(deep, to - (SZ * ch + CZ)), high_msg)
            to = 24 * j + 3 * LAYERS + 2 * ch
            inside = (lane >= to) & (lane < to + 2)
            low_msg = jnp.where(inside, shift_lanes(vel, to - (SZ * ch + OFF)), low_msg)
            high_msg = jnp.where(inside, shift_lanes(vel, to - (SZ * ch + OFF + CZ)), high_msg)
    low_ref[...] = low_msg
    high_ref[...] = jnp.where(lane >= 120, counts_ref[0].astype(F32), high_msg)


def join_z_kernel(place_ref, deep_ref, vel_ref, before_ref, after_ref, deep_out, vel_out, low_ref, high_ref):
    lane = lane_index(GROUP)
    before = jnp.where(place_ref[2] > 0, before_ref[...], 0.0)
    after = after_ref[...]
    for j in range(5):
        rows = slice(GROUP * j, GROUP * (j + 1))
        deep = jnp.zeros((GROUP, 128), F32)
        vel = jnp.zeros((GROUP, 128), F32)
        for ch in range(3):
            source = 24 * j + LAYERS * ch
            to = SZ * ch
            inside = (lane >= to) & (lane < to + LAYERS)
            deep = jnp.where(inside, shift_lanes(before, to - source), deep)
            to = SZ * ch + OFF + CZ
            inside = (lane >= to) & (lane < to + LAYERS)
            deep = jnp.where(inside, shift_lanes(after, to - source), deep)
            source = 24 * j + 3 * LAYERS + 2 * ch
            to = SZ * ch + OFF
            inside = (lane >= to) & (lane < to + 2)
            vel = jnp.where(inside, shift_lanes(before, to - source), vel)
            to = SZ * ch + OFF + CZ
            inside = (lane >= to) & (lane < to + 2)
            vel = jnp.where(inside, shift_lanes(after, to - source), vel)
        deep_out[rows, :] = deep_ref[rows, :] + deep
        vel_out[rows, :] = vel_ref[rows, :] + vel
    for x in range(EX):
        row = EY * x
        low_ref[LAYERS * x : LAYERS * (x + 1), :] = deep_out[row : row + LAYERS, :]
        high_ref[LAYERS * x : LAYERS * (x + 1), :] = deep_out[row + EY - LAYERS : row + EY, :]
        at = LAYERS * EX + 2 * x
        low_ref[at : at + 2, :] = vel_out[row : row + 2, :]
        high_ref[at : at + 2, :] = vel_out[row + EY - 2 : row + EY, :]


def join_y_kernel(deep_ref, vel_ref, before_ref, after_ref, deep_out, vel_out, low_ref, high_ref):
    deep_out[...] = jnp.zeros_like(deep_out)
    vel_out[...] = jnp.zeros_like(vel_out)
    for x in range(EX):
        row = EY * x
        deep_out[x, OFF : OFF + EY, :] = deep_ref[row : row + EY, :]
        deep_out[x, 0:LAYERS, :] += before_ref[LAYERS * x : LAYERS * (x + 1), :]
        deep_out[x, OFF + CY : OFF + CY + LAYERS, :] += after_ref[LAYERS * x : LAYERS * (x + 1), :]
        at = LAYERS * EX + 2 * x
        vel_out[x, OFF : OFF + EY, :] = vel_ref[row : row + EY, :]
        vel_out[x, OFF : OFF + 2, :] += before_ref[at : at + 2, :]
        vel_out[x, OFF + CY : OFF + CY + 2, :] += after_ref[at : at + 2, :]
    for x in range(LAYERS):
        low_ref[SY * x : SY * (x + 1), :] = deep_out[x, 0:SY, :]
        high_ref[SY * x : SY * (x + 1), :] = deep_out[EX - LAYERS + x, 0:SY, :]
    for x in range(2):
        at = SY * LAYERS + EY * x
        low_ref[at : at + EY, :] = vel_out[x, OFF : OFF + EY, :]
        high_ref[at : at + EY, :] = vel_out[EX - 2 + x, OFF : OFF + EY, :]


def gather_update(index, nodes_ref, part_ref, base_ref, w_ref, g_ref, out_ref, out_index):
    lanes = pl.ds(pl.multiple_of(index * CHUNK, CHUNK), CHUNK)
    to = pl.ds(pl.multiple_of(out_index * CHUNK, CHUNK), CHUNK)
    onehot = onehot_rows(base_ref, lanes)
    base_z = base_ref[2:3, lanes]
    rows = lax.broadcasted_iota(jnp.int32, (ZROWS, CHUNK), 0) - base_z
    at = rows == 0
    after = rows == 1

    def pick(mask, value):
        kept = jnp.where(mask, value, 0.0)
        total = kept[0:8]
        for t in range(1, ZROWS // 8):
            total = total + kept[8 * t : 8 * t + 8]
        return total

    moved = [jnp.zeros((8, CHUNK), F32) for _ in range(3)]
    velgrad = [[jnp.zeros((8, CHUNK), F32) for _ in range(3)] for _ in range(3)]
    damage_node = jnp.zeros((8, CHUNK), F32)
    rows_ab = 4 * ZROWS
    for corner in range(4):
        start = 2 * rows_ab * corner
        near = jnp.dot(nodes_ref[start : start + rows_ab, 0:AROWS], onehot, preferred_element_type=F32) + jnp.dot(
            nodes_ref[start + rows_ab : start + 2 * rows_ab, 0:AROWS], onehot, preferred_element_type=F32
        )
        for c, mask in enumerate((at, after)):
            k = 2 * corner + c
            weight = w_ref[k : k + 1, lanes]
            slope = [g_ref[j, k : k + 1, lanes] for j in range(3)]
            for i in range(3):
                value = pick(mask, near[ZROWS * i : ZROWS * (i + 1)])
                moved[i] = moved[i] + value * weight
                for j in range(3):
                    velgrad[i][j] = velgrad[i][j] + value * slope[j]
            damage_node = damage_node + pick(mask, near[3 * ZROWS : 4 * ZROWS]) * weight
    moved = [jnp.sum(v, axis=0, keepdims=True) for v in moved]
    velgrad = [[jnp.sum(v, axis=0, keepdims=True) for v in row] for row in velgrad]
    damage_node = jnp.sum(damage_node, axis=0, keepdims=True)

    def field(i):
        return part_ref[i : i + 1, lanes]

    deform = [[field(5 + 3 * i + j) for j in range(3)] for i in range(3)]
    stretch = [[(1.0 if i == j else 0.0) + time_step * velgrad[i][j] for j in range(3)] for i in range(3)]
    mapped = [
        [
            stretch[i][0] * deform[0][j] + stretch[i][1] * deform[1][j] + stretch[i][2] * deform[2][j]
            for j in range(3)
        ]
        for i in range(3)
    ]
    jacobian = (
        mapped[0][0] * (mapped[1][1] * mapped[2][2] - mapped[1][2] * mapped[2][1])
        - mapped[0][1] * (mapped[1][0] * mapped[2][2] - mapped[1][2] * mapped[2][0])
        + mapped[0][2] * (mapped[1][0] * mapped[2][1] - mapped[1][1] * mapped[2][0])
    )
    left = {}
    for i in range(3):
        for j in range(i, 3):
            left[i, j] = left[j, i] = (
                mapped[i][0] * mapped[j][0] + mapped[i][1] * mapped[j][1] + mapped[i][2] * mapped[j][2]
            )
    damaged = jnp.maximum(field(23), damage_node)
    degrade = (1.0 - damaged) ** 2
    pressure = bulk_coef * (jacobian - 1.0)
    energy = (
        0.5 * shear_mod * (left[0, 0] + left[1, 1] + left[2, 2] - 3.0) + 0.5 * bulk_coef * (jacobian - 1.0) ** 2
    )
    out_ref[0:2, to] = part_ref[0:2, lanes]
    for i in range(3):
        out_ref[2 + i : 3 + i, to] = moved[i]
        out_ref[25 + i : 26 + i, to] = field(25 + i) + time_step * moved[i]
        for j in range(3):
            out_ref[5 + 3 * i + j : 6 + 3 * i + j, to] = mapped[i][j]
            term = shear_mod * (left[i, j] - (1.0 if i == j else 0.0))
            if i == j:
                term = term + pressure
            out_ref[14 + 3 * i + j : 15 + 3 * i + j, to] = degrade * term
    out_ref[23:24, to] = damaged
    out_ref[24:25, to] = jnp.maximum(field(24), energy)


def relax_kernel(
    axis_sizes,
    place_ref,
    deep_ref,
    vel_ref,
    before_ref,
    after_ref,
    part_ref,
    base_ref,
    w_ref,
    g_ref,
    damage_ref,
    nodes_ref,
    tail_ref,
    one_ref,
    two_ref,
    keep_ref,
    add_ref,
    inverse_ref,
    fv_ref,
    fd_ref,
):
    count_x, count_y, count_z = axis_sizes
    lane = lane_index(PITCH)
    row = lax.broadcasted_iota(jnp.int32, (PITCH, 128), 0)
    pos_y = place_ref[1] * CY + row - WIDE
    pos_z = place_ref[2] * CZ + lane - WIDE
    inside_yz = (
        (lane < SZ) & (pos_y >= 0) & (pos_y < count_y * CY) & (pos_z >= 0) & (pos_z < count_z * CZ)
    ).astype(F32)

    def inside(xd):
        pos = place_ref[0] * CX + xd - WIDE
        flag = jnp.where((pos >= 0) & (pos < count_x * CX), 1.0, 0.0).astype(F32)
        return inside_yz * flag

    one_ref[...] = jnp.zeros_like(one_ref)
    for xd in range(SX):
        if OFF <= xd < OFF + EX:
            one_ref[xd] = deep_ref[xd - OFF]
        if xd < LAYERS:
            one_ref[xd, 0:SY, :] += before_ref[SY * xd : SY * (xd + 1), :]
        if xd >= SX - LAYERS:
            at = SY * (xd - SX + LAYERS)
            one_ref[xd, 0:SY, :] += after_ref[at : at + SY, :]
    for xd in range(SX):
        sums = one_ref[xd]
        mask = inside(xd)
        inverse = mask / jnp.maximum(sums, mass_floor)
        drive = shift_lanes(sums, -2 * SZ) * inverse
        keep_ref[xd] = (1.0 - relax_rate * (1.0 + 6.0 * length_sq)) * mask - 2.0 * relax_rate * drive
        add_ref[xd] = 2.0 * relax_rate * drive
        one_ref[xd] = shift_lanes(sums, -SZ) * inverse
        if OFF <= xd < OFF + EX:
            inverse_ref[xd - OFF] = inverse
    source, target = one_ref, two_ref
    for step in range(SUBSTEPS):
        for xd in range(step + 1, SX - 1 - step):
            centre = source[xd]
            around = (
                source[xd - 1]
                + source[xd + 1]
                + pltpu.roll(centre, 1, 0)
                + pltpu.roll(centre, PITCH - 1, 0)
                + shift_lanes(centre, 1)
                + shift_lanes(centre, -1)
            )
            target[xd] = centre * keep_ref[xd] + add_ref[xd] + (relax_rate * length_sq) * inside(xd) * around
        source, target = target, source
    for x in range(CX):
        damage_ref[x] = shift_lanes(source[x + WIDE], -WIDE)[WIDE : WIDE + CY, 0:CZ]
    fv_ref[...] = jnp.zeros_like(fv_ref)
    fd_ref[...] = jnp.zeros_like(fd_ref)
    vel_at = SY * LAYERS
    for x in range(EX):
        vel = vel_ref[x, OFF : OFF + EY, :]
        if x < 2:
            vel = vel + before_ref[vel_at + EY * x : vel_at + EY * (x + 1), :]
        if x >= EX - 2:
            at = vel_at + EY * (x - EX + 2)
            vel = vel + after_ref[at : at + EY, :]
        inverse = inverse_ref[x, OFF : OFF + EY, :]
        vel = vel * (inverse + shift_lanes(inverse, SZ) + shift_lanes(inverse, 2 * SZ))
        lanes = lane_index(EY)
        vel = jnp.where(
            lanes < ZROWS,
            shift_lanes(vel, -OFF),
            jnp.where(
                lanes < 2 * ZROWS,
                shift_lanes(vel, ZROWS - SZ - OFF),
                shift_lanes(vel, 2 * (ZROWS - SZ) - OFF),
            ),
        )
        fv_ref[EY * x : EY * (x + 1), :] = vel
        fd_ref[EY * x : EY * (x + 1), :] = shift_lanes(source[x + OFF], -OFF)[OFF : OFF + EY, :]
    nodes = jnp.concatenate([fv_ref[...].T[0 : 3 * ZROWS], fd_ref[...].T[0:ZROWS]], axis=0)
    for corner in range(4):
        shift = (corner >> 1) * EY + (corner & 1)
        value = nodes if shift == 0 else pltpu.roll(nodes, 256 - shift, 1)
        high = value.astype(BF16)
        low = (value - high.astype(F32)).astype(BF16)
        start = 8 * ZROWS * corner
        nodes_ref[start : start + 4 * ZROWS, :] = high
        nodes_ref[start + 4 * ZROWS : start + 8 * ZROWS, :] = low

    def step(index, carry):
        gather_update((COUNT - TAIL) // CHUNK + index, nodes_ref, part_ref, base_ref, w_ref, g_ref, tail_ref, index)
        return carry

    lax.fori_loop(0, TAIL // CHUNK, step, 0)


def head_kernel(nodes_ref, part_ref, base_ref, w_ref, g_ref, head_ref):
    def step(index, carry):
        gather_update(index, nodes_ref, part_ref, base_ref, w_ref, g_ref, head_ref, index)
        return carry

    lax.fori_loop(0, (COUNT - TAIL) // CHUNK, step, 0)


def assemble_kernel(counts_ref, prior_ref, recv_ref, head_ref, tail_ref, out_ref, line_ref):
    line_ref[:, 0:TAIL] = recv_ref[...]
    line_ref[:, TAIL:COUNT] = head_ref[...]
    line_ref[:, COUNT : COUNT + TAIL] = tail_ref[...]
    prior = prior_ref[0, 120].astype(jnp.int32)
    live = NBIN - counts_ref[0] + prior
    for slot in range(NBIN + MOST):
        source = jnp.minimum(MOST - prior + slot, NBIN + MOST - 1)
        value = line_ref[:, pl.ds(pl.multiple_of(source * BIN, BIN), BIN)]
        out_ref[:, slot * BIN : (slot + 1) * BIN] = jnp.where(slot < live, value, 0.0)


def shape(*dims, kind=F32):
    return jax.ShapeDtypeStruct(dims, kind)


def smem():
    return pl.BlockSpec(memory_space=pltpu.SMEM)


def vmem(n):
    return [pl.BlockSpec(memory_space=VMEM)] * n


def call(kernel, out_shape, n_smem, args, scratch=(), flops=0):
    return pl.pallas_call(
        kernel,
        out_shape=out_shape,
        in_specs=[smem()] * n_smem + vmem(len(args) - n_smem),
        out_specs=jax.tree.map(lambda _: pl.BlockSpec(memory_space=VMEM), out_shape),
        scratch_shapes=list(scratch),
        compiler_params=pltpu.CompilerParams(vmem_limit_bytes=VMEM_LIMIT),
        cost_estimate=pl.CostEstimate(flops=flops, bytes_accessed=2000000, transcendentals=0),
    )(*args)


def exchange(low, high, axis, ring=False):
    count = lax.axis_size(axis)
    up = [(i, (i + 1) % count) for i in range(count if ring else count - 1)]
    down = [(i + 1, i) for i in range(count - 1)]
    return lax.ppermute(high, axis, up), lax.ppermute(low, axis, down)


def per_device(particles, stencil_base, weights, gradients, counts):
    axes = ("gx", "gy", "gz")
    place = jnp.stack([lax.axis_index(a) for a in axes]).astype(jnp.int32)
    sizes = tuple(lax.axis_size(a) for a in axes)
    ring = [(i, (i + 1) % sizes[2]) for i in range(sizes[2])]
    inputs = (particles, stencil_base, weights, gradients)
    deep, vel, low, high = call(
        scatter_kernel,
        (shape(GROWS, 128), shape(GROWS, 128), shape(GROUP, 128), shape(GROUP, 128)),
        1,
        (counts,) + inputs,
        [VMEM((AROWS, 1024), F32), VMEM((GROWS, 256), F32)],
    )
    before_z, after_z = exchange(low, high, "gz", ring=True)
    message = LAYERS * EX + 2 * EX
    deep, vel, low, high = call(
        join_z_kernel,
        (shape(GROWS, 128), shape(GROWS, 128), shape(message, 128), shape(message, 128)),
        1,
        (place, deep, vel, before_z, after_z),
    )
    before, after = exchange(low, high, "gy")
    message = LAYERS * SY + 2 * EY
    deep, vel, low, high = call(
        join_y_kernel,
        (shape(EX, PITCH, 128), shape(EX, PITCH, 128), shape(message, 128), shape(message, 128)),
        0,
        (deep, vel, before, after),
    )
    before, after = exchange(low, high, "gx")

    def relax(*refs):
        relax_kernel(sizes, *refs)

    damage, nodes, tail = call(
        relax,
        (shape(CX, CY, CZ), shape(32 * ZROWS, 256, kind=BF16), shape(FIELDS, TAIL)),
        1,
        (place, deep, vel, before, after) + inputs,
        [VMEM((SX, PITCH, 128), F32)] * 4 + [VMEM((EX, PITCH, 128), F32)] + [VMEM((256, 128), F32)] * 2,
    )
    recv = lax.ppermute(tail, "gz", ring)
    head = call(head_kernel, shape(FIELDS, COUNT - TAIL), 0, (nodes,) + inputs, flops=2 * 1280 * 256 * 1024)
    migrated = call(
        assemble_kernel,
        shape(FIELDS, SLOTS),
        2,
        (counts, before_z[0:8], recv, head, tail),
        [VMEM((FIELDS, COUNT + TAIL), F32)],
    )
    return (migrated, damage)


def solution(mesh):
    return jax.shard_map(
        per_device,
        mesh=mesh,
        in_specs=(
            P(None, ("gx", "gy", "gz")),
            P(None, ("gx", "gy", "gz")),
            P(None, ("gx", "gy", "gz")),
            P(None, None, ("gx", "gy", "gz")),
            P(("gx", "gy", "gz")),
        ),
        out_specs=(P(None, ("gx", "gy", "gz")), P("gx", "gy", "gz")),
        check_vma=False,
    )
```

time: 329 us -> 66.5 us (0.20)
  other arithmetic: 98 us -> 0.08 us
  local copies, waits for them, and re-layouts: 96.6 us -> 3.49 us
  starting transfers between devices: 76.7 us -> 26.2 us
  waiting for transfers between devices: 53.7 us -> 20.6 us
  Pallas kernels: 0 us -> 14.1 us
    scatter-add x1 -> x0, other arithmetic: 88.4 us -> none  [per_device(): grid_sum = jnp.zeros((9, span_x * span_y * span_z), jnp.float32).at[:, al...]
    gather x1 -> x0, local copies, waits for them, and re-layouts: 54.4 us -> none  [per_device(): near = near_all[:, all_index].reshape(4, 8, count)]
    ppermute x20 -> x7, starting transfers between devices: 76.7 us -> 26.2 us  [the longest x6 23.3 us: exchange(): return (lax.ppermute(high, axis, up), lax.ppermute(low, axis, down))]
    ppermute x20 -> x7, waiting for transfers between devices: 53.7 us -> 20.6 us  [the longest x6 16.3 us: exchange(): return (lax.ppermute(high, axis, up), lax.ppermute(low, axis, down))]
    slice x13 -> x1, local copies, waits for them, and re-layouts: 30.5 us -> 0.01 us  [per_device(): before_z[0:8]]
    pallas_call x0 -> x6, Pallas kernels: none -> 14.1 us  [call(): pl.pallas_call(kernel, out_shape=out_shape, in_specs=[smem()] * n_smem +...]
    mul x19 -> x0, other arithmetic: 5.74 us -> none  [the longest x2 2.18 us: node_terms(): share * particles[24]]
    concatenate x11 -> x0, local copies, waits for them, and re-layouts: 5.67 us -> none  [the longest x2 4.68 us: per_device(): jnp.concatenate(terms, axis=1)]
  transfers between devices with their start and end apart: 20 -> 7, of which waited for: 12 -> 4; matrix products, arithmetic and copies ran while one was open for 0% -> 0% of each run, Pallas kernels for 0% -> 3%
where the time goes in v1:
time: 66.5 us; the launch traced here: 66 us
  starting transfers between devices  26.2 us (39%)
  waiting for transfers between devices  20.6 us (31%)
  Pallas kernels  14.1 us (21%)
  local copies, waits for them, and re-layouts  3.49 us (5%)
  between operations  1.43 us (2%)
    ppermute x6, starting transfers between devices, exchange(): return (lax.ppermute(high, axis, up), lax.ppermute(low, axis, down))  23.3 us
    ppermute x6, waiting for transfers between devices, exchange(): return (lax.ppermute(high, axis, up), lax.ppermute(low, axis, down))  16.3 us
    pallas_call x6, Pallas kernels, call(): pl.pallas_call(kernel, out_shape=out_shape, in_specs=[smem()] * n_smem +...  14.1 us
    ppermute x1, waiting for transfers between devices, per_device(): recv = lax.ppermute(tail, 'gz', ring)  4.35 us
    unnamed x16, local copies, waits for them, and re-layouts  3.49 us
    ppermute x1, starting transfers between devices, per_device(): recv = lax.ppermute(tail, 'gz', ring)  2.9 us
  transfers between devices with their start and end apart: 7, of which 4 were waited for; matrix products, arithmetic and copies ran while one was open for 0% of the time, Pallas kernels for 3%

profile of v1, /device:TPU:1, one launch (start us, length us, event | category | flops | bytes accessed | tf_op | source)
XLA Modules:
  0.0 66.0 jit_solution(17967187083325067509)
XLA Ops:
  1.3 0.0 copy-start
  1.3 0.9 %copy-done = f32[28,2048]{1,0:T(8,128)S(1)} copy-done((f32[28,2048]{1,0:T(8,128)S(1)}, f32[28,2048]{1,0:T(8,128)}, u32[]{:S(2)}) %copy-start) | copy-done | bytes 229400
  2.2 0.9 %copy-done.2 = f32[3,8,2048]{2,1,0:T(8,128)S(1)} copy-done((f32[3,8,2048]{2,1,0:T(8,128)S(1)}, f32[3,8,2048]{2,1,0:T(8,128)}, u32[]{:S(2)}) %copy-start.2) | copy-done | bytes 196632
  3.2 0.8 %copy-done.4 = f32[8,2048]{1,0:T(8,128)S(1)} copy-done((f32[8,2048]{1,0:T(8,128)S(1)}, f32[8,2048]{1,0:T(8,128)}, u32[]{:S(2)}) %copy-start.4) | copy-done | bytes 65560
  4.0 0.8 %copy-done.6 = s32[3,2048]{1,0:T(4,128)S(1)} copy-done((s32[3,2048]{1,0:T(4,128)S(1)}, s32[3,2048]{1,0:T(4,128)}, u32[]{:S(2)}) %copy-start.6) | copy-done | bytes 24600
  4.8 5.1 %shard_map.68 = (f32[200,128]{1,0:T(8,128)S(1)}, f32[200,128]{1,0:T(8,128)S(1)}, f32[40,128]{1,0:T(8,128)S(1)}, f32[40,128]{1,0:T(8,128)S(1)}) custom-call(s32[1]{0:T(128)S(6)} %copy.7.counts_ref, f32[28,2048]{1,0:T(8,128)S(1)} %copy-done, s32[3,2048]{1,0:T(4,128)S(1)} %copy-done.6, f32[8,2048]{1,0:T(8,128)S(1)} %copy-done.4, f32[3,8,2048]{2,1,0:T(8,128)S(1)} %copy-done.2), custom_call_target="tpu_custom_call" | custom-call | bytes 2000000 | tf_op jit(solution)/shard_map/pallas_call | solution.py:420
  9.9 4.0 %collective-permute-start = (f32[40,128]{1,0:T(8,128)S(1)}, f32[40,128]{1,0:T(8,128)S(1)}, u32[]{:S(2)}, u32[]{:S(2)}) collective-permute-start(f32[40,128]{1,0:T(8,128)S(1)} %get-tuple-element.17), channel_id=1, source_target_pairs={{0,1},{1,2},{2,3},{3,4},{4,5},{5,6},{6,7},{7,8},{8,9},{9,10},{10,1... | collective-permute-start | bytes 61448 | tf_op jit(solution)/shard_map/ppermute | solution.py:435
  13.9 1.3 %collective-permute-start.1 = (f32[40,128]{1,0:T(8,128)S(1)}, f32[40,128]{1,0:T(8,128)S(1)}, u32[]{:S(2)}, u32[]{:S(2)}) collective-permute-start(f32[40,128]{1,0:T(8,128)S(1)} %get-tuple-element.20), channel_id=1, source_target_pairs={{1,0},{2,1},{3,2},{4,3},{5,4},{6,5},{7,6},{8,7},{9,8},{10,9},{11,1... | collective-permute-start | bytes 61448 | tf_op jit(solution)/shard_map/ppermute | solution.py:435
  15.2 0.0 copy-start.7
  15.2 0.1 pad_add_fusion.place_ref.refs_0_
  15.3 3.4 %collective-permute-done.before_ref = f32[40,128]{1,0:T(8,128)S(1)} collective-permute-done((f32[40,128]{1,0:T(8,128)S(1)}, f32[40,128]{1,0:T(8,128)S(1)}, u32[]{:S(2)}, u32[]{:S(2)}) %collective-permute-start) | collective-permute-done | bytes 20512 | tf_op jit(solution)/shard_map/ppermute | solution.py:435
  18.7 0.0 collective-permute-done.1.after_ref
  18.7 0.9 %shard_map.69 = (f32[200,128]{1,0:T(8,128)S(1)}, f32[200,128]{1,0:T(8,128)S(1)}, f32[80,128]{1,0:T(8,128)S(1)}, f32[80,128]{1,0:T(8,128)S(1)}) custom-call(s32[3]{0:T(128)S(1)} %pad_add_fusion.place_ref.refs_0_, f32[200,128]{1,0:T(8,128)S(1)} %get-tuple-element.18.deep_ref, f32[200,128]{1,0:T(8,128)S(1)} %get-tuple-element.19.vel_ref, ...), custom_call_target="tpu_custom_call" | custom-call | bytes 2000000 | tf_op jit(solution)/shard_map/pallas_call | solution.py:420
  19.6 0.0 copy-start.3
  19.6 9.0 %collective-permute-start.2 = (f32[80,128]{1,0:T(8,128)S(1)}, f32[80,128]{1,0:T(8,128)S(1)}, u32[]{:S(2)}, u32[]{:S(2)}) collective-permute-start(f32[80,128]{1,0:T(8,128)S(1)} %get-tuple-element.23), channel_id=1, source_target_pairs={{0,16},{16,32},{32,48},{1,17},{17,33},{33,49},{2,18},{18,34},{34,5... | collective-permute-start | bytes 122888 | tf_op jit(solution)/shard_map/ppermute | solution.py:435
  28.6 1.3 %collective-permute-start.3 = (f32[80,128]{1,0:T(8,128)S(1)}, f32[80,128]{1,0:T(8,128)S(1)}, u32[]{:S(2)}, u32[]{:S(2)}) collective-permute-start(f32[80,128]{1,0:T(8,128)S(1)} %get-tuple-element.24), channel_id=1, source_target_pairs={{16,0},{32,16},{48,32},{17,1},{33,17},{49,33},{18,2},{34,18},{50,3... | collective-permute-start | bytes 122888 | tf_op jit(solution)/shard_map/ppermute | solution.py:435
  29.9 0.0 collective-permute-done.2.before_ref
  29.9 8.9 %collective-permute-done.3.after_ref = f32[80,128]{1,0:T(8,128)S(1)} collective-permute-done((f32[80,128]{1,0:T(8,128)S(1)}, f32[80,128]{1,0:T(8,128)S(1)}, u32[]{:S(2)}, u32[]{:S(2)}) %collective-permute-start.3) | collective-permute-done | bytes 40992 | tf_op jit(solution)/shard_map/ppermute | solution.py:435
  38.8 0.1 shard_map.70
  38.9 5.8 %collective-permute-start.4 = (f32[192,128]{1,0:T(8,128)S(1)}, f32[192,128]{1,0:T(8,128)S(1)}, u32[]{:S(2)}, u32[]{:S(2)}) collective-permute-start(f32[192,128]{1,0:T(8,128)S(1)} %get-tuple-element.27), channel_id=1, source_target_pairs={{0,64},{64,128},{128,192},{192,256},{256,320},{320,384},{384,448},... | collective-permute-start | bytes 294920 | tf_op jit(solution)/shard_map/ppermute | solution.py:435
  44.7 1.9 %collective-permute-start.5 = (f32[192,128]{1,0:T(8,128)S(1)}, f32[192,128]{1,0:T(8,128)S(1)}, u32[]{:S(2)}, u32[]{:S(2)}) collective-permute-start(f32[192,128]{1,0:T(8,128)S(1)} %get-tuple-element.28), channel_id=1, source_target_pairs={{64,0},{128,64},{192,128},{256,192},{320,256},{384,320},{448,384},... | collective-permute-start | bytes 294920 | tf_op jit(solution)/shard_map/ppermute | solution.py:435
  46.6 0.0 collective-permute-done.4.refs_3_
  46.6 4.0 %collective-permute-done.5.refs_4_ = f32[192,128]{1,0:T(8,128)S(1)} collective-permute-done((f32[192,128]{1,0:T(8,128)S(1)}, f32[192,128]{1,0:T(8,128)S(1)}, u32[]{:S(2)}, u32[]{:S(2)}) %collective-permute-start.5) | collective-permute-done | bytes 98336 | tf_op jit(solution)/shard_map/ppermute | solution.py:435
  50.6 0.0 copy-done.7
  50.6 0.0 copy-done.1
  50.6 0.0 copy-done.3
  50.6 0.0 copy-done.5
  50.6 4.9 %shard_map.71 = (f32[8,16,32]{2,1,0:T(8,128)}, bf16[1280,256]{1,0:T(8,128)(2,1)S(1)}, f32[28,1024]{1,0:T(8,128)S(1)}) custom-call(s32[3]{0:T(128)S(1)} %pad_add_fusion.place_ref.refs_0_, f32[10,32,128]{2,1,0:T(8,128)S(1)} %get-tuple-element.25.refs_1_, f32[10,32,128]{2,1,0:T(8,128)S(1)} %get-tuple-element.26.refs_2_, ...), custom_call_target="tpu_custom_call" | custom-call | bytes 2000000 | tf_op jit(solution)/shard_map/pallas_call | solution.py:420
  55.5 2.9 %collective-permute-start.6 = (f32[28,1024]{1,0:T(8,128)S(1)}, f32[28,1024]{1,0:T(8,128)S(1)}, u32[]{:S(2)}, u32[]{:S(2)}) collective-permute-start(f32[28,1024]{1,0:T(8,128)S(1)} %get-tuple-element.29.tail_ref), channel_id=1, source_target_pairs={{0,1},{1,2},{2,3},{3,4},{4,5},{5,6},{6,7},{7,8},{8,9},{9,10},{10,1... | collective-permute-start | bytes 344072 | tf_op jit(solution)/shard_map/ppermute | solution.py:479
  58.5 1.7 %shard_map.72.head_ref = f32[28,1024]{1,0:T(8,128)S(1)} custom-call(bf16[1280,256]{1,0:T(8,128)(2,1)S(1)} %get-tuple-element.30.nodes_ref, f32[28,2048]{1,0:T(8,128)S(1)} %copy-done.1, s32[3,2048]{1,0:T(4,128)S(1)} %copy-done.7, f32[8,2048]{1,0:T(8,128)S(1)} %copy-done.5, f32[3,8,2048]{2,1,0:T(8,128)S(1)} %copy-done.3), custom_call_target="tpu_custom_call" | custom-call | flops 671088640 | bytes 2000000 | tf_op jit(solution)/shard_map/pallas_call | solution.py:420
  60.2 4.4 %collective-permute-done.6.recv_ref = f32[28,1024]{1,0:T(8,128)S(1)} collective-permute-done((f32[28,1024]{1,0:T(8,128)S(1)}, f32[28,1024]{1,0:T(8,128)S(1)}, u32[]{:S(2)}, u32[]{:S(2)}) %collective-permute-start.6) | collective-permute-done | bytes 114720 | tf_op jit(solution)/shard_map/ppermute | solution.py:479
  64.6 1.4 %shard_map.73 = f32[28,3072]{1,0:T(8,128)} custom-call(s32[1]{0:T(128)S(6)} %copy.7.counts_ref, f32[8,128]{1,0:T(8,128)S(1)} %slice.4.prior_ref, f32[28,1024]{1,0:T(8,128)S(1)} %collective-permute-done.6.recv_ref, f32[28,1024]{1,0:T(8,128)S(1)} %shard_map.72.head_ref, f32[28,1024]{1,0:T(8,128)S(1)} %get-tuple-element.29.tail_ref), custom_call_target="tpu_custom_call" | custom-call | bytes 2000000 | tf_op jit(solution)/shard_map/pallas_call | solution.py:420
  (6 shorter events, 0.0 us)
Async XLA Ops:
  1.3 1.0 %copy-start = (f32[28,2048]{1,0:T(8,128)S(1)}, f32[28,2048]{1,0:T(8,128)}, u32[]{:S(2)}) copy-start(f32[28,2048]{1,0:T(8,128)} %part_ref.3) | copy-start | bytes 688132
  2.2 0.9 %copy-start.2 = (f32[3,8,2048]{2,1,0:T(8,128)S(1)}, f32[3,8,2048]{2,1,0:T(8,128)}, u32[]{:S(2)}) copy-start(f32[3,8,2048]{2,1,0:T(8,128)} %g_ref.3) | copy-start | bytes 589828
  3.2 0.8 %copy-start.4 = (f32[8,2048]{1,0:T(8,128)S(1)}, f32[8,2048]{1,0:T(8,128)}, u32[]{:S(2)}) copy-start(f32[8,2048]{1,0:T(8,128)} %w_ref.3) | copy-start | bytes 196612
  4.0 0.8 %copy-start.6 = (s32[3,2048]{1,0:T(4,128)S(1)}, s32[3,2048]{1,0:T(4,128)}, u32[]{:S(2)}) copy-start(s32[3,2048]{1,0:T(4,128)} %base_ref.3) | copy-start | bytes 73732
  9.9 8.8 %collective-permute-start = (f32[40,128]{1,0:T(8,128)S(1)}, f32[40,128]{1,0:T(8,128)S(1)}, u32[]{:S(2)}, u32[]{:S(2)}) collective-permute-start(f32[40,128]{1,0:T(8,128)S(1)} %get-tuple-element.17), channel_id=1, source_target_pairs={{0,1},{1,2},{2,3},{3,4},{4,5},{5,6},{6,7},{7,8},{8,9},{9,10},{10,1... | collective-permute-start | bytes 61448 | tf_op jit(solution)/shard_map/ppermute | solution.py:435
  13.9 4.8 %collective-permute-start.1 = (f32[40,128]{1,0:T(8,128)S(1)}, f32[40,128]{1,0:T(8,128)S(1)}, u32[]{:S(2)}, u32[]{:S(2)}) collective-permute-start(f32[40,128]{1,0:T(8,128)S(1)} %get-tuple-element.20), channel_id=1, source_target_pairs={{1,0},{2,1},{3,2},{4,3},{5,4},{6,5},{7,6},{8,7},{9,8},{10,9},{11,1... | collective-permute-start | bytes 61448 | tf_op jit(solution)/shard_map/ppermute | solution.py:435
  15.2 35.4 %copy-start.7 = (s32[3,2048]{1,0:T(4,128)S(1)}, s32[3,2048]{1,0:T(4,128)}, u32[]{:S(2)}) copy-start(s32[3,2048]{1,0:T(4,128)} %base_ref.3) | copy-start | bytes 73732
  18.7 31.9 %copy-start.1 = (f32[28,2048]{1,0:T(8,128)S(1)}, f32[28,2048]{1,0:T(8,128)}, u32[]{:S(2)}) copy-start(f32[28,2048]{1,0:T(8,128)} %part_ref.3) | copy-start | bytes 688132
  19.6 31.1 %copy-start.3 = (f32[3,8,2048]{2,1,0:T(8,128)S(1)}, f32[3,8,2048]{2,1,0:T(8,128)}, u32[]{:S(2)}) copy-start(f32[3,8,2048]{2,1,0:T(8,128)} %g_ref.3) | copy-start | bytes 589828
  19.6 10.3 %collective-permute-start.2 = (f32[80,128]{1,0:T(8,128)S(1)}, f32[80,128]{1,0:T(8,128)S(1)}, u32[]{:S(2)}, u32[]{:S(2)}) collective-permute-start(f32[80,128]{1,0:T(8,128)S(1)} %get-tuple-element.23), channel_id=1, source_target_pairs={{0,16},{16,32},{32,48},{1,17},{17,33},{33,49},{2,18},{18,34},{34,5... | collective-permute-start | bytes 122888 | tf_op jit(solution)/shard_map/ppermute | solution.py:435
  28.6 10.2 %collective-permute-start.3 = (f32[80,128]{1,0:T(8,128)S(1)}, f32[80,128]{1,0:T(8,128)S(1)}, u32[]{:S(2)}, u32[]{:S(2)}) collective-permute-start(f32[80,128]{1,0:T(8,128)S(1)} %get-tuple-element.24), channel_id=1, source_target_pairs={{16,0},{32,16},{48,32},{17,1},{33,17},{49,33},{18,2},{34,18},{50,3... | collective-permute-start | bytes 122888 | tf_op jit(solution)/shard_map/ppermute | solution.py:435
  38.8 11.9 %copy-start.5 = (f32[8,2048]{1,0:T(8,128)S(1)}, f32[8,2048]{1,0:T(8,128)}, u32[]{:S(2)}) copy-start(f32[8,2048]{1,0:T(8,128)} %w_ref.3) | copy-start | bytes 196612
  38.9 7.8 %collective-permute-start.4 = (f32[192,128]{1,0:T(8,128)S(1)}, f32[192,128]{1,0:T(8,128)S(1)}, u32[]{:S(2)}, u32[]{:S(2)}) collective-permute-start(f32[192,128]{1,0:T(8,128)S(1)} %get-tuple-element.27), channel_id=1, source_target_pairs={{0,64},{64,128},{128,192},{192,256},{256,320},{320,384},{384,448},... | collective-permute-start | bytes 294920 | tf_op jit(solution)/shard_map/ppermute | solution.py:435
  44.7 5.9 %collective-permute-start.5 = (f32[192,128]{1,0:T(8,128)S(1)}, f32[192,128]{1,0:T(8,128)S(1)}, u32[]{:S(2)}, u32[]{:S(2)}) collective-permute-start(f32[192,128]{1,0:T(8,128)S(1)} %get-tuple-element.28), channel_id=1, source_target_pairs={{64,0},{128,64},{192,128},{256,192},{320,256},{384,320},{448,384},... | collective-permute-start | bytes 294920 | tf_op jit(solution)/shard_map/ppermute | solution.py:435
  55.5 9.0 %collective-permute-start.6 = (f32[28,1024]{1,0:T(8,128)S(1)}, f32[28,1024]{1,0:T(8,128)S(1)}, u32[]{:S(2)}, u32[]{:S(2)}) collective-permute-start(f32[28,1024]{1,0:T(8,128)S(1)} %get-tuple-element.29.tail_ref), channel_id=1, source_target_pairs={{0,1},{1,2},{2,3},{3,4},{4,5},{5,6},{6,7},{7,8},{8,9},{9,10},{10,1... | collective-permute-start | bytes 344072 | tf_op jit(solution)/shard_map/ppermute | solution.py:479

commit v2 on v1

v2 whole, which is shorter than its diff:
```python
import jax
import jax.numpy as jnp
from jax import lax
from jax.experimental import pallas as pl
from jax.experimental.pallas import tpu as pltpu
from jax.sharding import PartitionSpec as P

CX = 8
CY = 16
CZ = 32
NBIN = 16
BIN = 128
SUBSTEPS = 4
FIELDS = 28
MOST = 8
COUNT = NBIN * BIN
TAIL = MOST * BIN
SLOTS = (NBIN + MOST) * BIN

time_step = 0.1
relax_rate = 0.2
length_sq = 0.6
shear_mod = 1.0
bulk_coef = 1.5
mass_floor = 0.5

EX = CX + 2
EY = CY + 2
EZ = CZ + 2
WIDE = SUBSTEPS + 1
LAYERS = WIDE + 1
SX = CX + 2 * WIDE
SY = CY + 2 * WIDE
SZ = CZ + 2 * WIDE
OFF = WIDE - 1
PITCH = 32
AROWS = 176
GROWS = 200
GROUP = 40
HALF = 104
PACK = SX // 3
ZROWS = 40
CHUNK = 256
F32 = jnp.float32
BF16 = jnp.bfloat16
SCATTER_KIB = 56000
VMEM = pltpu.VMEM


def shift_lanes(value, by):
    by = by % 128
    return value if by == 0 else pltpu.roll(value, by, 1)


def channel_lane(lane):
    return jnp.where(
        lane < SZ, lane, jnp.where(lane < 2 * SZ, lane - SZ, jnp.where(lane < 3 * SZ, lane - 2 * SZ, 1000))
    )


def three(lane, width, a, b, c):
    return jnp.where(lane < width, a, jnp.where(lane < 2 * width, b, c))


def lane_index(rows):
    return lax.broadcasted_iota(jnp.int32, (rows, 128), 1)


def onehot_rows(base_ref, lanes):
    xy = base_ref[0:1, lanes] * EY + base_ref[1:2, lanes]
    rows = lax.broadcasted_iota(jnp.int32, (AROWS, CHUNK), 0)
    return jnp.where(rows == xy, 1.0, 0.0).astype(BF16)


def scatter_kernel(
    counts_ref,
    part_hbm,
    base_hbm,
    w_hbm,
    g_hbm,
    deep_ref,
    vel_ref,
    low_ref,
    high_ref,
    part_ref,
    base_ref,
    w_ref,
    g_ref,
    acc_ref,
    wide_ref,
    term_ref,
    rows_ref,
    onehot_ref,
    sems,
):
    moves = [
        pltpu.make_async_copy(source, target, sems.at[i])
        for i, (source, target) in enumerate(
            ((base_hbm, base_ref), (part_hbm, part_ref), (w_hbm, w_ref), (g_hbm, g_ref))
        )
    ]
    for move in moves:
        move.start()
    acc_ref[...] = jnp.zeros_like(acc_ref)
    wide_ref[...] = jnp.zeros_like(wide_ref)
    moves[0].wait()
    for index in range(COUNT // CHUNK):
        lanes = slice(index * CHUNK, (index + 1) * CHUNK)
        onehot_ref[:, lanes] = onehot_rows(base_ref, lanes)
    for move in moves[1:]:
        move.wait()
    for index in range(COUNT // CHUNK):
        lanes = slice(index * CHUNK, (index + 1) * CHUNK)
        minus_vol = -time_step * part_ref[1:2, lanes]
        share = part_ref[0:1, lanes] * w_ref[:, lanes]
        slope = [g_ref[j, :, lanes] for j in range(3)]
        terms = [share, share * part_ref[23:24, lanes], share * part_ref[24:25, lanes]]
        for i in range(3):
            row = 14 + 3 * i
            pull = (
                part_ref[row : row + 1, lanes] * slope[0]
                + part_ref[row + 1 : row + 2, lanes] * slope[1]
                + part_ref[row + 2 : row + 3, lanes] * slope[2]
            )
            terms.append(share * part_ref[2 + i : 3 + i, lanes] + minus_vol * pull)
        for ch, term in enumerate(terms):
            high = term.astype(BF16).astype(F32)
            term_ref[0, ch, :, lanes] = high
            term_ref[1, ch, :, lanes] = term - high
    nt = (((1,), (1,)), ((), ()))
    for corner in range(4):
        k = 2 * corner
        for index in range(COUNT // CHUNK):
            lanes = slice(index * CHUNK, (index + 1) * CHUNK)
            sub = lax.broadcasted_iota(jnp.int32, (8, CHUNK), 0) - base_ref[2:3, lanes]
            for part in range(2):
                tiles = {}
                for tile in range(HALF // 8):
                    first = [(ch, EZ * ch - 8 * tile) for ch in range(3) if EZ * ch < 8 * tile + 8 and EZ * (ch + 1) > 8 * tile]
                    for half in range(2):
                        value = jnp.zeros((8, CHUNK), F32)
                        for ch, at in first:
                            value = jnp.where(sub == at, term_ref[part, 3 * half + ch, k : k + 1, lanes], value)
                            value = jnp.where(sub == at + 1, term_ref[part, 3 * half + ch, k + 1 : k + 2, lanes], value)
                        tiles[half * (HALF // 8) + tile] = value
                to = slice(part * COUNT + index * CHUNK, part * COUNT + (index + 1) * CHUNK)
                for pair in range(HALF // 8):
                    row = 2 * HALF * corner + 16 * pair
                    rows_ref[row : row + 16, to] = jnp.concatenate([tiles[2 * pair], tiles[2 * pair + 1]], axis=0).astype(BF16)
        rows = slice(2 * HALF * corner, 2 * HALF * (corner + 1))
        piece = lax.dot_general(rows_ref[rows, 0:COUNT], onehot_ref[...], nt, preferred_element_type=F32)
        piece = piece + lax.dot_general(rows_ref[rows, COUNT:], onehot_ref[...], nt, preferred_element_type=F32)
        acc_ref[corner, :, 0:AROWS] = piece
    total = acc_ref[0]
    for corner in range(1, 4):
        total = total + pltpu.roll(acc_ref[corner], (corner >> 1) * EY + (corner & 1), 1)
    for half in range(2):
        for ch in range(3):
            row = half * HALF + EZ * ch
            to = half * 128 + SZ * ch + OFF
            wide_ref[to : to + EZ, :] = total[row : row + EZ]
    deep_ref[...] = wide_ref[0:128, :].T[0:GROWS]
    vel_ref[...] = wide_ref[128:256, :].T[0:GROWS]
    lane = lane_index(GROUP)
    place = channel_lane(lane)
    low_msg = jnp.zeros((GROUP, 128), F32)
    high_msg = jnp.zeros((GROUP, 128), F32)
    for j in range(5):
        rows = slice(GROUP * j, GROUP * (j + 1))
        deep = deep_ref[rows, :]
        vel = vel_ref[rows, :]
        inside = (place >= 8 * j) & (place < 8 * j + LAYERS)
        low_msg = jnp.where(inside, shift_lanes(deep, 8 * j - OFF), low_msg)
        high_msg = jnp.where(inside, shift_lanes(deep, 8 * j - CZ), high_msg)
        inside = (place >= 8 * j + LAYERS) & (place < 8 * j + LAYERS + 2)
        low_msg = jnp.where(inside, shift_lanes(vel, 8 * j + LAYERS - OFF), low_msg)
        high_msg = jnp.where(inside, shift_lanes(vel, 8 * j + LAYERS - OFF - CZ), high_msg)
    low_ref[...] = low_msg
    high_ref[...] = jnp.where(lane >= 3 * SZ, counts_ref[0].astype(F32), high_msg)


def join_z_kernel(place_ref, deep_ref, vel_ref, before_ref, after_ref, deep_out, vel_out, low_ref, high_ref):
    place = channel_lane(lane_index(GROUP))
    before = jnp.where(place_ref[2] > 0, before_ref[...], 0.0)
    after = after_ref[...]
    deep_low, deep_high = place < LAYERS, (place >= SZ - LAYERS) & (place < SZ)
    vel_low = (place >= OFF) & (place < OFF + 2)
    vel_high = (place >= OFF + CZ) & (place < OFF + CZ + 2)
    for j in range(5):
        rows = slice(GROUP * j, GROUP * (j + 1))
        deep = jnp.where(
            deep_low,
            shift_lanes(before, -8 * j),
            jnp.where(deep_high, shift_lanes(after, SZ - LAYERS - 8 * j), 0.0),
        )
        vel = jnp.where(
            vel_low,
            shift_lanes(before, OFF - 8 * j - LAYERS),
            jnp.where(vel_high, shift_lanes(after, OFF + CZ - 8 * j - LAYERS), 0.0),
        )
        deep_out[rows, :] = deep_ref[rows, :] + deep
        vel_out[rows, :] = vel_ref[rows, :] + vel
    for x in range(EX):
        row = EY * x
        low_ref[LAYERS * x : LAYERS * (x + 1), :] = deep_out[row : row + LAYERS, :]
        high_ref[LAYERS * x : LAYERS * (x + 1), :] = deep_out[row + EY - LAYERS : row + EY, :]
        at = LAYERS * EX + 2 * x
        low_ref[at : at + 2, :] = vel_out[row : row + 2, :]
        high_ref[at : at + 2, :] = vel_out[row + EY - 2 : row + EY, :]


def join_y_kernel(deep_ref, vel_ref, before_ref, after_ref, deep_out, vel_out, low_ref, high_ref):
    deep_out[...] = jnp.zeros_like(deep_out)
    vel_out[...] = jnp.zeros_like(vel_out)
    for x in range(EX):
        row = EY * x
        deep_out[x, OFF : OFF + EY, :] = deep_ref[row : row + EY, :]
        deep_out[x, 0:LAYERS, :] += before_ref[LAYERS * x : LAYERS * (x + 1), :]
        deep_out[x, OFF + CY : OFF + CY + LAYERS, :] += after_ref[LAYERS * x : LAYERS * (x + 1), :]
        at = LAYERS * EX + 2 * x
        vel_out[x, OFF : OFF + EY, :] = vel_ref[row : row + EY, :]
        vel_out[x, OFF : OFF + 2, :] += before_ref[at : at + 2, :]
        vel_out[x, OFF + CY : OFF + CY + 2, :] += after_ref[at : at + 2, :]
    for x in range(LAYERS):
        low_ref[SY * x : SY * (x + 1), :] = deep_out[x, 0:SY, :]
        high_ref[SY * x : SY * (x + 1), :] = deep_out[EX - LAYERS + x, 0:SY, :]
    for x in range(2):
        at = SY * LAYERS + EY * x
        low_ref[at : at + EY, :] = vel_out[x, OFF : OFF + EY, :]
        high_ref[at : at + EY, :] = vel_out[EX - 2 + x, OFF : OFF + EY, :]


def gather_update(index, nodes_ref, part_ref, base_ref, w_ref, g_ref, out_ref, out_index):
    lanes = slice(index * CHUNK, (index + 1) * CHUNK)
    to = slice(out_index * CHUNK, (out_index + 1) * CHUNK)
    onehot = onehot_rows(base_ref, lanes)
    base_z = base_ref[2:3, lanes]
    rows = lax.broadcasted_iota(jnp.int32, (ZROWS, CHUNK), 0) - base_z
    at = rows == 0
    after = rows == 1

    def pick(mask, value):
        kept = jnp.where(mask, value, 0.0)
        total = kept[0:8]
        for t in range(1, ZROWS // 8):
            total = total + kept[8 * t : 8 * t + 8]
        return total

    moved = [jnp.zeros((8, CHUNK), F32) for _ in range(3)]
    velgrad = [[jnp.zeros((8, CHUNK), F32) for _ in range(3)] for _ in range(3)]
    damage_node = jnp.zeros((8, CHUNK), F32)
    rows_ab = 4 * ZROWS
    for corner in range(4):
        start = 2 * rows_ab * corner
        near = jnp.dot(nodes_ref[start : start + rows_ab, 0:AROWS], onehot, preferred_element_type=F32) + jnp.dot(
            nodes_ref[start + rows_ab : start + 2 * rows_ab, 0:AROWS], onehot, preferred_element_type=F32
        )
        for c, mask in enumerate((at, after)):
            k = 2 * corner + c
            weight = w_ref[k : k + 1, lanes]
            slope = [g_ref[j, k : k + 1, lanes] for j in range(3)]
            for i in range(3):
                value = pick(mask, near[ZROWS * i : ZROWS * (i + 1)])
                moved[i] = moved[i] + value * weight
                for j in range(3):
                    velgrad[i][j] = velgrad[i][j] + value * slope[j]
            damage_node = damage_node + pick(mask, near[3 * ZROWS : 4 * ZROWS]) * weight
    moved = [jnp.sum(v, axis=0, keepdims=True) for v in moved]
    velgrad = [[jnp.sum(v, axis=0, keepdims=True) for v in row] for row in velgrad]
    damage_node = jnp.sum(damage_node, axis=0, keepdims=True)

    def field(i):
        return part_ref[i : i + 1, lanes]

    deform = [[field(5 + 3 * i + j) for j in range(3)] for i in range(3)]
    stretch = [[(1.0 if i == j else 0.0) + time_step * velgrad[i][j] for j in range(3)] for i in range(3)]
    mapped = [
        [
            stretch[i][0] * deform[0][j] + stretch[i][1] * deform[1][j] + stretch[i][2] * deform[2][j]
            for j in range(3)
        ]
        for i in range(3)
    ]
    jacobian = (
        mapped[0][0] * (mapped[1][1] * mapped[2][2] - mapped[1][2] * mapped[2][1])
        - mapped[0][1] * (mapped[1][0] * mapped[2][2] - mapped[1][2] * mapped[2][0])
        + mapped[0][2] * (mapped[1][0] * mapped[2][1] - mapped[1][1] * mapped[2][0])
    )
    left = {}
    for i in range(3):
        for j in range(i, 3):
            left[i, j] = left[j, i] = (
                mapped[i][0] * mapped[j][0] + mapped[i][1] * mapped[j][1] + mapped[i][2] * mapped[j][2]
            )
    damaged = jnp.maximum(field(23), damage_node)
    degrade = (1.0 - damaged) ** 2
    pressure = bulk_coef * (jacobian - 1.0)
    energy = (
        0.5 * shear_mod * (left[0, 0] + left[1, 1] + left[2, 2] - 3.0) + 0.5 * bulk_coef * (jacobian - 1.0) ** 2
    )
    out_ref[0:2, to] = part_ref[0:2, lanes]
    for i in range(3):
        out_ref[2 + i : 3 + i, to] = moved[i]
        out_ref[25 + i : 26 + i, to] = field(25 + i) + time_step * moved[i]
        for j in range(3):
            out_ref[5 + 3 * i + j : 6 + 3 * i + j, to] = mapped[i][j]
            term = shear_mod * (left[i, j] - (1.0 if i == j else 0.0))
            if i == j:
                term = term + pressure
            out_ref[14 + 3 * i + j : 15 + 3 * i + j, to] = degrade * term
    out_ref[23:24, to] = damaged
    out_ref[24:25, to] = jnp.maximum(field(24), energy)


def relax_kernel(
    axis_sizes,
    place_ref,
    deep_ref,
    vel_ref,
    before_ref,
    after_ref,
    part_ref,
    base_ref,
    w_ref,
    g_ref,
    damage_hbm,
    nodes_ref,
    tail_ref,
    sums_ref,
    one_ref,
    two_ref,
    keep_ref,
    add_ref,
    spread_ref,
    inverse_ref,
    fv_ref,
    fd_ref,
    damage_ref,
    sem,
):
    count_x, count_y, count_z = axis_sizes
    sums_ref[...] = jnp.zeros_like(sums_ref)
    for xd in range(SX):
        if OFF <= xd < OFF + EX:
            sums_ref[xd] = deep_ref[xd - OFF]
        if xd < LAYERS:
            sums_ref[xd, 0:SY, :] += before_ref[SY * xd : SY * (xd + 1), :]
        if xd >= SX - LAYERS:
            at = SY * (xd - SX + LAYERS)
            sums_ref[xd, 0:SY, :] += after_ref[at : at + SY, :]
    lane = lane_index(PITCH)
    pos_x = place_ref[0] * CX - WIDE + three(lane, SZ, 0, PACK, 2 * PACK)
    pos_y = place_ref[1] * CY - WIDE + lax.broadcasted_iota(jnp.int32, (PITCH, 128), 0)
    pos_z = place_ref[2] * CZ - WIDE + lane - three(lane, SZ, 0, SZ, 2 * SZ)
    inside_yz = (
        (lane < 3 * SZ) & (pos_y >= 0) & (pos_y < count_y * CY) & (pos_z >= 0) & (pos_z < count_z * CZ)
    )
    for j in range(PACK):
        first, second, third = sums_ref[j], sums_ref[j + PACK], sums_ref[j + 2 * PACK]
        mass = three(lane, SZ, first, shift_lanes(second, SZ), shift_lanes(third, 2 * SZ))
        damage = three(lane, SZ, shift_lanes(first, -SZ), second, shift_lanes(third, SZ))
        drive = three(lane, SZ, shift_lanes(first, -2 * SZ), shift_lanes(second, -SZ), third)
        mask = (inside_yz & (pos_x + j >= 0) & (pos_x + j < count_x * CX)).astype(F32)
        inverse = mask / jnp.maximum(mass, mass_floor)
        drive = (2.0 * relax_rate) * (drive * inverse)
        keep_ref[j] = (1.0 - relax_rate * (1.0 + 6.0 * length_sq)) * mask - drive
        add_ref[j] = drive
        spread_ref[j] = (relax_rate * length_sq) * mask
        one_ref[j] = damage * inverse
        inverse_ref[j] = inverse
    source, target = one_ref, two_ref
    for _ in range(SUBSTEPS):
        for j in range(PACK):
            centre = source[j]
            lower = source[j - 1] if j > 0 else shift_lanes(source[PACK - 1], SZ)
            upper = source[j + 1] if j < PACK - 1 else shift_lanes(source[0], -SZ)
            around = (
                (lower + upper)
                + (pltpu.roll(centre, 1, 0) + pltpu.roll(centre, PITCH - 1, 0))
                + (shift_lanes(centre, 1) + shift_lanes(centre, -1))
            )
            target[j] = (centre * keep_ref[j] + add_ref[j]) + spread_ref[j] * around
        source, target = target, source
    for x in range(CX):
        xd = x + WIDE
        value = shift_lanes(source[xd % PACK], -SZ * (xd // PACK) - WIDE)
        damage_ref[x] = value[WIDE : WIDE + CY, 0:CZ]
    move = pltpu.make_async_copy(damage_ref, damage_hbm, sem)
    move.start()
    fv_ref[...] = jnp.zeros_like(fv_ref)
    fd_ref[...] = jnp.zeros_like(fd_ref)
    vel_at = SY * LAYERS
    lane = lane_index(EY)
    for x in range(EX):
        vel = vel_ref[x, OFF : OFF + EY, :]
        if x < 2:
            vel = vel + before_ref[vel_at + EY * x : vel_at + EY * (x + 1), :]
        if x >= EX - 2:
            at = vel_at + EY * (x - EX + 2)
            vel = vel + after_ref[at : at + EY, :]
        slot, group = (x + OFF) % PACK, (x + OFF) // PACK
        inverse = inverse_ref[slot, OFF : OFF + EY, :]
        vel = three(lane, ZROWS, *(shift_lanes(vel, (ZROWS - SZ) * ch - OFF) for ch in range(3)))
        inverse = three(lane, ZROWS, *(shift_lanes(inverse, ZROWS * ch - SZ * group - OFF) for ch in range(3)))
        fv_ref[EY * x : EY * (x + 1), :] = vel * inverse
        fd_ref[EY * x : EY * (x + 1), :] = shift_lanes(source[slot], -SZ * group - OFF)[OFF : OFF + EY, :]
    nodes = jnp.concatenate([fv_ref[...].T[0 : 3 * ZROWS], fd_ref[...].T[0:ZROWS]], axis=0)
    for corner in range(4):
        shift = (corner >> 1) * EY + (corner & 1)
        value = nodes if shift == 0 else pltpu.roll(nodes, 256 - shift, 1)
        high = value.astype(BF16)
        low = (value - high.astype(F32)).astype(BF16)
        start = 8 * ZROWS * corner
        nodes_ref[start : start + 4 * ZROWS, :] = high
        nodes_ref[start + 4 * ZROWS : start + 8 * ZROWS, :] = low
    for index in range(TAIL // CHUNK):
        gather_update((COUNT - TAIL) // CHUNK + index, nodes_ref, part_ref, base_ref, w_ref, g_ref, tail_ref, index)
    move.wait()


def head_kernel(
    counts_ref, prior_ref, nodes_ref, tail_ref, part_ref, base_ref, w_ref, g_ref, out_hbm, head_ref, left_ref, zero_ref, sems
):
    prior = prior_ref[0, 3 * SZ].astype(jnp.int32)
    left = MOST - counts_ref[0]
    zero_ref[...] = jnp.zeros_like(zero_ref)
    blanks = []
    for i in range(MOST):
        to = pl.ds(pl.multiple_of((NBIN + MOST - 1 - i) * BIN, BIN), BIN)
        blanks.append((i < MOST - prior, pltpu.make_async_copy(zero_ref, out_hbm.at[:, to], sems.at[2 + i])))
    for wanted, move in blanks:
        pl.when(wanted)(move.start)
    for i in range(MOST):
        bins = slice(i * BIN, (i + 1) * BIN)
        left_ref[:, bins] = jnp.where(i < left, tail_ref[:, bins], 0.0)
    to = pl.ds(pl.multiple_of((prior + NBIN - MOST) * BIN, BIN), TAIL)
    own = pltpu.make_async_copy(left_ref, out_hbm.at[:, to], sems.at[0])
    own.start()
    for index in range((COUNT - TAIL) // CHUNK):
        gather_update(index, nodes_ref, part_ref, base_ref, w_ref, g_ref, head_ref, index)
    to = pl.ds(pl.multiple_of(prior * BIN, BIN), COUNT - TAIL)
    stay = pltpu.make_async_copy(head_ref, out_hbm.at[:, to], sems.at[1])
    stay.start()
    for wanted, move in blanks:
        pl.when(wanted)(move.wait)
    own.wait()
    stay.wait()


def arrive_kernel(prior_ref, recv_ref, partial_hbm, out_hbm, sems):
    prior = prior_ref[0, 3 * SZ].astype(jnp.int32)
    moves = []
    for slot in range(MOST):
        source = pl.ds(pl.multiple_of(jnp.minimum(MOST - prior + slot, MOST - 1) * BIN, BIN), BIN)
        moves.append(
            (
                slot < prior,
                pltpu.make_async_copy(recv_ref.at[:, source], out_hbm.at[:, slot * BIN : (slot + 1) * BIN], sems.at[slot]),
            )
        )
    for wanted, move in moves:
        pl.when(wanted)(move.start)
    for wanted, move in moves:
        pl.when(wanted)(move.wait)


def shape(*dims, kind=F32):
    return jax.ShapeDtypeStruct(dims, kind)


SMEM = pltpu.SMEM
HBM = pltpu.HBM


def call(kernel, out_shape, spaces, args, out_spaces=None, scratch=(), flops=0, aliases=None, limit=None):
    leaves = jax.tree.leaves(out_shape)
    out_spaces = out_spaces or [VMEM] * len(leaves)
    out_specs = [pl.BlockSpec(memory_space=s) for s in out_spaces]
    return pl.pallas_call(
        kernel,
        out_shape=out_shape,
        in_specs=[pl.BlockSpec(memory_space=s) for s in spaces],
        out_specs=tuple(out_specs) if isinstance(out_shape, tuple) else out_specs[0],
        scratch_shapes=list(scratch),
        input_output_aliases=aliases or {},
        compiler_params=pltpu.CompilerParams(vmem_limit_bytes=(limit or 48 * 1024) * 1024),
        cost_estimate=pl.CostEstimate(flops=flops, bytes_accessed=2000000, transcendentals=0),
    )(*args)


def exchange(low, high, axis, ring=False):
    count = lax.axis_size(axis)
    up = [(i, (i + 1) % count) for i in range(count if ring else count - 1)]
    down = [(i + 1, i) for i in range(count - 1)]
    return lax.ppermute(high, axis, up), lax.ppermute(low, axis, down)


def per_device(particles, stencil_base, weights, gradients, counts):
    axes = ("gx", "gy", "gz")
    place = jnp.stack([lax.axis_index(a) for a in axes]).astype(jnp.int32)
    sizes = tuple(lax.axis_size(a) for a in axes)
    ring = [(i, (i + 1) % sizes[2]) for i in range(sizes[2])]
    inputs = (particles, stencil_base, weights, gradients)
    deep, vel, low, high = call(
        scatter_kernel,
        (VMEM((GROWS, 128), F32), VMEM((GROWS, 128), F32), VMEM((GROUP, 128), F32), VMEM((GROUP, 128), F32)),
        [SMEM] + [HBM] * 4,
        (counts,) + inputs,
        scratch=[
            VMEM((FIELDS, COUNT), F32),
            VMEM((3, COUNT), jnp.int32),
            VMEM((8, COUNT), F32),
            VMEM((3, 8, COUNT), F32),
            VMEM((4, 2 * HALF, 256), F32),
            VMEM((256, 256), F32),
            VMEM((2, 6, 8, COUNT), F32),
            VMEM((8 * HALF, 2 * COUNT), BF16),
            VMEM((AROWS, COUNT), BF16),
            pltpu.SemaphoreType.DMA((4,)),
        ],
        limit=SCATTER_KIB,
    )
    before_z, after_z = exchange(low, high, "gz", ring=True)
    message = LAYERS * EX + 2 * EX
    deep, vel, low, high = call(
        join_z_kernel,
        (shape(GROWS, 128), shape(GROWS, 128), shape(message, 128), shape(message, 128)),
        [SMEM] + [VMEM] * 4,
        (place, deep, vel, before_z, after_z),
    )
    before, after = exchange(low, high, "gy")
    message = LAYERS * SY + 2 * EY
    deep, vel, low, high = call(
        join_y_kernel,
        (shape(EX, PITCH, 128), shape(EX, PITCH, 128), shape(message, 128), shape(message, 128)),
        [VMEM] * 4,
        (deep, vel, before, after),
    )
    before, after = exchange(low, high, "gx")

    def relax(*refs):
        relax_kernel(sizes, *refs)

    damage, nodes, tail = call(
        relax,
        (shape(CX, CY, CZ), shape(32 * ZROWS, 256, kind=BF16), shape(FIELDS, TAIL)),
        [SMEM] + [VMEM] * 8,
        (place, deep, vel, before, after) + inputs,
        out_spaces=[HBM, VMEM, VMEM],
        scratch=[VMEM((SX, PITCH, 128), F32)]
        + [VMEM((PACK, PITCH, 128), F32)] * 6
        + [VMEM((256, 128), F32)] * 2
        + [VMEM((CX, CY, CZ), F32), pltpu.SemaphoreType.DMA],
    )
    recv = lax.ppermute(tail, "gz", ring)
    prior = before_z[0:8]
    own = call(
        head_kernel,
        shape(FIELDS, SLOTS),
        [SMEM] + [VMEM] * 7,
        (counts, prior, nodes, tail) + inputs,
        out_spaces=[HBM],
        scratch=[
            VMEM((FIELDS, COUNT - TAIL), F32),
            VMEM((FIELDS, TAIL), F32),
            VMEM((FIELDS, BIN), F32),
            pltpu.SemaphoreType.DMA((2 + MOST,)),
        ],
        flops=2 * 1280 * 256 * 1024,
    )
    migrated = call(
        arrive_kernel,
        shape(FIELDS, SLOTS),
        [VMEM, VMEM, HBM],
        (prior, recv, own),
        out_spaces=[HBM],
        scratch=[pltpu.SemaphoreType.DMA((MOST,))],
        aliases={2: 0},
    )
    return (migrated, damage)


def solution(mesh):
    return jax.shard_map(
        per_device,
        mesh=mesh,
        in_specs=(
            P(None, ("gx", "gy", "gz")),
            P(None, ("gx", "gy", "gz")),
            P(None, ("gx", "gy", "gz")),
            P(None, None, ("gx", "gy", "gz")),
            P(("gx", "gy", "gz")),
        ),
        out_specs=(P(None, ("gx", "gy", "gz")), P("gx", "gy", "gz")),
        check_vma=False,
    )
```

time: 66.5 us -> 58.7 us (0.88)
  Pallas kernels: 14.1 us -> 10.3 us
  local copies, waits for them, and re-layouts: 3.49 us -> 0.02 us
    pallas_call x6, Pallas kernels: 14.1 us -> 10.3 us  [call(): pl.pallas_call(kernel, out_shape=out_shape, in_specs=[pl.BlockSpec(memory...]
    unnamed x16 -> x8, local copies, waits for them, and re-layouts: 3.49 us -> 0.02 us
  transfers between devices with their start and end apart: 7 -> 7, of which waited for: 4 -> 4; matrix products, arithmetic and copies ran while one was open for 0% -> 0% of each run, Pallas kernels for 3% -> 4%
where the time goes in v2:
time: 58.7 us; the launch traced here: 58.4 us
  starting transfers between devices  26.2 us (45%)
  waiting for transfers between devices  20.3 us (35%)
  Pallas kernels  10.3 us (18%)
  between operations  1.43 us (2%)
    ppermute x6, starting transfers between devices, exchange(): return (lax.ppermute(high, axis, up), lax.ppermute(low, axis, down))  23.3 us
    ppermute x6, waiting for transfers between devices, exchange(): return (lax.ppermute(high, axis, up), lax.ppermute(low, axis, down))  16.3 us
    pallas_call x6, Pallas kernels, call(): pl.pallas_call(kernel, out_shape=out_shape, in_specs=[pl.BlockSpec(memory...  10.3 us
    ppermute x1, waiting for transfers between devices, per_device(): recv = lax.ppermute(tail, 'gz', ring)  4.02 us
    ppermute x1, starting transfers between devices, per_device(): recv = lax.ppermute(tail, 'gz', ring)  2.91 us
  transfers between devices with their start and end apart: 7, of which 4 were waited for; matrix products, arithmetic and copies ran while one was open for 0% of the time, Pallas kernels for 4%

profile of v2, /device:TPU:1, one launch (start us, length us, event | category | flops | bytes accessed | tf_op | source)
XLA Modules:
  0.0 58.4 jit_solution(7715905416103001696)
XLA Ops:
  1.3 3.9 %shard_map.68 = (f32[200,128]{1,0:T(8,128)S(1)}, f32[200,128]{1,0:T(8,128)S(1)}, f32[40,128]{1,0:T(8,128)S(1)}, f32[40,128]{1,0:T(8,128)S(1)}) custom-call(s32[1]{0:T(128)S(6)} %copy.9.counts_ref, f32[28,2048]{1,0:T(8,128)} %part_ref.1, s32[3,2048]{1,0:T(4,128)} %base_ref.1, f32[8,2048]{1,0:T(8,128)} %w_ref.1, f32[3,8,2048]{2,1,0:T(8,128)} %g_ref.1), custom_call_target="tpu_custom_call" | custom-call | bytes 2000000 | tf_op jit(solution)/shard_map/pallas_call | solution.py:479
  5.2 4.0 %collective-permute-start = (f32[40,128]{1,0:T(8,128)S(1)}, f32[40,128]{1,0:T(8,128)S(1)}, u32[]{:S(2)}, u32[]{:S(2)}) collective-permute-start(f32[40,128]{1,0:T(8,128)S(1)} %get-tuple-element.17), channel_id=1, source_target_pairs={{0,1},{1,2},{2,3},{3,4},{4,5},{5,6},{6,7},{7,8},{8,9},{9,10},{10,1... | collective-permute-start | bytes 61448 | tf_op jit(solution)/shard_map/ppermute | solution.py:495
  9.3 1.3 %collective-permute-start.1 = (f32[40,128]{1,0:T(8,128)S(1)}, f32[40,128]{1,0:T(8,128)S(1)}, u32[]{:S(2)}, u32[]{:S(2)}) collective-permute-start(f32[40,128]{1,0:T(8,128)S(1)} %get-tuple-element.20), channel_id=1, source_target_pairs={{1,0},{2,1},{3,2},{4,3},{5,4},{6,5},{7,6},{8,7},{9,8},{10,9},{11,1... | collective-permute-start | bytes 61448 | tf_op jit(solution)/shard_map/ppermute | solution.py:495
  10.6 0.0 copy-start.3
  10.6 0.1 pad_add_fusion.place_ref.refs_0_
  10.7 3.4 %collective-permute-done.before_ref = f32[40,128]{1,0:T(8,128)S(1)} collective-permute-done((f32[40,128]{1,0:T(8,128)S(1)}, f32[40,128]{1,0:T(8,128)S(1)}, u32[]{:S(2)}, u32[]{:S(2)}) %collective-permute-start) | collective-permute-done | bytes 20512 | tf_op jit(solution)/shard_map/ppermute | solution.py:495
  14.1 0.0 collective-permute-done.1.after_ref
  14.1 0.0 copy-start
  14.1 0.7 %shard_map.69 = (f32[200,128]{1,0:T(8,128)S(1)}, f32[200,128]{1,0:T(8,128)S(1)}, f32[80,128]{1,0:T(8,128)S(1)}, f32[80,128]{1,0:T(8,128)S(1)}) custom-call(s32[3]{0:T(128)S(1)} %pad_add_fusion.place_ref.refs_0_, f32[200,128]{1,0:T(8,128)S(1)} %get-tuple-element.18.deep_ref, f32[200,128]{1,0:T(8,128)S(1)} %get-tuple-element.19.vel_ref, ...), custom_call_target="tpu_custom_call" | custom-call | bytes 2000000 | tf_op jit(solution)/shard_map/pallas_call | solution.py:479
  14.8 0.0 copy-start.1
  14.8 9.0 %collective-permute-start.2 = (f32[80,128]{1,0:T(8,128)S(1)}, f32[80,128]{1,0:T(8,128)S(1)}, u32[]{:S(2)}, u32[]{:S(2)}) collective-permute-start(f32[80,128]{1,0:T(8,128)S(1)} %get-tuple-element.23), channel_id=1, source_target_pairs={{0,16},{16,32},{32,48},{1,17},{17,33},{33,49},{2,18},{18,34},{34,5... | collective-permute-start | bytes 122888 | tf_op jit(solution)/shard_map/ppermute | solution.py:495
  23.8 1.3 %collective-permute-start.3 = (f32[80,128]{1,0:T(8,128)S(1)}, f32[80,128]{1,0:T(8,128)S(1)}, u32[]{:S(2)}, u32[]{:S(2)}) collective-permute-start(f32[80,128]{1,0:T(8,128)S(1)} %get-tuple-element.24), channel_id=1, source_target_pairs={{16,0},{32,16},{48,32},{17,1},{33,17},{49,33},{18,2},{34,18},{50,3... | collective-permute-start | bytes 122888 | tf_op jit(solution)/shard_map/ppermute | solution.py:495
  25.1 0.0 collective-permute-done.2.before_ref
  25.1 8.9 %collective-permute-done.3.after_ref = f32[80,128]{1,0:T(8,128)S(1)} collective-permute-done((f32[80,128]{1,0:T(8,128)S(1)}, f32[80,128]{1,0:T(8,128)S(1)}, u32[]{:S(2)}, u32[]{:S(2)}) %collective-permute-start.3) | collective-permute-done | bytes 40992 | tf_op jit(solution)/shard_map/ppermute | solution.py:495
  34.0 0.0 copy-start.2
  34.0 0.1 shard_map.70
  34.1 5.8 %collective-permute-start.4 = (f32[192,128]{1,0:T(8,128)S(1)}, f32[192,128]{1,0:T(8,128)S(1)}, u32[]{:S(2)}, u32[]{:S(2)}) collective-permute-start(f32[192,128]{1,0:T(8,128)S(1)} %get-tuple-element.27), channel_id=1, source_target_pairs={{0,64},{64,128},{128,192},{192,256},{256,320},{320,384},{384,448},... | collective-permute-start | bytes 294920 | tf_op jit(solution)/shard_map/ppermute | solution.py:495
  39.9 1.9 %collective-permute-start.5 = (f32[192,128]{1,0:T(8,128)S(1)}, f32[192,128]{1,0:T(8,128)S(1)}, u32[]{:S(2)}, u32[]{:S(2)}) collective-permute-start(f32[192,128]{1,0:T(8,128)S(1)} %get-tuple-element.28), channel_id=1, source_target_pairs={{64,0},{128,64},{192,128},{256,192},{320,256},{384,320},{448,384},... | collective-permute-start | bytes 294920 | tf_op jit(solution)/shard_map/ppermute | solution.py:495
  41.8 0.0 collective-permute-done.4.refs_3_
  41.8 4.0 %collective-permute-done.5.refs_4_ = f32[192,128]{1,0:T(8,128)S(1)} collective-permute-done((f32[192,128]{1,0:T(8,128)S(1)}, f32[192,128]{1,0:T(8,128)S(1)}, u32[]{:S(2)}, u32[]{:S(2)}) %collective-permute-start.5) | collective-permute-done | bytes 98336 | tf_op jit(solution)/shard_map/ppermute | solution.py:495
  45.8 0.0 copy-done.3
  45.8 0.0 copy-done
  45.8 0.0 copy-done.1
  45.9 0.0 copy-done.2
  45.9 2.7 %shard_map.71 = (f32[8,16,32]{2,1,0:T(8,128)}, bf16[1280,256]{1,0:T(8,128)(2,1)S(1)}, f32[28,1024]{1,0:T(8,128)S(1)}) custom-call(s32[3]{0:T(128)S(1)} %pad_add_fusion.place_ref.refs_0_, f32[10,32,128]{2,1,0:T(8,128)S(1)} %get-tuple-element.25.refs_1_, f32[10,32,128]{2,1,0:T(8,128)S(1)} %get-tuple-element.26.refs_2_, ...), custom_call_target="tpu_custom_call" | custom-call | bytes 2000000 | tf_op jit(solution)/shard_map/pallas_call | solution.py:479
  48.5 2.9 %collective-permute-start.6 = (f32[28,1024]{1,0:T(8,128)S(1)}, f32[28,1024]{1,0:T(8,128)S(1)}, u32[]{:S(2)}, u32[]{:S(2)}) collective-permute-start(f32[28,1024]{1,0:T(8,128)S(1)} %get-tuple-element.29.tail_ref), channel_id=1, source_target_pairs={{0,1},{1,2},{2,3},{3,4},{4,5},{5,6},{6,7},{7,8},{8,9},{9,10},{10,1... | collective-permute-start | bytes 344072 | tf_op jit(solution)/shard_map/ppermute | solution.py:555
  51.5 2.1 %shard_map.72.partial_hbm = f32[28,3072]{1,0:T(8,128)} custom-call(s32[1]{0:T(128)S(6)} %copy.9.counts_ref, f32[8,128]{1,0:T(8,128)S(1)} %slice.4.prior_ref, bf16[1280,256]{1,0:T(8,128)(2,1)S(1)} %get-tuple-element.30.nodes_ref, f32[28,1024]{1,0:T(8,128)S(1)} %get-tuple-element.29.tail_ref, f32[28,2048]{1,0:T(8,128)S(1)} %copy-done, ...), custom_call_target="tpu_custom_call" | custom-call | flops 671088640 | bytes 2000000 | tf_op jit(solution)/shard_map/pallas_call | solution.py:479
  53.5 4.0 %collective-permute-done.6.recv_ref = f32[28,1024]{1,0:T(8,128)S(1)} collective-permute-done((f32[28,1024]{1,0:T(8,128)S(1)}, f32[28,1024]{1,0:T(8,128)S(1)}, u32[]{:S(2)}, u32[]{:S(2)}) %collective-permute-start.6) | collective-permute-done | bytes 114720 | tf_op jit(solution)/shard_map/ppermute | solution.py:555
  57.6 0.8 %shard_map.73 = f32[28,3072]{1,0:T(8,128)} custom-call(f32[8,128]{1,0:T(8,128)S(1)} %slice.4.prior_ref, f32[28,1024]{1,0:T(8,128)S(1)} %collective-permute-done.6.recv_ref, f32[28,3072]{1,0:T(8,128)} %shard_map.72.partial_hbm), custom_call_target="tpu_custom_call", output_to_operand_aliasing={{}: (2, {})} | custom-call | bytes 2000000 | tf_op jit(solution)/shard_map/pallas_call | solution.py:479
  (1 shorter events, 0.0 us)
Async XLA Ops:
  5.2 8.8 %collective-permute-start = (f32[40,128]{1,0:T(8,128)S(1)}, f32[40,128]{1,0:T(8,128)S(1)}, u32[]{:S(2)}, u32[]{:S(2)}) collective-permute-start(f32[40,128]{1,0:T(8,128)S(1)} %get-tuple-element.17), channel_id=1, source_target_pairs={{0,1},{1,2},{2,3},{3,4},{4,5},{5,6},{6,7},{7,8},{8,9},{9,10},{10,1... | collective-permute-start | bytes 61448 | tf_op jit(solution)/shard_map/ppermute | solution.py:495
  9.3 4.8 %collective-permute-start.1 = (f32[40,128]{1,0:T(8,128)S(1)}, f32[40,128]{1,0:T(8,128)S(1)}, u32[]{:S(2)}, u32[]{:S(2)}) collective-permute-start(f32[40,128]{1,0:T(8,128)S(1)} %get-tuple-element.20), channel_id=1, source_target_pairs={{1,0},{2,1},{3,2},{4,3},{5,4},{6,5},{7,6},{8,7},{9,8},{10,9},{11,1... | collective-permute-start | bytes 61448 | tf_op jit(solution)/shard_map/ppermute | solution.py:495
  10.6 35.3 %copy-start.3 = (s32[3,2048]{1,0:T(4,128)S(1)}, s32[3,2048]{1,0:T(4,128)}, u32[]{:S(2)}) copy-start(s32[3,2048]{1,0:T(4,128)} %base_ref.1) | copy-start | bytes 73732
  14.1 31.8 %copy-start = (f32[28,2048]{1,0:T(8,128)S(1)}, f32[28,2048]{1,0:T(8,128)}, u32[]{:S(2)}) copy-start(f32[28,2048]{1,0:T(8,128)} %part_ref.1) | copy-start | bytes 688132
  14.8 31.1 %copy-start.1 = (f32[3,8,2048]{2,1,0:T(8,128)S(1)}, f32[3,8,2048]{2,1,0:T(8,128)}, u32[]{:S(2)}) copy-start(f32[3,8,2048]{2,1,0:T(8,128)} %g_ref.1) | copy-start | bytes 589828
  14.8 10.3 %collective-permute-start.2 = (f32[80,128]{1,0:T(8,128)S(1)}, f32[80,128]{1,0:T(8,128)S(1)}, u32[]{:S(2)}, u32[]{:S(2)}) collective-permute-start(f32[80,128]{1,0:T(8,128)S(1)} %get-tuple-element.23), channel_id=1, source_target_pairs={{0,16},{16,32},{32,48},{1,17},{17,33},{33,49},{2,18},{18,34},{34,5... | collective-permute-start | bytes 122888 | tf_op jit(solution)/shard_map/ppermute | solution.py:495
  23.8 10.2 %collective-permute-start.3 = (f32[80,128]{1,0:T(8,128)S(1)}, f32[80,128]{1,0:T(8,128)S(1)}, u32[]{:S(2)}, u32[]{:S(2)}) collective-permute-start(f32[80,128]{1,0:T(8,128)S(1)} %get-tuple-element.24), channel_id=1, source_target_pairs={{16,0},{32,16},{48,32},{17,1},{33,17},{49,33},{18,2},{34,18},{50,3... | collective-permute-start | bytes 122888 | tf_op jit(solution)/shard_map/ppermute | solution.py:495
  34.0 11.9 %copy-start.2 = (f32[8,2048]{1,0:T(8,128)S(1)}, f32[8,2048]{1,0:T(8,128)}, u32[]{:S(2)}) copy-start(f32[8,2048]{1,0:T(8,128)} %w_ref.1) | copy-start | bytes 196612
  34.1 7.8 %collective-permute-start.4 = (f32[192,128]{1,0:T(8,128)S(1)}, f32[192,128]{1,0:T(8,128)S(1)}, u32[]{:S(2)}, u32[]{:S(2)}) collective-permute-start(f32[192,128]{1,0:T(8,128)S(1)} %get-tuple-element.27), channel_id=1, source_target_pairs={{0,64},{64,128},{128,192},{192,256},{256,320},{320,384},{384,448},... | collective-permute-start | bytes 294920 | tf_op jit(solution)/shard_map/ppermute | solution.py:495
  39.9 5.9 %collective-permute-start.5 = (f32[192,128]{1,0:T(8,128)S(1)}, f32[192,128]{1,0:T(8,128)S(1)}, u32[]{:S(2)}, u32[]{:S(2)}) collective-permute-start(f32[192,128]{1,0:T(8,128)S(1)} %get-tuple-element.28), channel_id=1, source_target_pairs={{64,0},{128,64},{192,128},{256,192},{320,256},{384,320},{448,384},... | collective-permute-start | bytes 294920 | tf_op jit(solution)/shard_map/ppermute | solution.py:495
  48.5 9.0 %collective-permute-start.6 = (f32[28,1024]{1,0:T(8,128)S(1)}, f32[28,1024]{1,0:T(8,128)S(1)}, u32[]{:S(2)}, u32[]{:S(2)}) collective-permute-start(f32[28,1024]{1,0:T(8,128)S(1)} %get-tuple-element.29.tail_ref), channel_id=1, source_target_pairs={{0,1},{1,2},{2,3},{3,4},{4,5},{5,6},{6,7},{7,8},{8,9},{9,10},{10,1... | collective-permute-start | bytes 344072 | tf_op jit(solution)/shard_map/ppermute | solution.py:555

commit v3 on v2

--- a/solution.py
+++ b/solution.py
@@ -209,7 +209,7 @@
         high_ref[at : at + 2, :] = vel_out[row + EY - 2 : row + EY, :]
 
 
-def join_y_kernel(deep_ref, vel_ref, before_ref, after_ref, deep_out, vel_out, low_ref, high_ref):
+def join_y_kernel(deep_ref, vel_ref, after_ref, before_ref, deep_out, vel_out, low_ref, high_ref):
     deep_out[...] = jnp.zeros_like(deep_out)
     vel_out[...] = jnp.zeros_like(vel_out)
     for x in range(EX):
@@ -317,8 +317,8 @@
     place_ref,
     deep_ref,
     vel_ref,
+    after_ref,
     before_ref,
-    after_ref,
     part_ref,
     base_ref,
     w_ref,
@@ -492,7 +492,8 @@
     count = lax.axis_size(axis)
     up = [(i, (i + 1) % count) for i in range(count if ring else count - 1)]
     down = [(i + 1, i) for i in range(count - 1)]
-    return lax.ppermute(high, axis, up), lax.ppermute(low, axis, down)
+    after = lax.ppermute(low, axis, down)
+    return lax.ppermute(high, axis, up), after
 
 
 def per_device(particles, stencil_base, weights, gradients, counts):
@@ -534,7 +535,7 @@
         join_y_kernel,
         (shape(EX, PITCH, 128), shape(EX, PITCH, 128), shape(message, 128), shape(message, 128)),
         [VMEM] * 4,
-        (deep, vel, before, after),
+        (deep, vel, after, before),
     )
     before, after = exchange(low, high, "gx")
 
@@ -545,7 +546,7 @@
         relax,
         (shape(CX, CY, CZ), shape(32 * ZROWS, 256, kind=BF16), shape(FIELDS, TAIL)),
         [SMEM] + [VMEM] * 8,
-        (place, deep, vel, before, after) + inputs,
+        (place, deep, vel, after, before) + inputs,
         out_spaces=[HBM, VMEM, VMEM],
         scratch=[VMEM((SX, PITCH, 128), F32)]
         + [VMEM((PACK, PITCH, 128), F32)] * 6

time: 58.7 us -> 53.2 us (0.906)
  waiting for transfers between devices: 20.3 us -> 12.5 us
  starting transfers between devices: 26.2 us -> 28.6 us
    ppermute x6, waiting for transfers between devices: 16.3 us -> 6.08 us  [the longest x3 6.07 us: exchange(): return (lax.ppermute(high, axis, up), after)]
    ppermute x6, starting transfers between devices: 23.3 us -> 26.6 us  [the longest x3 15.4 us: exchange(): return (lax.ppermute(high, axis, up), after)]
    ppermute x1, waiting for transfers between devices: 4.02 us -> 6.41 us  [per_device(): recv = lax.ppermute(tail, 'gz', ring)]
    ppermute x1, starting transfers between devices: 2.91 us -> 1.92 us  [per_device(): recv = lax.ppermute(tail, 'gz', ring)]
where the time goes in v3:
time: 53.2 us; the launch traced here: 52.9 us
  starting transfers between devices  28.6 us (54%)
  waiting for transfers between devices  12.5 us (23%)
  Pallas kernels  10.3 us (19%)
  between operations  1.42 us (3%)
    ppermute x3, starting transfers between devices, exchange(): return (lax.ppermute(high, axis, up), after)  15.4 us
    ppermute x3, starting transfers between devices, exchange(): after = lax.ppermute(low, axis, down)  11.2 us
    pallas_call x6, Pallas kernels, call(): pl.pallas_call(kernel, out_shape=out_shape, in_specs=[pl.BlockSpec(memory...  10.3 us
    ppermute x1, waiting for transfers between devices, per_device(): recv = lax.ppermute(tail, 'gz', ring)  6.41 us
    ppermute x3, waiting for transfers between devices, exchange(): return (lax.ppermute(high, axis, up), after)  6.07 us
    ppermute x1, starting transfers between devices, per_device(): recv = lax.ppermute(tail, 'gz', ring)  1.92 us
  transfers between devices with their start and end apart: 7, of which 4 were waited for; matrix products, arithmetic and copies ran while one was open for 0% of the time, Pallas kernels for 4%

profile of v3, /device:TPU:1, one launch (start us, length us, event | category | flops | bytes accessed | tf_op | source)
XLA Modules:
  0.0 52.9 jit_solution(1151296831981190647)
XLA Ops:
  1.3 3.9 %shard_map.68 = (f32[200,128]{1,0:T(8,128)S(1)}, f32[200,128]{1,0:T(8,128)S(1)}, f32[40,128]{1,0:T(8,128)S(1)}, f32[40,128]{1,0:T(8,128)S(1)}) custom-call(s32[1]{0:T(128)S(6)} %copy.9.counts_ref, f32[28,2048]{1,0:T(8,128)} %part_ref.1, s32[3,2048]{1,0:T(4,128)} %base_ref.1, f32[8,2048]{1,0:T(8,128)} %w_ref.1, f32[3,8,2048]{2,1,0:T(8,128)} %g_ref.1), custom_call_target="tpu_custom_call" | custom-call | bytes 2000000 | tf_op jit(solution)/shard_map/pallas_call | solution.py:479
  5.2 4.0 %collective-permute-start = (f32[40,128]{1,0:T(8,128)S(1)}, f32[40,128]{1,0:T(8,128)S(1)}, u32[]{:S(2)}, u32[]{:S(2)}) collective-permute-start(f32[40,128]{1,0:T(8,128)S(1)} %get-tuple-element.17), channel_id=1, source_target_pairs={{0,1},{1,2},{2,3},{3,4},{4,5},{5,6},{6,7},{7,8},{8,9},{9,10},{10,1... | collective-permute-start | bytes 61448 | tf_op jit(solution)/shard_map/ppermute | solution.py:496
  9.3 1.3 %collective-permute-start.1 = (f32[40,128]{1,0:T(8,128)S(1)}, f32[40,128]{1,0:T(8,128)S(1)}, u32[]{:S(2)}, u32[]{:S(2)}) collective-permute-start(f32[40,128]{1,0:T(8,128)S(1)} %get-tuple-element.20), channel_id=1, source_target_pairs={{1,0},{2,1},{3,2},{4,3},{5,4},{6,5},{7,6},{8,7},{9,8},{10,9},{11,1... | collective-permute-start | bytes 61448 | tf_op jit(solution)/shard_map/ppermute | solution.py:495
  10.6 0.0 copy-start.3
  10.6 0.1 pad_add_fusion.place_ref.refs_0_
  10.7 3.4 %collective-permute-done.before_ref = f32[40,128]{1,0:T(8,128)S(1)} collective-permute-done((f32[40,128]{1,0:T(8,128)S(1)}, f32[40,128]{1,0:T(8,128)S(1)}, u32[]{:S(2)}, u32[]{:S(2)}) %collective-permute-start) | collective-permute-done | bytes 20512 | tf_op jit(solution)/shard_map/ppermute | solution.py:496
  14.1 0.0 collective-permute-done.1.after_ref
  14.1 0.0 copy-start
  14.1 0.7 %shard_map.69 = (f32[200,128]{1,0:T(8,128)S(1)}, f32[200,128]{1,0:T(8,128)S(1)}, f32[80,128]{1,0:T(8,128)S(1)}, f32[80,128]{1,0:T(8,128)S(1)}) custom-call(s32[3]{0:T(128)S(1)} %pad_add_fusion.place_ref.refs_0_, f32[200,128]{1,0:T(8,128)S(1)} %get-tuple-element.18.deep_ref, f32[200,128]{1,0:T(8,128)S(1)} %get-tuple-element.19.vel_ref, ...), custom_call_target="tpu_custom_call" | custom-call | bytes 2000000 | tf_op jit(solution)/shard_map/pallas_call | solution.py:479
  14.8 0.0 copy-start.1
  14.8 1.4 %collective-permute-start.2 = (f32[80,128]{1,0:T(8,128)S(1)}, f32[80,128]{1,0:T(8,128)S(1)}, u32[]{:S(2)}, u32[]{:S(2)}) collective-permute-start(f32[80,128]{1,0:T(8,128)S(1)} %get-tuple-element.23), channel_id=1, source_target_pairs={{16,0},{32,16},{48,32},{17,1},{33,17},{49,33},{18,2},{34,18},{50,3... | collective-permute-start | bytes 122888 | tf_op jit(solution)/shard_map/ppermute | solution.py:495
  16.2 9.5 %collective-permute-start.3 = (f32[80,128]{1,0:T(8,128)S(1)}, f32[80,128]{1,0:T(8,128)S(1)}, u32[]{:S(2)}, u32[]{:S(2)}) collective-permute-start(f32[80,128]{1,0:T(8,128)S(1)} %get-tuple-element.24), channel_id=1, source_target_pairs={{0,16},{16,32},{32,48},{1,17},{17,33},{33,49},{2,18},{18,34},{34,5... | collective-permute-start | bytes 122888 | tf_op jit(solution)/shard_map/ppermute | solution.py:496
  25.7 0.0 collective-permute-done.2.after_ref
  25.7 1.1 %collective-permute-done.3.before_ref = f32[80,128]{1,0:T(8,128)S(1)} collective-permute-done((f32[80,128]{1,0:T(8,128)S(1)}, f32[80,128]{1,0:T(8,128)S(1)}, u32[]{:S(2)}, u32[]{:S(2)}) %collective-permute-start.3) | collective-permute-done | bytes 40992 | tf_op jit(solution)/shard_map/ppermute | solution.py:496
  26.8 0.0 copy-start.2
  26.8 0.1 shard_map.70
  26.9 8.5 %collective-permute-start.4 = (f32[192,128]{1,0:T(8,128)S(1)}, f32[192,128]{1,0:T(8,128)S(1)}, u32[]{:S(2)}, u32[]{:S(2)}) collective-permute-start(f32[192,128]{1,0:T(8,128)S(1)} %get-tuple-element.27), channel_id=1, source_target_pairs={{64,0},{128,64},{192,128},{256,192},{320,256},{384,320},{448,384},... | collective-permute-start | bytes 294920 | tf_op jit(solution)/shard_map/ppermute | solution.py:495
  35.4 1.9 %collective-permute-start.5 = (f32[192,128]{1,0:T(8,128)S(1)}, f32[192,128]{1,0:T(8,128)S(1)}, u32[]{:S(2)}, u32[]{:S(2)}) collective-permute-start(f32[192,128]{1,0:T(8,128)S(1)} %get-tuple-element.28), channel_id=1, source_target_pairs={{0,64},{64,128},{128,192},{192,256},{256,320},{320,384},{384,448},... | collective-permute-start | bytes 294920 | tf_op jit(solution)/shard_map/ppermute | solution.py:496
  37.3 0.0 collective-permute-done.4.refs_3_
  37.3 1.6 %collective-permute-done.5.refs_4_ = f32[192,128]{1,0:T(8,128)S(1)} collective-permute-done((f32[192,128]{1,0:T(8,128)S(1)}, f32[192,128]{1,0:T(8,128)S(1)}, u32[]{:S(2)}, u32[]{:S(2)}) %collective-permute-start.5) | collective-permute-done | bytes 98336 | tf_op jit(solution)/shard_map/ppermute | solution.py:496
  39.0 0.0 copy-done.3
  39.0 0.0 copy-done
  39.0 0.0 copy-done.1
  39.0 0.0 copy-done.2
  39.0 2.7 %shard_map.71 = (f32[8,16,32]{2,1,0:T(8,128)}, bf16[1280,256]{1,0:T(8,128)(2,1)S(1)}, f32[28,1024]{1,0:T(8,128)S(1)}) custom-call(s32[3]{0:T(128)S(1)} %pad_add_fusion.place_ref.refs_0_, f32[10,32,128]{2,1,0:T(8,128)S(1)} %get-tuple-element.25.refs_1_, f32[10,32,128]{2,1,0:T(8,128)S(1)} %get-tuple-element.26.refs_2_, ...), custom_call_target="tpu_custom_call" | custom-call | bytes 2000000 | tf_op jit(solution)/shard_map/pallas_call | solution.py:479
  41.6 1.9 %collective-permute-start.6 = (f32[28,1024]{1,0:T(8,128)S(1)}, f32[28,1024]{1,0:T(8,128)S(1)}, u32[]{:S(2)}, u32[]{:S(2)}) collective-permute-start(f32[28,1024]{1,0:T(8,128)S(1)} %get-tuple-element.29.tail_ref), channel_id=1, source_target_pairs={{0,1},{1,2},{2,3},{3,4},{4,5},{5,6},{6,7},{7,8},{8,9},{9,10},{10,1... | collective-permute-start | bytes 344072 | tf_op jit(solution)/shard_map/ppermute | solution.py:556
  43.6 2.1 %shard_map.72.partial_hbm = f32[28,3072]{1,0:T(8,128)} custom-call(s32[1]{0:T(128)S(6)} %copy.9.counts_ref, f32[8,128]{1,0:T(8,128)S(1)} %slice.4.prior_ref, bf16[1280,256]{1,0:T(8,128)(2,1)S(1)} %get-tuple-element.30.nodes_ref, f32[28,1024]{1,0:T(8,128)S(1)} %get-tuple-element.29.tail_ref, f32[28,2048]{1,0:T(8,128)S(1)} %copy-done, ...), custom_call_target="tpu_custom_call" | custom-call | flops 671088640 | bytes 2000000 | tf_op jit(solution)/shard_map/pallas_call | solution.py:479
  45.7 6.4 %collective-permute-done.6.recv_ref = f32[28,1024]{1,0:T(8,128)S(1)} collective-permute-done((f32[28,1024]{1,0:T(8,128)S(1)}, f32[28,1024]{1,0:T(8,128)S(1)}, u32[]{:S(2)}, u32[]{:S(2)}) %collective-permute-start.6) | collective-permute-done | bytes 114720 | tf_op jit(solution)/shard_map/ppermute | solution.py:556
  52.1 0.8 %shard_map.73 = f32[28,3072]{1,0:T(8,128)} custom-call(f32[8,128]{1,0:T(8,128)S(1)} %slice.4.prior_ref, f32[28,1024]{1,0:T(8,128)S(1)} %collective-permute-done.6.recv_ref, f32[28,3072]{1,0:T(8,128)} %shard_map.72.partial_hbm), custom_call_target="tpu_custom_call", output_to_operand_aliasing={{}: (2, {})} | custom-call | bytes 2000000 | tf_op jit(solution)/shard_map/pallas_call | solution.py:479
  (1 shorter events, 0.0 us)
Async XLA Ops:
  5.2 8.8 %collective-permute-start = (f32[40,128]{1,0:T(8,128)S(1)}, f32[40,128]{1,0:T(8,128)S(1)}, u32[]{:S(2)}, u32[]{:S(2)}) collective-permute-start(f32[40,128]{1,0:T(8,128)S(1)} %get-tuple-element.17), channel_id=1, source_target_pairs={{0,1},{1,2},{2,3},{3,4},{4,5},{5,6},{6,7},{7,8},{8,9},{9,10},{10,1... | collective-permute-start | bytes 61448 | tf_op jit(solution)/shard_map/ppermute | solution.py:496
  9.3 4.8 %collective-permute-start.1 = (f32[40,128]{1,0:T(8,128)S(1)}, f32[40,128]{1,0:T(8,128)S(1)}, u32[]{:S(2)}, u32[]{:S(2)}) collective-permute-start(f32[40,128]{1,0:T(8,128)S(1)} %get-tuple-element.20), channel_id=1, source_target_pairs={{1,0},{2,1},{3,2},{4,3},{5,4},{6,5},{7,6},{8,7},{9,8},{10,9},{11,1... | collective-permute-start | bytes 61448 | tf_op jit(solution)/shard_map/ppermute | solution.py:495
  10.6 28.4 %copy-start.3 = (s32[3,2048]{1,0:T(4,128)S(1)}, s32[3,2048]{1,0:T(4,128)}, u32[]{:S(2)}) copy-start(s32[3,2048]{1,0:T(4,128)} %base_ref.1) | copy-start | bytes 73732
  14.1 24.9 %copy-start = (f32[28,2048]{1,0:T(8,128)S(1)}, f32[28,2048]{1,0:T(8,128)}, u32[]{:S(2)}) copy-start(f32[28,2048]{1,0:T(8,128)} %part_ref.1) | copy-start | bytes 688132
  14.8 24.2 %copy-start.1 = (f32[3,8,2048]{2,1,0:T(8,128)S(1)}, f32[3,8,2048]{2,1,0:T(8,128)}, u32[]{:S(2)}) copy-start(f32[3,8,2048]{2,1,0:T(8,128)} %g_ref.1) | copy-start | bytes 589828
  14.8 10.9 %collective-permute-start.2 = (f32[80,128]{1,0:T(8,128)S(1)}, f32[80,128]{1,0:T(8,128)S(1)}, u32[]{:S(2)}, u32[]{:S(2)}) collective-permute-start(f32[80,128]{1,0:T(8,128)S(1)} %get-tuple-element.23), channel_id=1, source_target_pairs={{16,0},{32,16},{48,32},{17,1},{33,17},{49,33},{18,2},{34,18},{50,3... | collective-permute-start | bytes 122888 | tf_op jit(solution)/shard_map/ppermute | solution.py:495
  16.2 10.6 %collective-permute-start.3 = (f32[80,128]{1,0:T(8,128)S(1)}, f32[80,128]{1,0:T(8,128)S(1)}, u32[]{:S(2)}, u32[]{:S(2)}) collective-permute-start(f32[80,128]{1,0:T(8,128)S(1)} %get-tuple-element.24), channel_id=1, source_target_pairs={{0,16},{16,32},{32,48},{1,17},{17,33},{33,49},{2,18},{18,34},{34,5... | collective-permute-start | bytes 122888 | tf_op jit(solution)/shard_map/ppermute | solution.py:496
  26.8 12.2 %copy-start.2 = (f32[8,2048]{1,0:T(8,128)S(1)}, f32[8,2048]{1,0:T(8,128)}, u32[]{:S(2)}) copy-start(f32[8,2048]{1,0:T(8,128)} %w_ref.1) | copy-start | bytes 196612
  26.9 10.4 %collective-permute-start.4 = (f32[192,128]{1,0:T(8,128)S(1)}, f32[192,128]{1,0:T(8,128)S(1)}, u32[]{:S(2)}, u32[]{:S(2)}) collective-permute-start(f32[192,128]{1,0:T(8,128)S(1)} %get-tuple-element.27), channel_id=1, source_target_pairs={{64,0},{128,64},{192,128},{256,192},{320,256},{384,320},{448,384},... | collective-permute-start | bytes 294920 | tf_op jit(solution)/shard_map/ppermute | solution.py:495
  35.4 3.5 %collective-permute-start.5 = (f32[192,128]{1,0:T(8,128)S(1)}, f32[192,128]{1,0:T(8,128)S(1)}, u32[]{:S(2)}, u32[]{:S(2)}) collective-permute-start(f32[192,128]{1,0:T(8,128)S(1)} %get-tuple-element.28), channel_id=1, source_target_pairs={{0,64},{64,128},{128,192},{192,256},{256,320},{320,384},{384,448},... | collective-permute-start | bytes 294920 | tf_op jit(solution)/shard_map/ppermute | solution.py:496
  41.6 10.5 %collective-permute-start.6 = (f32[28,1024]{1,0:T(8,128)S(1)}, f32[28,1024]{1,0:T(8,128)S(1)}, u32[]{:S(2)}, u32[]{:S(2)}) collective-permute-start(f32[28,1024]{1,0:T(8,128)S(1)} %get-tuple-element.29.tail_ref), channel_id=1, source_target_pairs={{0,1},{1,2},{2,3},{3,4},{4,5},{5,6},{6,7},{7,8},{8,9},{9,10},{10,1... | collective-permute-start | bytes 344072 | tf_op jit(solution)/shard_map/ppermute | solution.py:556

commit v4 on v3

--- a/solution.py
+++ b/solution.py
@@ -41,6 +41,8 @@
 PACK = SX // 3
 ZROWS = 40
 CHUNK = 256
+SENT = tuple(range(14)) + tuple(range(23, FIELDS))
+AXES = ("gx", "gy", "gz")
 F32 = jnp.float32
 BF16 = jnp.bfloat16
 SCATTER_KIB = 56000
@@ -80,8 +82,8 @@
     g_hbm,
     deep_ref,
     vel_ref,
-    low_ref,
-    high_ref,
+    odd_ref,
+    even_ref,
     part_ref,
     base_ref,
     w_ref,
@@ -175,14 +177,19 @@
         inside = (place >= 8 * j + LAYERS) & (place < 8 * j + LAYERS + 2)
         low_msg = jnp.where(inside, shift_lanes(vel, 8 * j + LAYERS - OFF), low_msg)
         high_msg = jnp.where(inside, shift_lanes(vel, 8 * j + LAYERS - OFF - CZ), high_msg)
-    low_ref[...] = low_msg
-    high_ref[...] = jnp.where(lane >= 3 * SZ, counts_ref[0].astype(F32), high_msg)
-
-
-def join_z_kernel(place_ref, deep_ref, vel_ref, before_ref, after_ref, deep_out, vel_out, low_ref, high_ref):
+    high_msg = jnp.where(lane >= 3 * SZ, counts_ref[0].astype(F32), high_msg)
+    is_even = lax.rem(lax.axis_index(AXES[2]), 2) == 0
+    odd_ref[...] = jnp.where(is_even, low_msg, high_msg)
+    even_ref[...] = jnp.where(is_even, high_msg, low_msg)
+
+
+def join_z_kernel(pairs, deep_ref, vel_ref, odd_ref, even_ref, deep_out, vel_out, prior_ref, *messages):
     place = channel_lane(lane_index(GROUP))
-    before = jnp.where(place_ref[2] > 0, before_ref[...], 0.0)
-    after = after_ref[...]
+    is_even = lax.rem(lax.axis_index(AXES[2]), 2) == 0
+    before = jnp.where(is_even, odd_ref[...], even_ref[...])
+    after = jnp.where(is_even, even_ref[...], odd_ref[...])
+    prior_ref[...] = before[0:8]
+    before = jnp.where(lax.axis_index(AXES[2]) > 0, before, 0.0)
     deep_low, deep_high = place < LAYERS, (place >= SZ - LAYERS) & (place < SZ)
     vel_low = (place >= OFF) & (place < OFF + 2)
     vel_high = (place >= OFF + CZ) & (place < OFF + CZ + 2)
@@ -200,16 +207,28 @@
         )
         deep_out[rows, :] = deep_ref[rows, :] + deep
         vel_out[rows, :] = vel_ref[rows, :] + vel
-    for x in range(EX):
-        row = EY * x
-        low_ref[LAYERS * x : LAYERS * (x + 1), :] = deep_out[row : row + LAYERS, :]
-        high_ref[LAYERS * x : LAYERS * (x + 1), :] = deep_out[row + EY - LAYERS : row + EY, :]
-        at = LAYERS * EX + 2 * x
-        low_ref[at : at + 2, :] = vel_out[row : row + 2, :]
-        high_ref[at : at + 2, :] = vel_out[row + EY - 2 : row + EY, :]
-
-
-def join_y_kernel(deep_ref, vel_ref, after_ref, before_ref, deep_out, vel_out, low_ref, high_ref):
+    for i in range(pairs):
+        is_lower = lax.axis_index(AXES[1]) == i
+        for x in range(EX):
+            row = EY * x
+            messages[i][LAYERS * x : LAYERS * (x + 1), :] = jnp.where(
+                is_lower, deep_out[row + EY - LAYERS : row + EY, :], deep_out[row : row + LAYERS, :]
+            )
+            at = LAYERS * EX + 2 * x
+            messages[i][at : at + 2, :] = jnp.where(
+                is_lower, vel_out[row + EY - 2 : row + EY, :], vel_out[row : row + 2, :]
+            )
+
+
+def join_y_kernel(pairs, deep_ref, vel_ref, *refs):
+    received, (deep_out, vel_out, low_ref, high_ref, before_ref, after_ref) = refs[:pairs], refs[pairs:]
+    before = jnp.zeros_like(before_ref)
+    after = jnp.zeros_like(after_ref)
+    for i in range(pairs):
+        before = jnp.where(lax.axis_index(AXES[1]) == i + 1, received[i][...], before)
+        after = jnp.where(lax.axis_index(AXES[1]) == i, received[i][...], after)
+    before_ref[...] = before
+    after_ref[...] = after
     deep_out[...] = jnp.zeros_like(deep_out)
     vel_out[...] = jnp.zeros_like(vel_out)
     for x in range(EX):
@@ -230,7 +249,43 @@
         high_ref[at : at + EY, :] = vel_out[EX - 2 + x, OFF : OFF + EY, :]
 
 
-def gather_update(index, nodes_ref, part_ref, base_ref, w_ref, g_ref, out_ref, out_index):
+def determinant(m):
+    return (
+        m[0][0] * (m[1][1] * m[2][2] - m[1][2] * m[2][1])
+        - m[0][1] * (m[1][0] * m[2][2] - m[1][2] * m[2][0])
+        + m[0][2] * (m[1][0] * m[2][1] - m[1][1] * m[2][0])
+    )
+
+
+def left_product(m, i, j):
+    return m[i][0] * m[j][0] + m[i][1] * m[j][1] + m[i][2] * m[j][2]
+
+
+def stress_rows(mapped, damaged):
+    degrade = (1.0 - damaged) ** 2
+    pressure = bulk_coef * (determinant(mapped) - 1.0)
+    rows = {}
+    for i in range(3):
+        for j in range(i, 3):
+            term = shear_mod * (left_product(mapped, i, j) - (1.0 if i == j else 0.0))
+            if i == j:
+                term = term + pressure
+            rows[14 + 3 * i + j] = rows[14 + 3 * j + i] = degrade * term
+    return rows
+
+
+def unpack(packed_ref, out_ref, left=None):
+    rows = {f: packed_ref[MOST * at : MOST * (at + 1), :] for at, f in enumerate(SENT)}
+    rows.update(stress_rows([[rows[5 + 3 * i + j] for j in range(3)] for i in range(3)], rows[23]))
+    for f in range(FIELDS):
+        value = rows[f]
+        if left is not None:
+            value = jnp.where(lax.broadcasted_iota(jnp.int32, (MOST, BIN), 0) < left, value, 0.0)
+        for t in range(MOST):
+            out_ref[f : f + 1, t * BIN : (t + 1) * BIN] = value[t : t + 1]
+
+
+def gather_update(index, nodes_ref, part_ref, base_ref, w_ref, g_ref, out_ref, out_index, packed):
     lanes = slice(index * CHUNK, (index + 1) * CHUNK)
     to = slice(out_index * CHUNK, (out_index + 1) * CHUNK)
     onehot = onehot_rows(base_ref, lanes)
@@ -281,40 +336,31 @@
         ]
         for i in range(3)
     ]
-    jacobian = (
-        mapped[0][0] * (mapped[1][1] * mapped[2][2] - mapped[1][2] * mapped[2][1])
-        - mapped[0][1] * (mapped[1][0] * mapped[2][2] - mapped[1][2] * mapped[2][0])
-        + mapped[0][2] * (mapped[1][0] * mapped[2][1] - mapped[1][1] * mapped[2][0])
-    )
-    left = {}
+    damaged = jnp.maximum(field(23), damage_node)
+    jacobian = determinant(mapped)
+    trace = left_product(mapped, 0, 0) + left_product(mapped, 1, 1) + left_product(mapped, 2, 2)
+    energy = 0.5 * shear_mod * (trace - 3.0) + 0.5 * bulk_coef * (jacobian - 1.0) ** 2
+    rows = {f: field(f) for f in range(2)}
     for i in range(3):
-        for j in range(i, 3):
-            left[i, j] = left[j, i] = (
-                mapped[i][0] * mapped[j][0] + mapped[i][1] * mapped[j][1] + mapped[i][2] * mapped[j][2]
-            )
-    damaged = jnp.maximum(field(23), damage_node)
-    degrade = (1.0 - damaged) ** 2
-    pressure = bulk_coef * (jacobian - 1.0)
-    energy = (
-        0.5 * shear_mod * (left[0, 0] + left[1, 1] + left[2, 2] - 3.0) + 0.5 * bulk_coef * (jacobian - 1.0) ** 2
-    )
-    out_ref[0:2, to] = part_ref[0:2, lanes]
-    for i in range(3):
-        out_ref[2 + i : 3 + i, to] = moved[i]
-        out_ref[25 + i : 26 + i, to] = field(25 + i) + time_step * moved[i]
+        rows[2 + i] = moved[i]
+        rows[25 + i] = field(25 + i) + time_step * moved[i]
         for j in range(3):
-            out_ref[5 + 3 * i + j : 6 + 3 * i + j, to] = mapped[i][j]
-            term = shear_mod * (left[i, j] - (1.0 if i == j else 0.0))
-            if i == j:
-                term = term + pressure
-            out_ref[14 + 3 * i + j : 15 + 3 * i + j, to] = degrade * term
-    out_ref[23:24, to] = damaged
-    out_ref[24:25, to] = jnp.maximum(field(24), energy)
+            rows[5 + 3 * i + j] = mapped[i][j]
+    rows[23] = damaged
+    rows[24] = jnp.maximum(field(24), energy)
+    if packed:
+        for at, f in enumerate(SENT):
+            for t in range(CHUNK // BIN):
+                row = MOST * (MOST * (at // MOST) + out_index * (CHUNK // BIN) + t) + at % MOST
+                out_ref[row : row + 1, :] = rows[f][:, t * BIN : (t + 1) * BIN]
+    else:
+        rows.update(stress_rows(mapped, damaged))
+        for f in range(FIELDS):
+            out_ref[f : f + 1, to] = rows[f]
 
 
 def relax_kernel(
     axis_sizes,
-    place_ref,
     deep_ref,
     vel_ref,
     after_ref,
@@ -336,6 +382,7 @@
     fv_ref,
     fd_ref,
     damage_ref,
+    rows_ref,
     sem,
 ):
     count_x, count_y, count_z = axis_sizes
@@ -349,9 +396,9 @@
             at = SY * (xd - SX + LAYERS)
             sums_ref[xd, 0:SY, :] += after_ref[at : at + SY, :]
     lane = lane_index(PITCH)
-    pos_x = place_ref[0] * CX - WIDE + three(lane, SZ, 0, PACK, 2 * PACK)
-    pos_y = place_ref[1] * CY - WIDE + lax.broadcasted_iota(jnp.int32, (PITCH, 128), 0)
-    pos_z = place_ref[2] * CZ - WIDE + lane - three(lane, SZ, 0, SZ, 2 * SZ)
+    pos_x = lax.axis_index(AXES[0]) * CX - WIDE + three(lane, SZ, 0, PACK, 2 * PACK)
+    pos_y = lax.axis_index(AXES[1]) * CY - WIDE + lax.broadcasted_iota(jnp.int32, (PITCH, 128), 0)
+    pos_z = lax.axis_index(AXES[2]) * CZ - WIDE + lane - three(lane, SZ, 0, SZ, 2 * SZ)
     inside_yz = (
         (lane < 3 * SZ) & (pos_y >= 0) & (pos_y < count_y * CY) & (pos_z >= 0) & (pos_z < count_z * CZ)
     )
@@ -414,7 +461,10 @@
         nodes_ref[start : start + 4 * ZROWS, :] = high
         nodes_ref[start + 4 * ZROWS : start + 8 * ZROWS, :] = low
     for index in range(TAIL // CHUNK):
-        gather_update((COUNT - TAIL) // CHUNK + index, nodes_ref, part_ref, base_ref, w_ref, g_ref, tail_ref, index)
+        gather_update((COUNT - TAIL) // CHUNK + index, nodes_ref, part_ref, base_ref, w_ref, g_ref, rows_ref, index, True)
+    for at in range(len(SENT)):
+        first = MOST * MOST * (at // MOST) + at % MOST
+        tail_ref[MOST * at : MOST * (at + 1), :] = rows_ref[pl.ds(first, MOST, stride=MOST), :]
     move.wait()
 
 
@@ -430,14 +480,12 @@
         blanks.append((i < MOST - prior, pltpu.make_async_copy(zero_ref, out_hbm.at[:, to], sems.at[2 + i])))
     for wanted, move in blanks:
         pl.when(wanted)(move.start)
-    for i in range(MOST):
-        bins = slice(i * BIN, (i + 1) * BIN)
-        left_ref[:, bins] = jnp.where(i < left, tail_ref[:, bins], 0.0)
+    unpack(tail_ref, left_ref, left)
     to = pl.ds(pl.multiple_of((prior + NBIN - MOST) * BIN, BIN), TAIL)
     own = pltpu.make_async_copy(left_ref, out_hbm.at[:, to], sems.at[0])
     own.start()
     for index in range((COUNT - TAIL) // CHUNK):
-        gather_update(index, nodes_ref, part_ref, base_ref, w_ref, g_ref, head_ref, index)
+        gather_update(index, nodes_ref, part_ref, base_ref, w_ref, g_ref, head_ref, index, False)
     to = pl.ds(pl.multiple_of(prior * BIN, BIN), COUNT - TAIL)
     stay = pltpu.make_async_copy(head_ref, out_hbm.at[:, to], sems.at[1])
     stay.start()
@@ -447,8 +495,9 @@
     stay.wait()
 
 
-def arrive_kernel(prior_ref, recv_ref, partial_hbm, out_hbm, sems):
+def arrive_kernel(prior_ref, packed_ref, partial_hbm, out_hbm, recv_ref, sems):
     prior = prior_ref[0, 3 * SZ].astype(jnp.int32)
+    unpack(packed_ref, recv_ref)
     moves = []
     for slot in range(MOST):
         source = pl.ds(pl.multiple_of(jnp.minimum(MOST - prior + slot, MOST - 1) * BIN, BIN), BIN)
@@ -488,21 +537,17 @@
     )(*args)
 
 
-def exchange(low, high, axis, ring=False):
-    count = lax.axis_size(axis)
-    up = [(i, (i + 1) % count) for i in range(count if ring else count - 1)]
-    down = [(i + 1, i) for i in range(count - 1)]
+def exchange(low, high, axis):
+    down = [(i + 1, i) for i in range(lax.axis_size(axis) - 1)]
     after = lax.ppermute(low, axis, down)
-    return lax.ppermute(high, axis, up), after
+    return lax.ppermute(high, axis, [(j, i) for i, j in down]), after
 
 
 def per_device(particles, stencil_base, weights, gradients, counts):
-    axes = ("gx", "gy", "gz")
-    place = jnp.stack([lax.axis_index(a) for a in axes]).astype(jnp.int32)
-    sizes = tuple(lax.axis_size(a) for a in axes)
+    sizes = tuple(lax.axis_size(a) for a in AXES)
     ring = [(i, (i + 1) % sizes[2]) for i in range(sizes[2])]
     inputs = (particles, stencil_base, weights, gradients)
-    deep, vel, low, high = call(
+    deep, vel, odd, even = call(
         scatter_kernel,
         (VMEM((GROWS, 128), F32), VMEM((GROWS, 128), F32), VMEM((GROUP, 128), F32), VMEM((GROUP, 128), F32)),
         [SMEM] + [HBM] * 4,
@@ -521,21 +566,27 @@
         ],
         limit=SCATTER_KIB,
     )
-    before_z, after_z = exchange(low, high, "gz", ring=True)
+    count_z = sizes[2]
+    odd_pairs = [(i, i + 1) for i in range(1, count_z - 1, 2)]
+    even_pairs = [(i, i + 1) for i in range(0, count_z, 2)]
+    from_odd = lax.ppermute(odd, "gz", odd_pairs + [(j, i) for i, j in odd_pairs] + [(count_z - 1, 0)])
+    from_even = lax.ppermute(even, "gz", even_pairs + [(j, i) for i, j in even_pairs])
     message = LAYERS * EX + 2 * EX
+    pairs = sizes[1] - 1
+    deep, vel, prior, *messages = call(
+        lambda *refs: join_z_kernel(pairs, *refs),
+        (shape(GROWS, 128), shape(GROWS, 128), shape(8, 128)) + (shape(message, 128),) * pairs,
+        [VMEM] * 4,
+        (deep, vel, from_odd, from_even),
+    )
+    received = [lax.ppermute(messages[i], "gy", [(i, i + 1), (i + 1, i)]) for i in range(pairs)]
+    wide_message = LAYERS * SY + 2 * EY
     deep, vel, low, high = call(
-        join_z_kernel,
-        (shape(GROWS, 128), shape(GROWS, 128), shape(message, 128), shape(message, 128)),
-        [SMEM] + [VMEM] * 4,
-        (place, deep, vel, before_z, after_z),
-    )
-    before, after = exchange(low, high, "gy")
-    message = LAYERS * SY + 2 * EY
-    deep, vel, low, high = call(
-        join_y_kernel,
-        (shape(EX, PITCH, 128), shape(EX, PITCH, 128), shape(message, 128), shape(message, 128)),
-        [VMEM] * 4,
-        (deep, vel, after, before),
+        lambda *refs: join_y_kernel(pairs, *refs),
+        (shape(EX, PITCH, 128), shape(EX, PITCH, 128), shape(wide_message, 128), shape(wide_message, 128)),
+        [VMEM] * (2 + pairs),
+        (deep, vel, *received),
+        scratch=[VMEM((message, 128), F32)] * 2,
     )
     before, after = exchange(low, high, "gx")
 
@@ -544,17 +595,16 @@
 
     damage, nodes, tail = call(
         relax,
-        (shape(CX, CY, CZ), shape(32 * ZROWS, 256, kind=BF16), shape(FIELDS, TAIL)),
-        [SMEM] + [VMEM] * 8,
-        (place, deep, vel, after, before) + inputs,
+        (shape(CX, CY, CZ), shape(32 * ZROWS, 256, kind=BF16), shape(len(SENT) * MOST, BIN)),
+        [VMEM] * 8,
+        (deep, vel, after, before) + inputs,
         out_spaces=[HBM, VMEM, VMEM],
         scratch=[VMEM((SX, PITCH, 128), F32)]
         + [VMEM((PACK, PITCH, 128), F32)] * 6
         + [VMEM((256, 128), F32)] * 2
-        + [VMEM((CX, CY, CZ), F32), pltpu.SemaphoreType.DMA],
+        + [VMEM((CX, CY, CZ), F32), VMEM((3 * MOST * MOST, BIN), F32), pltpu.SemaphoreType.DMA],
     )
     recv = lax.ppermute(tail, "gz", ring)
-    prior = before_z[0:8]
     own = call(
         head_kernel,
         shape(FIELDS, SLOTS),
@@ -575,7 +625,7 @@
         [VMEM, VMEM, HBM],
         (prior, recv, own),
         out_spaces=[HBM],
-        scratch=[pltpu.SemaphoreType.DMA((MOST,))],
+        scratch=[VMEM((FIELDS, TAIL), F32), pltpu.SemaphoreType.DMA((MOST,))],
         aliases={2: 0},
     )
     return (migrated, damage)

time: 53.2 us -> 51.7 us (0.972)
  the two profiles are of different devices: /device:TPU:1 before, /device:TPU:288 now
where the time goes in v4:
time: 51.7 us; the launch traced here: 51.3 us
  waiting for transfers between devices  21.7 us (42%)
  starting transfers between devices  19 us (37%)
  Pallas kernels  9.24 us (18%)
  between operations  1.42 us (3%)
    pallas_call x6, Pallas kernels, call(): pl.pallas_call(kernel, out_shape=out_shape, in_specs=[pl.BlockSpec(memory...  9.24 us
    ppermute x3, waiting for transfers between devices, per_device(): lax.ppermute(messages[i], 'gy', [(i, i + 1), (i + 1, i)])  8.08 us
    ppermute x1, waiting for transfers between devices, exchange(): return (lax.ppermute(high, axis, [(j, i) for i, j in down]), after)  6.05 us
    ppermute x3, starting transfers between devices, per_device(): lax.ppermute(messages[i], 'gy', [(i, i + 1), (i + 1, i)])  5.75 us
    ppermute x1, starting transfers between devices, per_device(): lax.ppermute(even, 'gz', even_pairs + [(j, i) for i, j in even_pairs])  5.68 us
    ppermute x1, waiting for transfers between devices, per_device(): recv = lax.ppermute(tail, 'gz', ring)  5.54 us
    ppermute x1, starting transfers between devices, exchange(): return (lax.ppermute(high, axis, [(j, i) for i, j in down]), after)  2.41 us
    ppermute x1, waiting for transfers between devices, per_device(): lax.ppermute(odd, 'gz', odd_pairs + [(j, i) for i, j in odd_pairs] + [(co...  2.01 us
  transfers between devices with their start and end apart: 8, of which 5 were waited for; matrix products, arithmetic and copies ran while one was open for 0% of the time, Pallas kernels for 4%

profile of v4, /device:TPU:288, one launch (start us, length us, event | category | flops | bytes accessed | tf_op | source)
XLA Modules:
  0.0 51.3 jit_solution(7402587318086425217)
XLA Ops:
  1.3 3.9 %shard_map.68 = (f32[200,128]{1,0:T(8,128)S(1)}, f32[200,128]{1,0:T(8,128)S(1)}, f32[40,128]{1,0:T(8,128)S(1)}, f32[40,128]{1,0:T(8,128)S(1)}) custom-call(s32[1]{0:T(128)S(6)} %copy.9.counts_ref, f32[28,2048]{1,0:T(8,128)} %part_ref.1, s32[3,2048]{1,0:T(4,128)} %base_ref.1, f32[8,2048]{1,0:T(8,128)} %w_ref.1, f32[3,8,2048]{2,1,0:T(8,128)} %g_ref.1), custom_call_target="tpu_custom_call" | custom-call | bytes 2000000 | tf_op jit(solution)/shard_map/pallas_call | solution.py:528
  5.2 1.3 %collective-permute-start = (f32[40,128]{1,0:T(8,128)S(1)}, f32[40,128]{1,0:T(8,128)S(1)}, u32[]{:S(2)}, u32[]{:S(2)}) collective-permute-start(f32[40,128]{1,0:T(8,128)S(1)} %get-tuple-element.21), channel_id=1, source_target_pairs={{1,2},{3,4},{5,6},{7,8},{9,10},{11,12},{13,14},{2,1},{4,3},{6,5},{... | collective-permute-start | bytes 61448 | tf_op jit(solution)/shard_map/ppermute | solution.py:572
  6.5 5.7 %collective-permute-start.1 = (f32[40,128]{1,0:T(8,128)S(1)}, f32[40,128]{1,0:T(8,128)S(1)}, u32[]{:S(2)}, u32[]{:S(2)}) collective-permute-start(f32[40,128]{1,0:T(8,128)S(1)} %get-tuple-element.22), channel_id=1, source_target_pairs={{0,1},{2,3},{4,5},{6,7},{8,9},{10,11},{12,13},{14,15},{1,0},{3,2},... | collective-permute-start | bytes 61448 | tf_op jit(solution)/shard_map/ppermute | solution.py:573
  12.2 2.0 %collective-permute-done.refs_2_ = f32[40,128]{1,0:T(8,128)S(1)} collective-permute-done((f32[40,128]{1,0:T(8,128)S(1)}, f32[40,128]{1,0:T(8,128)S(1)}, u32[]{:S(2)}, u32[]{:S(2)}) %collective-permute-start) | collective-permute-done | bytes 20512 | tf_op jit(solution)/shard_map/ppermute | solution.py:572
  14.2 0.0 collective-permute-done.1.refs_3_
  14.2 0.0 copy-start
  14.2 0.2 shard_map.69
  14.4 0.0 copy-start.1
  14.4 0.8 %collective-permute-start.2 = (f32[80,128]{1,0:T(8,128)S(1)}, f32[80,128]{1,0:T(8,128)S(1)}, u32[]{:S(2)}, u32[]{:S(2)}) collective-permute-start(f32[80,128]{1,0:T(8,128)S(1)} %get-tuple-element.26), channel_id=1, source_target_pairs={{0,16},{16,0},{1,17},{17,1},{2,18},{18,2},{3,19},{19,3},{4,20},{20... | collective-permute-start | bytes 122888 | tf_op jit(solution)/shard_map/ppermute | solution.py:582
  15.2 2.8 %collective-permute-start.3 = (f32[80,128]{1,0:T(8,128)S(1)}, f32[80,128]{1,0:T(8,128)S(1)}, u32[]{:S(2)}, u32[]{:S(2)}) collective-permute-start(f32[80,128]{1,0:T(8,128)S(1)} %get-tuple-element.27), channel_id=1, source_target_pairs={{16,32},{32,16},{17,33},{33,17},{18,34},{34,18},{19,35},{35,19},{2... | collective-permute-start | bytes 122888 | tf_op jit(solution)/shard_map/ppermute | solution.py:582
  18.1 2.1 %collective-permute-start.4 = (f32[80,128]{1,0:T(8,128)S(1)}, f32[80,128]{1,0:T(8,128)S(1)}, u32[]{:S(2)}, u32[]{:S(2)}) collective-permute-start(f32[80,128]{1,0:T(8,128)S(1)} %get-tuple-element.28), channel_id=1, source_target_pairs={{32,48},{48,32},{33,49},{49,33},{34,50},{50,34},{35,51},{51,35},{3... | collective-permute-start | bytes 122888 | tf_op jit(solution)/shard_map/ppermute | solution.py:582
  20.2 0.0 collective-permute-done.2.refs_2_
  20.2 4.9 %collective-permute-done.3.refs_3_ = f32[80,128]{1,0:T(8,128)S(1)} collective-permute-done((f32[80,128]{1,0:T(8,128)S(1)}, f32[80,128]{1,0:T(8,128)S(1)}, u32[]{:S(2)}, u32[]{:S(2)}) %collective-permute-start.3) | collective-permute-done | bytes 40992 | tf_op jit(solution)/shard_map/ppermute | solution.py:582
  25.1 3.2 %collective-permute-done.4.refs_4_ = f32[80,128]{1,0:T(8,128)S(1)} collective-permute-done((f32[80,128]{1,0:T(8,128)S(1)}, f32[80,128]{1,0:T(8,128)S(1)}, u32[]{:S(2)}, u32[]{:S(2)}) %collective-permute-start.4) | collective-permute-done | bytes 40992 | tf_op jit(solution)/shard_map/ppermute | solution.py:582
  28.3 0.0 copy-start.2
  28.3 0.0 copy-start.3
  28.3 0.1 shard_map.70
  28.4 1.9 %collective-permute-start.5 = (f32[192,128]{1,0:T(8,128)S(1)}, f32[192,128]{1,0:T(8,128)S(1)}, u32[]{:S(2)}, u32[]{:S(2)}) collective-permute-start(f32[192,128]{1,0:T(8,128)S(1)} %get-tuple-element.31), channel_id=1, source_target_pairs={{64,0},{128,64},{192,128},{256,192},{320,256},{384,320},{448,384},... | collective-permute-start | bytes 294920 | tf_op jit(solution)/shard_map/ppermute | solution.py:542
  30.3 2.4 %collective-permute-start.6 = (f32[192,128]{1,0:T(8,128)S(1)}, f32[192,128]{1,0:T(8,128)S(1)}, u32[]{:S(2)}, u32[]{:S(2)}) collective-permute-start(f32[192,128]{1,0:T(8,128)S(1)} %get-tuple-element.32), channel_id=1, source_target_pairs={{0,64},{64,128},{128,192},{192,256},{256,320},{320,384},{384,448},... | collective-permute-start | bytes 294920 | tf_op jit(solution)/shard_map/ppermute | solution.py:543
  32.7 0.0 collective-permute-done.5.refs_2_
  32.7 6.1 %collective-permute-done.6.refs_3_ = f32[192,128]{1,0:T(8,128)S(1)} collective-permute-done((f32[192,128]{1,0:T(8,128)S(1)}, f32[192,128]{1,0:T(8,128)S(1)}, u32[]{:S(2)}, u32[]{:S(2)}) %collective-permute-start.6) | collective-permute-done | bytes 98336 | tf_op jit(solution)/shard_map/ppermute | solution.py:543
  38.8 0.0 copy-done
  38.8 0.0 copy-done.1
  38.8 0.0 copy-done.2
  38.8 0.0 copy-done.3
  38.8 2.1 %shard_map.71 = (f32[8,16,32]{2,1,0:T(8,128)}, bf16[1280,256]{1,0:T(8,128)(2,1)S(1)}, f32[152,128]{1,0:T(8,128)S(1)}) custom-call(f32[10,32,128]{2,1,0:T(8,128)S(1)} %get-tuple-element.29.refs_0_, f32[10,32,128]{2,1,0:T(8,128)S(1)} %get-tuple-element.30.refs_1_, f32[192,128]{1,0:T(8,128)S(1)} %collective-permute-done.5.refs_2_, ...), custom_call_target="tpu_custom_call" | custom-call | bytes 2000000 | tf_op jit(solution)/shard_map/pallas_call | solution.py:528
  40.9 1.9 %collective-permute-start.7 = (f32[152,128]{1,0:T(8,128)S(1)}, f32[152,128]{1,0:T(8,128)S(1)}, u32[]{:S(2)}, u32[]{:S(2)}) collective-permute-start(f32[152,128]{1,0:T(8,128)S(1)} %get-tuple-element.33.tail_ref), channel_id=1, source_target_pairs={{0,1},{1,2},{2,3},{3,4},{4,5},{5,6},{6,7},{7,8},{8,9},{9,10},{10,1... | collective-permute-start | bytes 233480 | tf_op jit(solution)/shard_map/ppermute | solution.py:607
  42.8 2.1 %shard_map.72.partial_hbm = f32[28,3072]{1,0:T(8,128)} custom-call(s32[1]{0:T(128)S(6)} %copy.9.counts_ref, f32[8,128]{1,0:T(8,128)S(1)} %get-tuple-element.23.prior_ref, bf16[1280,256]{1,0:T(8,128)(2,1)S(1)} %get-tuple-element.34.nodes_ref, f32[152,128]{1,0:T(8,128)S(1)} %get-tuple-element.33.tail_ref, f32[28,2048]{1,0:T(8,128)S(1)} %copy-done, ...), custom_call_target="tpu_custom_call" | custom-call | flops 671088640 | bytes 2000000 | tf_op jit(solution)/shard_map/pallas_call | solution.py:528
  45.0 5.5 %collective-permute-done.7.packed_ref = f32[152,128]{1,0:T(8,128)S(1)} collective-permute-done((f32[152,128]{1,0:T(8,128)S(1)}, f32[152,128]{1,0:T(8,128)S(1)}, u32[]{:S(2)}, u32[]{:S(2)}) %collective-permute-start.7) | collective-permute-done | bytes 77856 | tf_op jit(solution)/shard_map/ppermute | solution.py:607
  50.5 0.8 %shard_map.73 = f32[28,3072]{1,0:T(8,128)} custom-call(f32[8,128]{1,0:T(8,128)S(1)} %get-tuple-element.23.prior_ref, f32[152,128]{1,0:T(8,128)S(1)} %collective-permute-done.7.packed_ref, f32[28,3072]{1,0:T(8,128)} %shard_map.72.partial_hbm), custom_call_target="tpu_custom_call", output_to_operand_aliasing={{}: (2, {})} | custom-call | bytes 2000000 | tf_op jit(solution)/shard_map/pallas_call | solution.py:528
Async XLA Ops:
  5.2 9.0 %collective-permute-start = (f32[40,128]{1,0:T(8,128)S(1)}, f32[40,128]{1,0:T(8,128)S(1)}, u32[]{:S(2)}, u32[]{:S(2)}) collective-permute-start(f32[40,128]{1,0:T(8,128)S(1)} %get-tuple-element.21), channel_id=1, source_target_pairs={{1,2},{3,4},{5,6},{7,8},{9,10},{11,12},{13,14},{2,1},{4,3},{6,5},{... | collective-permute-start | bytes 61448 | tf_op jit(solution)/shard_map/ppermute | solution.py:572
  6.5 7.7 %collective-permute-start.1 = (f32[40,128]{1,0:T(8,128)S(1)}, f32[40,128]{1,0:T(8,128)S(1)}, u32[]{:S(2)}, u32[]{:S(2)}) collective-permute-start(f32[40,128]{1,0:T(8,128)S(1)} %get-tuple-element.22), channel_id=1, source_target_pairs={{0,1},{2,3},{4,5},{6,7},{8,9},{10,11},{12,13},{14,15},{1,0},{3,2},... | collective-permute-start | bytes 61448 | tf_op jit(solution)/shard_map/ppermute | solution.py:573
  14.2 24.6 %copy-start = (f32[28,2048]{1,0:T(8,128)S(1)}, f32[28,2048]{1,0:T(8,128)}, u32[]{:S(2)}) copy-start(f32[28,2048]{1,0:T(8,128)} %part_ref.1) | copy-start | bytes 688132
  14.4 24.4 %copy-start.1 = (f32[3,8,2048]{2,1,0:T(8,128)S(1)}, f32[3,8,2048]{2,1,0:T(8,128)}, u32[]{:S(2)}) copy-start(f32[3,8,2048]{2,1,0:T(8,128)} %g_ref.1) | copy-start | bytes 589828
  14.4 5.8 %collective-permute-start.2 = (f32[80,128]{1,0:T(8,128)S(1)}, f32[80,128]{1,0:T(8,128)S(1)}, u32[]{:S(2)}, u32[]{:S(2)}) collective-permute-start(f32[80,128]{1,0:T(8,128)S(1)} %get-tuple-element.26), channel_id=1, source_target_pairs={{0,16},{16,0},{1,17},{17,1},{2,18},{18,2},{3,19},{19,3},{4,20},{20... | collective-permute-start | bytes 122888 | tf_op jit(solution)/shard_map/ppermute | solution.py:582
  15.2 9.8 %collective-permute-start.3 = (f32[80,128]{1,0:T(8,128)S(1)}, f32[80,128]{1,0:T(8,128)S(1)}, u32[]{:S(2)}, u32[]{:S(2)}) collective-permute-start(f32[80,128]{1,0:T(8,128)S(1)} %get-tuple-element.27), channel_id=1, source_target_pairs={{16,32},{32,16},{17,33},{33,17},{18,34},{34,18},{19,35},{35,19},{2... | collective-permute-start | bytes 122888 | tf_op jit(solution)/shard_map/ppermute | solution.py:582
  18.1 10.2 %collective-permute-start.4 = (f32[80,128]{1,0:T(8,128)S(1)}, f32[80,128]{1,0:T(8,128)S(1)}, u32[]{:S(2)}, u32[]{:S(2)}) collective-permute-start(f32[80,128]{1,0:T(8,128)S(1)} %get-tuple-element.28), channel_id=1, source_target_pairs={{32,48},{48,32},{33,49},{49,33},{34,50},{50,34},{35,51},{51,35},{3... | collective-permute-start | bytes 122888 | tf_op jit(solution)/shard_map/ppermute | solution.py:582
  28.3 10.5 %copy-start.2 = (f32[8,2048]{1,0:T(8,128)S(1)}, f32[8,2048]{1,0:T(8,128)}, u32[]{:S(2)}) copy-start(f32[8,2048]{1,0:T(8,128)} %w_ref.1) | copy-start | bytes 196612
  28.3 10.5 %copy-start.3 = (s32[3,2048]{1,0:T(4,128)S(1)}, s32[3,2048]{1,0:T(4,128)}, u32[]{:S(2)}) copy-start(s32[3,2048]{1,0:T(4,128)} %base_ref.1) | copy-start | bytes 73732
  28.4 4.3 %collective-permute-start.5 = (f32[192,128]{1,0:T(8,128)S(1)}, f32[192,128]{1,0:T(8,128)S(1)}, u32[]{:S(2)}, u32[]{:S(2)}) collective-permute-start(f32[192,128]{1,0:T(8,128)S(1)} %get-tuple-element.31), channel_id=1, source_target_pairs={{64,0},{128,64},{192,128},{256,192},{320,256},{384,320},{448,384},... | collective-permute-start | bytes 294920 | tf_op jit(solution)/shard_map/ppermute | solution.py:542
  30.3 8.5 %collective-permute-start.6 = (f32[192,128]{1,0:T(8,128)S(1)}, f32[192,128]{1,0:T(8,128)S(1)}, u32[]{:S(2)}, u32[]{:S(2)}) collective-permute-start(f32[192,128]{1,0:T(8,128)S(1)} %get-tuple-element.32), channel_id=1, source_target_pairs={{0,64},{64,128},{128,192},{192,256},{256,320},{320,384},{384,448},... | collective-permute-start | bytes 294920 | tf_op jit(solution)/shard_map/ppermute | solution.py:543
  40.9 9.6 %collective-permute-start.7 = (f32[152,128]{1,0:T(8,128)S(1)}, f32[152,128]{1,0:T(8,128)S(1)}, u32[]{:S(2)}, u32[]{:S(2)}) collective-permute-start(f32[152,128]{1,0:T(8,128)S(1)} %get-tuple-element.33.tail_ref), channel_id=1, source_target_pairs={{0,1},{1,2},{2,3},{3,4},{4,5},{5,6},{6,7},{7,8},{8,9},{9,10},{10,1... | collective-permute-start | bytes 233480 | tf_op jit(solution)/shard_map/ppermute | solution.py:607

commit v5 on v4

--- a/solution.py
+++ b/solution.py
@@ -41,6 +41,7 @@
 PACK = SX // 3
 ZROWS = 40
 CHUNK = 256
+FAR = 4
 SENT = tuple(range(14)) + tuple(range(23, FIELDS))
 AXES = ("gx", "gy", "gz")
 F32 = jnp.float32
@@ -359,7 +360,23 @@
             out_ref[f : f + 1, to] = rows[f]
 
 
-def relax_kernel(
+def relax_kernel(turn, axis_sizes, *refs):
+    tail_before = refs[10]
+    refs = refs if turn == 0 else refs[:8] + refs[11:]
+    is_far = lax.rem(lax.axis_index(AXES[2]), FAR) == 0
+
+    @pl.when(is_far if turn else jnp.logical_not(is_far))
+    def _():
+        relax_body(axis_sizes, *refs)
+
+    if turn:
+
+        @pl.when(jnp.logical_not(is_far))
+        def _():
+            refs[10][...] = tail_before[...]
+
+
+def relax_body(
     axis_sizes,
     deep_ref,
     vel_ref,
@@ -495,22 +512,22 @@
     stay.wait()
 
 
-def arrive_kernel(prior_ref, packed_ref, partial_hbm, out_hbm, recv_ref, sems):
-    prior = prior_ref[0, 3 * SZ].astype(jnp.int32)
-    unpack(packed_ref, recv_ref)
-    moves = []
-    for slot in range(MOST):
-        source = pl.ds(pl.multiple_of(jnp.minimum(MOST - prior + slot, MOST - 1) * BIN, BIN), BIN)
-        moves.append(
-            (
-                slot < prior,
-                pltpu.make_async_copy(recv_ref.at[:, source], out_hbm.at[:, slot * BIN : (slot + 1) * BIN], sems.at[slot]),
-            )
-        )
-    for wanted, move in moves:
-        pl.when(wanted)(move.start)
-    for wanted, move in moves:
-        pl.when(wanted)(move.wait)
+def arrive_kernel(turn, prior_ref, packed_ref, partial_hbm, out_hbm, recv_ref, sems):
+    is_far = lax.rem(lax.axis_index(AXES[2]), FAR) == 0
+
+    @pl.when(jnp.logical_not(is_far) if turn else is_far)
+    def _():
+        prior = prior_ref[0, 3 * SZ].astype(jnp.int32)
+        unpack(packed_ref, recv_ref)
+        moves = []
+        for slot in range(MOST):
+            source = pl.ds(pl.multiple_of(jnp.minimum(MOST - prior + slot, MOST - 1) * BIN, BIN), BIN)
+            target = out_hbm.at[:, slot * BIN : (slot + 1) * BIN]
+            moves.append((slot < prior, pltpu.make_async_copy(recv_ref.at[:, source], target, sems.at[slot])))
+        for wanted, move in moves:
+            pl.when(wanted)(move.start)
+        for wanted, move in moves:
+            pl.when(wanted)(move.wait)
 
 
 def shape(*dims, kind=F32):
@@ -545,7 +562,6 @@
 
 def per_device(particles, stencil_base, weights, gradients, counts):
     sizes = tuple(lax.axis_size(a) for a in AXES)
-    ring = [(i, (i + 1) % sizes[2]) for i in range(sizes[2])]
     inputs = (particles, stencil_base, weights, gradients)
     deep, vel, odd, even = call(
         scatter_kernel,
@@ -590,21 +606,27 @@
     )
     before, after = exchange(low, high, "gx")
 
-    def relax(*refs):
-        relax_kernel(sizes, *refs)
-
-    damage, nodes, tail = call(
-        relax,
-        (shape(CX, CY, CZ), shape(32 * ZROWS, 256, kind=BF16), shape(len(SENT) * MOST, BIN)),
-        [VMEM] * 8,
-        (deep, vel, after, before) + inputs,
-        out_spaces=[HBM, VMEM, VMEM],
-        scratch=[VMEM((SX, PITCH, 128), F32)]
-        + [VMEM((PACK, PITCH, 128), F32)] * 6
-        + [VMEM((256, 128), F32)] * 2
-        + [VMEM((CX, CY, CZ), F32), VMEM((3 * MOST * MOST, BIN), F32), pltpu.SemaphoreType.DMA],
-    )
-    recv = lax.ppermute(tail, "gz", ring)
+    ring = [(i, (i + 1) % count_z) for i in range(count_z)]
+    far = [edge for edge in ring if edge[1] % FAR == 0]
+    near = [edge for edge in ring if edge[1] % FAR != 0]
+    results = ()
+    for turn in range(2):
+        results = call(
+            lambda *refs, turn=turn: relax_kernel(turn, sizes, *refs),
+            (shape(CX, CY, CZ), VMEM((32 * ZROWS, 256), BF16), VMEM((len(SENT) * MOST, BIN), F32)),
+            [VMEM] * 8 + [HBM, VMEM, VMEM][: len(results)],
+            (deep, vel, after, before) + inputs + tuple(results),
+            out_spaces=[HBM, VMEM, VMEM],
+            scratch=[VMEM((SX, PITCH, 128), F32)]
+            + [VMEM((PACK, PITCH, 128), F32)] * 6
+            + [VMEM((256, 128), F32)] * 2
+            + [VMEM((CX, CY, CZ), F32), VMEM((3 * MOST * MOST, BIN), F32), pltpu.SemaphoreType.DMA],
+            aliases={8: 0, 9: 1} if turn else {},
+        )
+        if turn == 0:
+            recv_far = lax.ppermute(results[2], "gz", far)
+    damage, nodes, tail = results
+    recv_near = lax.ppermute(tail, "gz", near)
     own = call(
         head_kernel,
         shape(FIELDS, SLOTS),
@@ -619,15 +641,17 @@
         ],
         flops=2 * 1280 * 256 * 1024,
     )
-    migrated = call(
-        arrive_kernel,
-        shape(FIELDS, SLOTS),
-        [VMEM, VMEM, HBM],
-        (prior, recv, own),
-        out_spaces=[HBM],
-        scratch=[VMEM((FIELDS, TAIL), F32), pltpu.SemaphoreType.DMA((MOST,))],
-        aliases={2: 0},
-    )
+    migrated = own
+    for turn, recv in enumerate((recv_far, recv_near)):
+        migrated = call(
+            lambda *refs, turn=turn: arrive_kernel(turn, *refs),
+            shape(FIELDS, SLOTS),
+            [VMEM, VMEM, HBM],
+            (prior, recv, migrated),
+            out_spaces=[HBM],
+            scratch=[VMEM((FIELDS, TAIL), F32), pltpu.SemaphoreType.DMA((MOST,))],
+            aliases={2: 0},
+        )
     return (migrated, damage)
 
 

time: 51.7 us -> 49.8 us (0.963)
  the two profiles are of different devices: /device:TPU:288 before, /device:TPU:376 now
where the time goes in v5:
time: 49.8 us; the launch traced here: 49.5 us
  starting transfers between devices  20.8 us (42%)
  waiting for transfers between devices  17.8 us (36%)
  Pallas kernels  9.45 us (19%)
  between operations  1.45 us (3%)
    pallas_call x8, Pallas kernels, call(): pl.pallas_call(kernel, out_shape=out_shape, in_specs=[pl.BlockSpec(memory...  9.45 us
    ppermute x3, waiting for transfers between devices, per_device(): lax.ppermute(messages[i], 'gy', [(i, i + 1), (i + 1, i)])  7.87 us
    ppermute x3, starting transfers between devices, per_device(): lax.ppermute(messages[i], 'gy', [(i, i + 1), (i + 1, i)])  7.32 us
    ppermute x1, waiting for transfers between devices, exchange(): return (lax.ppermute(high, axis, [(j, i) for i, j in down]), after)  3.51 us
    ppermute x1, starting transfers between devices, per_device(): lax.ppermute(odd, 'gz', odd_pairs + [(j, i) for i, j in odd_pairs] + [(co...  3.05 us
    ppermute x1, starting transfers between devices, per_device(): recv_far = lax.ppermute(results[2], 'gz', far)  2.81 us
    ppermute x1, waiting for transfers between devices, per_device(): lax.ppermute(odd, 'gz', odd_pairs + [(j, i) for i, j in odd_pairs] + [(co...  2.76 us
    ppermute x1, waiting for transfers between devices, per_device(): recv_near = lax.ppermute(tail, 'gz', near)  2.71 us
  transfers between devices with their start and end apart: 9, of which 6 were waited for; matrix products, arithmetic and copies ran while one was open for 0% of the time, Pallas kernels for 5%

profile of v5, /device:TPU:376, one launch (start us, length us, event | category | flops | bytes accessed | tf_op | source)
XLA Modules:
  0.0 49.5 jit_solution(6510089375809053236)
XLA Ops:
  1.3 3.9 %shard_map.68 = (f32[200,128]{1,0:T(8,128)S(1)}, f32[200,128]{1,0:T(8,128)S(1)}, f32[40,128]{1,0:T(8,128)S(1)}, f32[40,128]{1,0:T(8,128)S(1)}) custom-call(s32[1]{0:T(128)S(6)} %copy.15.counts_ref, f32[28,2048]{1,0:T(8,128)} %part_ref.1, s32[3,2048]{1,0:T(4,128)} %base_ref.1, f32[8,2048]{1,0:T(8,128)} %w_ref.1, f32[3,8,2048]{2,1,0:T(8,128)} %g_ref.1), custom_call_target="tpu_custom_call" | custom-call | bytes 2000000 | tf_op jit(solution)/shard_map/pallas_call | solution.py:545
  5.2 3.1 %collective-permute-start = (f32[40,128]{1,0:T(8,128)S(1)}, f32[40,128]{1,0:T(8,128)S(1)}, u32[]{:S(2)}, u32[]{:S(2)}) collective-permute-start(f32[40,128]{1,0:T(8,128)S(1)} %get-tuple-element.24), channel_id=1, source_target_pairs={{1,2},{3,4},{5,6},{7,8},{9,10},{11,12},{13,14},{2,1},{4,3},{6,5},{... | collective-permute-start | bytes 61448 | tf_op jit(solution)/shard_map/ppermute | solution.py:588
  8.3 2.0 %collective-permute-start.1 = (f32[40,128]{1,0:T(8,128)S(1)}, f32[40,128]{1,0:T(8,128)S(1)}, u32[]{:S(2)}, u32[]{:S(2)}) collective-permute-start(f32[40,128]{1,0:T(8,128)S(1)} %get-tuple-element.25), channel_id=1, source_target_pairs={{0,1},{2,3},{4,5},{6,7},{8,9},{10,11},{12,13},{14,15},{1,0},{3,2},... | collective-permute-start | bytes 61448 | tf_op jit(solution)/shard_map/ppermute | solution.py:589
  10.2 2.8 %collective-permute-done.refs_2_ = f32[40,128]{1,0:T(8,128)S(1)} collective-permute-done((f32[40,128]{1,0:T(8,128)S(1)}, f32[40,128]{1,0:T(8,128)S(1)}, u32[]{:S(2)}, u32[]{:S(2)}) %collective-permute-start) | collective-permute-done | bytes 20512 | tf_op jit(solution)/shard_map/ppermute | solution.py:588
  13.0 1.0 %collective-permute-done.1.refs_3_ = f32[40,128]{1,0:T(8,128)S(1)} collective-permute-done((f32[40,128]{1,0:T(8,128)S(1)}, f32[40,128]{1,0:T(8,128)S(1)}, u32[]{:S(2)}, u32[]{:S(2)}) %collective-permute-start.1) | collective-permute-done | bytes 20512 | tf_op jit(solution)/shard_map/ppermute | solution.py:589
  14.0 0.0 copy-start
  14.0 0.2 shard_map.69
  14.2 0.0 copy-start.1
  14.2 0.8 %collective-permute-start.2 = (f32[80,128]{1,0:T(8,128)S(1)}, f32[80,128]{1,0:T(8,128)S(1)}, u32[]{:S(2)}, u32[]{:S(2)}) collective-permute-start(f32[80,128]{1,0:T(8,128)S(1)} %get-tuple-element.29), channel_id=1, source_target_pairs={{0,16},{16,0},{1,17},{17,1},{2,18},{18,2},{3,19},{19,3},{4,20},{20... | collective-permute-start | bytes 122888 | tf_op jit(solution)/shard_map/ppermute | solution.py:598
  15.0 4.6 %collective-permute-start.3 = (f32[80,128]{1,0:T(8,128)S(1)}, f32[80,128]{1,0:T(8,128)S(1)}, u32[]{:S(2)}, u32[]{:S(2)}) collective-permute-start(f32[80,128]{1,0:T(8,128)S(1)} %get-tuple-element.30), channel_id=1, source_target_pairs={{16,32},{32,16},{17,33},{33,17},{18,34},{34,18},{19,35},{35,19},{2... | collective-permute-start | bytes 122888 | tf_op jit(solution)/shard_map/ppermute | solution.py:598
  19.6 1.9 %collective-permute-start.4 = (f32[80,128]{1,0:T(8,128)S(1)}, f32[80,128]{1,0:T(8,128)S(1)}, u32[]{:S(2)}, u32[]{:S(2)}) collective-permute-start(f32[80,128]{1,0:T(8,128)S(1)} %get-tuple-element.31), channel_id=1, source_target_pairs={{32,48},{48,32},{33,49},{49,33},{34,50},{50,34},{35,51},{51,35},{3... | collective-permute-start | bytes 122888 | tf_op jit(solution)/shard_map/ppermute | solution.py:598
  21.5 0.0 collective-permute-done.2.refs_2_
  21.5 3.2 %collective-permute-done.3.refs_3_ = f32[80,128]{1,0:T(8,128)S(1)} collective-permute-done((f32[80,128]{1,0:T(8,128)S(1)}, f32[80,128]{1,0:T(8,128)S(1)}, u32[]{:S(2)}, u32[]{:S(2)}) %collective-permute-start.3) | collective-permute-done | bytes 40992 | tf_op jit(solution)/shard_map/ppermute | solution.py:598
  24.8 4.6 %collective-permute-done.4.refs_4_ = f32[80,128]{1,0:T(8,128)S(1)} collective-permute-done((f32[80,128]{1,0:T(8,128)S(1)}, f32[80,128]{1,0:T(8,128)S(1)}, u32[]{:S(2)}, u32[]{:S(2)}) %collective-permute-start.4) | collective-permute-done | bytes 40992 | tf_op jit(solution)/shard_map/ppermute | solution.py:598
  29.4 0.0 copy-start.2
  29.4 0.1 shard_map.70
  29.5 1.9 %collective-permute-start.5 = (f32[192,128]{1,0:T(8,128)S(1)}, f32[192,128]{1,0:T(8,128)S(1)}, u32[]{:S(2)}, u32[]{:S(2)}) collective-permute-start(f32[192,128]{1,0:T(8,128)S(1)} %get-tuple-element.34), channel_id=1, source_target_pairs={{64,0},{128,64},{192,128},{256,192},{320,256},{384,320},{448,384},... | collective-permute-start | bytes 294920 | tf_op jit(solution)/shard_map/ppermute | solution.py:559
  31.4 2.4 %collective-permute-start.6 = (f32[192,128]{1,0:T(8,128)S(1)}, f32[192,128]{1,0:T(8,128)S(1)}, u32[]{:S(2)}, u32[]{:S(2)}) collective-permute-start(f32[192,128]{1,0:T(8,128)S(1)} %get-tuple-element.35), channel_id=1, source_target_pairs={{0,64},{64,128},{128,192},{192,256},{256,320},{320,384},{384,448},... | collective-permute-start | bytes 294920 | tf_op jit(solution)/shard_map/ppermute | solution.py:560
  33.8 0.0 collective-permute-done.5.refs_2_
  33.8 3.5 %collective-permute-done.6.refs_3_ = f32[192,128]{1,0:T(8,128)S(1)} collective-permute-done((f32[192,128]{1,0:T(8,128)S(1)}, f32[192,128]{1,0:T(8,128)S(1)}, u32[]{:S(2)}, u32[]{:S(2)}) %collective-permute-start.6) | collective-permute-done | bytes 98336 | tf_op jit(solution)/shard_map/ppermute | solution.py:560
  37.4 0.0 copy-done
  37.4 0.0 copy-done.1
  37.4 0.0 copy-done.2
  37.4 0.0 copy-done.3
  37.4 2.1 %shard_map.71 = (f32[8,16,32]{2,1,0:T(8,128)}, bf16[1280,256]{1,0:T(8,128)(2,1)S(1)}, f32[152,128]{1,0:T(8,128)S(1)}) custom-call(f32[10,32,128]{2,1,0:T(8,128)S(1)} %get-tuple-element.32.refs_0_, f32[10,32,128]{2,1,0:T(8,128)S(1)} %get-tuple-element.33.refs_1_, f32[192,128]{1,0:T(8,128)S(1)} %collective-permute-done.5.refs_2_, ...), custom_call_target="tpu_custom_call" | custom-call | bytes 2000000 | tf_op jit(solution)/shard_map/pallas_call | solution.py:545
  39.5 2.8 %collective-permute-start.8 = (f32[152,128]{1,0:T(8,128)S(1)}, f32[152,128]{1,0:T(8,128)S(1)}, u32[]{:S(2)}, u32[]{:S(2)}) collective-permute-start(f32[152,128]{1,0:T(8,128)S(1)} %get-tuple-element.38.refs_10_), channel_id=1, source_target_pairs={{3,4},{7,8},{11,12},{15,0},{19,20},{23,24},{27,28},{31,16},{35,36}... | collective-permute-start | bytes 233480 | tf_op jit(solution)/shard_map/ppermute | solution.py:627
  42.4 1.3 %collective-permute-start.7 = (f32[152,128]{1,0:T(8,128)S(1)}, f32[152,128]{1,0:T(8,128)S(1)}, u32[]{:S(2)}, u32[]{:S(2)}) collective-permute-start(f32[152,128]{1,0:T(8,128)S(1)} %get-tuple-element.39.tail_ref), channel_id=1, source_target_pairs={{0,1},{1,2},{2,3},{4,5},{5,6},{6,7},{8,9},{9,10},{10,11},{12,13},{... | collective-permute-start | bytes 233480 | tf_op jit(solution)/shard_map/ppermute | solution.py:629
  43.7 2.2 %shard_map.73.refs_2_ = f32[28,3072]{1,0:T(8,128)} custom-call(s32[1]{0:T(128)S(6)} %copy.15.counts_ref, f32[8,128]{1,0:T(8,128)S(1)} %get-tuple-element.26.prior_ref.refs_0_, bf16[1280,256]{1,0:T(8,128)(2,1)S(1)} %get-tuple-element.40.nodes_ref, f32[152,128]{1,0:T(8,128)S(1)} %get-tuple-element.39.tail_ref, f32[28,2048]{1,0:T(8,128)S(1)} %copy-done, ...), custom_call_target="tpu_custom_call" | custom-call | flops 671088640 | bytes 2000000 | tf_op jit(solution)/shard_map/pallas_call | solution.py:545
  45.8 0.0 collective-permute-done.8.refs_1_
  45.8 0.1 shard_map.74.refs_2_
  45.9 2.7 %collective-permute-done.7.refs_1_ = f32[152,128]{1,0:T(8,128)S(1)} collective-permute-done((f32[152,128]{1,0:T(8,128)S(1)}, f32[152,128]{1,0:T(8,128)S(1)}, u32[]{:S(2)}, u32[]{:S(2)}) %collective-permute-start.7) | collective-permute-done | bytes 77856 | tf_op jit(solution)/shard_map/ppermute | solution.py:629
  48.6 0.8 %shard_map.75 = f32[28,3072]{1,0:T(8,128)} custom-call(f32[8,128]{1,0:T(8,128)S(1)} %get-tuple-element.26.prior_ref.refs_0_, f32[152,128]{1,0:T(8,128)S(1)} %collective-permute-done.7.refs_1_, f32[28,3072]{1,0:T(8,128)} %shard_map.74.refs_2_), custom_call_target="tpu_custom_call", output_to_operand_aliasing={{}: (2, {})} | custom-call | bytes 2000000 | tf_op jit(solution)/shard_map/pallas_call | solution.py:545
  (2 shorter events, 0.0 us)
Async XLA Ops:
  5.2 7.8 %collective-permute-start = (f32[40,128]{1,0:T(8,128)S(1)}, f32[40,128]{1,0:T(8,128)S(1)}, u32[]{:S(2)}, u32[]{:S(2)}) collective-permute-start(f32[40,128]{1,0:T(8,128)S(1)} %get-tuple-element.24), channel_id=1, source_target_pairs={{1,2},{3,4},{5,6},{7,8},{9,10},{11,12},{13,14},{2,1},{4,3},{6,5},{... | collective-permute-start | bytes 61448 | tf_op jit(solution)/shard_map/ppermute | solution.py:588
  8.3 5.7 %collective-permute-start.1 = (f32[40,128]{1,0:T(8,128)S(1)}, f32[40,128]{1,0:T(8,128)S(1)}, u32[]{:S(2)}, u32[]{:S(2)}) collective-permute-start(f32[40,128]{1,0:T(8,128)S(1)} %get-tuple-element.25), channel_id=1, source_target_pairs={{0,1},{2,3},{4,5},{6,7},{8,9},{10,11},{12,13},{14,15},{1,0},{3,2},... | collective-permute-start | bytes 61448 | tf_op jit(solution)/shard_map/ppermute | solution.py:589
  14.0 23.4 %copy-start = (f32[28,2048]{1,0:T(8,128)S(1)}, f32[28,2048]{1,0:T(8,128)}, u32[]{:S(2)}) copy-start(f32[28,2048]{1,0:T(8,128)} %part_ref.1) | copy-start | bytes 688132
  14.2 23.2 %copy-start.1 = (f32[3,8,2048]{2,1,0:T(8,128)S(1)}, f32[3,8,2048]{2,1,0:T(8,128)}, u32[]{:S(2)}) copy-start(f32[3,8,2048]{2,1,0:T(8,128)} %g_ref.1) | copy-start | bytes 589828
  14.2 7.3 %collective-permute-start.2 = (f32[80,128]{1,0:T(8,128)S(1)}, f32[80,128]{1,0:T(8,128)S(1)}, u32[]{:S(2)}, u32[]{:S(2)}) collective-permute-start(f32[80,128]{1,0:T(8,128)S(1)} %get-tuple-element.29), channel_id=1, source_target_pairs={{0,16},{16,0},{1,17},{17,1},{2,18},{18,2},{3,19},{19,3},{4,20},{20... | collective-permute-start | bytes 122888 | tf_op jit(solution)/shard_map/ppermute | solution.py:598
  15.0 9.8 %collective-permute-start.3 = (f32[80,128]{1,0:T(8,128)S(1)}, f32[80,128]{1,0:T(8,128)S(1)}, u32[]{:S(2)}, u32[]{:S(2)}) collective-permute-start(f32[80,128]{1,0:T(8,128)S(1)} %get-tuple-element.30), channel_id=1, source_target_pairs={{16,32},{32,16},{17,33},{33,17},{18,34},{34,18},{19,35},{35,19},{2... | collective-permute-start | bytes 122888 | tf_op jit(solution)/shard_map/ppermute | solution.py:598
  19.6 9.8 %collective-permute-start.4 = (f32[80,128]{1,0:T(8,128)S(1)}, f32[80,128]{1,0:T(8,128)S(1)}, u32[]{:S(2)}, u32[]{:S(2)}) collective-permute-start(f32[80,128]{1,0:T(8,128)S(1)} %get-tuple-element.31), channel_id=1, source_target_pairs={{32,48},{48,32},{33,49},{49,33},{34,50},{50,34},{35,51},{51,35},{3... | collective-permute-start | bytes 122888 | tf_op jit(solution)/shard_map/ppermute | solution.py:598
  29.4 8.0 %copy-start.2 = (f32[8,2048]{1,0:T(8,128)S(1)}, f32[8,2048]{1,0:T(8,128)}, u32[]{:S(2)}) copy-start(f32[8,2048]{1,0:T(8,128)} %w_ref.1) | copy-start | bytes 196612
  29.4 8.0 %copy-start.3 = (s32[3,2048]{1,0:T(4,128)S(1)}, s32[3,2048]{1,0:T(4,128)}, u32[]{:S(2)}) copy-start(s32[3,2048]{1,0:T(4,128)} %base_ref.1) | copy-start | bytes 73732
  29.5 4.3 %collective-permute-start.5 = (f32[192,128]{1,0:T(8,128)S(1)}, f32[192,128]{1,0:T(8,128)S(1)}, u32[]{:S(2)}, u32[]{:S(2)}) collective-permute-start(f32[192,128]{1,0:T(8,128)S(1)} %get-tuple-element.34), channel_id=1, source_target_pairs={{64,0},{128,64},{192,128},{256,192},{320,256},{384,320},{448,384},... | collective-permute-start | bytes 294920 | tf_op jit(solution)/shard_map/ppermute | solution.py:559
  31.4 5.9 %collective-permute-start.6 = (f32[192,128]{1,0:T(8,128)S(1)}, f32[192,128]{1,0:T(8,128)S(1)}, u32[]{:S(2)}, u32[]{:S(2)}) collective-permute-start(f32[192,128]{1,0:T(8,128)S(1)} %get-tuple-element.35), channel_id=1, source_target_pairs={{0,64},{64,128},{128,192},{192,256},{256,320},{320,384},{384,448},... | collective-permute-start | bytes 294920 | tf_op jit(solution)/shard_map/ppermute | solution.py:560
  39.5 6.3 %collective-permute-start.8 = (f32[152,128]{1,0:T(8,128)S(1)}, f32[152,128]{1,0:T(8,128)S(1)}, u32[]{:S(2)}, u32[]{:S(2)}) collective-permute-start(f32[152,128]{1,0:T(8,128)S(1)} %get-tuple-element.38.refs_10_), channel_id=1, source_target_pairs={{3,4},{7,8},{11,12},{15,0},{19,20},{23,24},{27,28},{31,16},{35,36}... | collective-permute-start | bytes 233480 | tf_op jit(solution)/shard_map/ppermute | solution.py:627
  42.4 6.3 %collective-permute-start.7 = (f32[152,128]{1,0:T(8,128)S(1)}, f32[152,128]{1,0:T(8,128)S(1)}, u32[]{:S(2)}, u32[]{:S(2)}) collective-permute-start(f32[152,128]{1,0:T(8,128)S(1)} %get-tuple-element.39.tail_ref), channel_id=1, source_target_pairs={{0,1},{1,2},{2,3},{4,5},{5,6},{6,7},{8,9},{9,10},{10,11},{12,13},{... | collective-permute-start | bytes 233480 | tf_op jit(solution)/shard_map/ppermute | solution.py:629

commit v6 on v5

--- a/solution.py
+++ b/solution.py
@@ -222,7 +222,7 @@
 
 
 def join_y_kernel(pairs, deep_ref, vel_ref, *refs):
-    received, (deep_out, vel_out, low_ref, high_ref, before_ref, after_ref) = refs[:pairs], refs[pairs:]
+    received, (deep_out, vel_out, odd_ref, even_ref, before_ref, after_ref) = refs[:pairs], refs[pairs:]
     before = jnp.zeros_like(before_ref)
     after = jnp.zeros_like(after_ref)
     for i in range(pairs):
@@ -241,13 +241,17 @@
         vel_out[x, OFF : OFF + EY, :] = vel_ref[row : row + EY, :]
         vel_out[x, OFF : OFF + 2, :] += before_ref[at : at + 2, :]
         vel_out[x, OFF + CY : OFF + CY + 2, :] += after_ref[at : at + 2, :]
+    is_even = lax.rem(lax.axis_index(AXES[0]), 2) == 0
+
+    def put(rows, low, high):
+        odd_ref[rows, :] = jnp.where(is_even, low, high)
+        even_ref[rows, :] = jnp.where(is_even, high, low)
+
     for x in range(LAYERS):
-        low_ref[SY * x : SY * (x + 1), :] = deep_out[x, 0:SY, :]
-        high_ref[SY * x : SY * (x + 1), :] = deep_out[EX - LAYERS + x, 0:SY, :]
+        put(slice(SY * x, SY * (x + 1)), deep_out[x, 0:SY, :], deep_out[EX - LAYERS + x, 0:SY, :])
     for x in range(2):
         at = SY * LAYERS + EY * x
-        low_ref[at : at + EY, :] = vel_out[x, OFF : OFF + EY, :]
-        high_ref[at : at + EY, :] = vel_out[EX - 2 + x, OFF : OFF + EY, :]
+        put(slice(at, at + EY), vel_out[x, OFF : OFF + EY, :], vel_out[EX - 2 + x, OFF : OFF + EY, :])
 
 
 def determinant(m):
@@ -380,8 +384,8 @@
     axis_sizes,
     deep_ref,
     vel_ref,
-    after_ref,
-    before_ref,
+    odd_ref,
+    even_ref,
     part_ref,
     base_ref,
     w_ref,
@@ -400,8 +404,13 @@
     fd_ref,
     damage_ref,
     rows_ref,
+    before_ref,
+    after_ref,
     sem,
 ):
+    is_even = lax.rem(lax.axis_index(AXES[0]), 2) == 0
+    before_ref[...] = jnp.where(is_even, odd_ref[...], even_ref[...])
+    after_ref[...] = jnp.where(is_even, even_ref[...], odd_ref[...])
     count_x, count_y, count_z = axis_sizes
     sums_ref[...] = jnp.zeros_like(sums_ref)
     for xd in range(SX):
@@ -554,10 +563,12 @@
     )(*args)
 
 
-def exchange(low, high, axis):
-    down = [(i + 1, i) for i in range(lax.axis_size(axis) - 1)]
-    after = lax.ppermute(low, axis, down)
-    return lax.ppermute(high, axis, [(j, i) for i, j in down]), after
+def swap_pairs(odd, even, axis, extra=()):
+    count = lax.axis_size(axis)
+    odd_pairs = [(i, i + 1) for i in range(1, count - 1, 2)]
+    even_pairs = [(i, i + 1) for i in range(0, count - 1, 2)]
+    from_odd = lax.ppermute(odd, axis, odd_pairs + [(j, i) for i, j in odd_pairs] + list(extra))
+    return from_odd, lax.ppermute(even, axis, even_pairs + [(j, i) for i, j in even_pairs])
 
 
 def per_device(particles, stencil_base, weights, gradients, counts):
@@ -583,10 +594,7 @@
         limit=SCATTER_KIB,
     )
     count_z = sizes[2]
-    odd_pairs = [(i, i + 1) for i in range(1, count_z - 1, 2)]
-    even_pairs = [(i, i + 1) for i in range(0, count_z, 2)]
-    from_odd = lax.ppermute(odd, "gz", odd_pairs + [(j, i) for i, j in odd_pairs] + [(count_z - 1, 0)])
-    from_even = lax.ppermute(even, "gz", even_pairs + [(j, i) for i, j in even_pairs])
+    from_odd, from_even = swap_pairs(odd, even, "gz", [(count_z - 1, 0)])
     message = LAYERS * EX + 2 * EX
     pairs = sizes[1] - 1
     deep, vel, prior, *messages = call(
@@ -597,14 +605,14 @@
     )
     received = [lax.ppermute(messages[i], "gy", [(i, i + 1), (i + 1, i)]) for i in range(pairs)]
     wide_message = LAYERS * SY + 2 * EY
-    deep, vel, low, high = call(
+    deep, vel, odd, even = call(
         lambda *refs: join_y_kernel(pairs, *refs),
         (shape(EX, PITCH, 128), shape(EX, PITCH, 128), shape(wide_message, 128), shape(wide_message, 128)),
         [VMEM] * (2 + pairs),
         (deep, vel, *received),
         scratch=[VMEM((message, 128), F32)] * 2,
     )
-    before, after = exchange(low, high, "gx")
+    from_odd, from_even = swap_pairs(odd, even, "gx")
 
     ring = [(i, (i + 1) % count_z) for i in range(count_z)]
     far = [edge for edge in ring if edge[1] % FAR == 0]
@@ -615,12 +623,14 @@
             lambda *refs, turn=turn: relax_kernel(turn, sizes, *refs),
             (shape(CX, CY, CZ), VMEM((32 * ZROWS, 256), BF16), VMEM((len(SENT) * MOST, BIN), F32)),
             [VMEM] * 8 + [HBM, VMEM, VMEM][: len(results)],
-            (deep, vel, after, before) + inputs + tuple(results),
+            (deep, vel, from_odd, from_even) + inputs + tuple(results),
             out_spaces=[HBM, VMEM, VMEM],
             scratch=[VMEM((SX, PITCH, 128), F32)]
             + [VMEM((PACK, PITCH, 128), F32)] * 6
             + [VMEM((256, 128), F32)] * 2
-            + [VMEM((CX, CY, CZ), F32), VMEM((3 * MOST * MOST, BIN), F32), pltpu.SemaphoreType.DMA],
+            + [VMEM((CX, CY, CZ), F32), VMEM((3 * MOST * MOST, BIN), F32)]
+            + [VMEM((wide_message, 128), F32)] * 2
+            + [pltpu.SemaphoreType.DMA],
             aliases={8: 0, 9: 1} if turn else {},
         )
         if turn == 0:

time: 49.8 us -> 47.9 us (0.962)
  the two profiles are of different devices: /device:TPU:376 before, /device:TPU:378 now
where the time goes in v6:
time: 47.9 us; the launch traced here: 47.6 us
  starting transfers between devices  20.2 us (42%)
  waiting for transfers between devices  16.4 us (34%)
  Pallas kernels  9.46 us (20%)
  between operations  1.45 us (3%)
    pallas_call x8, Pallas kernels, call(): pl.pallas_call(kernel, out_shape=out_shape, in_specs=[pl.BlockSpec(memory...  9.46 us
    ppermute x3, waiting for transfers between devices, per_device(): lax.ppermute(messages[i], 'gy', [(i, i + 1), (i + 1, i)])  7.87 us
    ppermute x3, starting transfers between devices, per_device(): lax.ppermute(messages[i], 'gy', [(i, i + 1), (i + 1, i)])  7.32 us
    ppermute x2, starting transfers between devices, swap_pairs(): lax.ppermute(odd, axis, odd_pairs + [(j, i) for i, j in odd_pairs] + list...  4.98 us
    ppermute x2, waiting for transfers between devices, swap_pairs(): lax.ppermute(odd, axis, odd_pairs + [(j, i) for i, j in odd_pairs] + list...  4.84 us
    ppermute x2, starting transfers between devices, swap_pairs(): lax.ppermute(even, axis, even_pairs + [(j, i) for i, j in even_pairs])  3.87 us
    ppermute x1, starting transfers between devices, per_device(): recv_far = lax.ppermute(results[2], 'gz', far)  2.78 us
    ppermute x1, waiting for transfers between devices, per_device(): recv_near = lax.ppermute(tail, 'gz', near)  2.72 us
  transfers between devices with their start and end apart: 9, of which 6 were waited for; matrix products, arithmetic and copies ran while one was open for 0% of the time, Pallas kernels for 5%

profile of v6, /device:TPU:378, one launch (start us, length us, event | category | flops | bytes accessed | tf_op | source)
XLA Modules:
  0.0 47.6 jit_solution(3687238910471343368)
XLA Ops:
  1.3 3.9 %shard_map.68 = (f32[200,128]{1,0:T(8,128)S(1)}, f32[200,128]{1,0:T(8,128)S(1)}, f32[40,128]{1,0:T(8,128)S(1)}, f32[40,128]{1,0:T(8,128)S(1)}) custom-call(s32[1]{0:T(128)S(6)} %copy.15.counts_ref, f32[28,2048]{1,0:T(8,128)} %part_ref.1, s32[3,2048]{1,0:T(4,128)} %base_ref.1, f32[8,2048]{1,0:T(8,128)} %w_ref.1, f32[3,8,2048]{2,1,0:T(8,128)} %g_ref.1), custom_call_target="tpu_custom_call" | custom-call | bytes 2000000 | tf_op jit(solution)/shard_map/pallas_call | solution.py:554
  5.2 3.1 %collective-permute-start = (f32[40,128]{1,0:T(8,128)S(1)}, f32[40,128]{1,0:T(8,128)S(1)}, u32[]{:S(2)}, u32[]{:S(2)}) collective-permute-start(f32[40,128]{1,0:T(8,128)S(1)} %get-tuple-element.24), channel_id=1, source_target_pairs={{1,2},{3,4},{5,6},{7,8},{9,10},{11,12},{13,14},{2,1},{4,3},{6,5},{... | collective-permute-start | bytes 61448 | tf_op jit(solution)/shard_map/ppermute | solution.py:570
  8.3 2.0 %collective-permute-start.1 = (f32[40,128]{1,0:T(8,128)S(1)}, f32[40,128]{1,0:T(8,128)S(1)}, u32[]{:S(2)}, u32[]{:S(2)}) collective-permute-start(f32[40,128]{1,0:T(8,128)S(1)} %get-tuple-element.25), channel_id=1, source_target_pairs={{0,1},{2,3},{4,5},{6,7},{8,9},{10,11},{12,13},{14,15},{1,0},{3,2},... | collective-permute-start | bytes 61448 | tf_op jit(solution)/shard_map/ppermute | solution.py:571
  10.2 2.8 %collective-permute-done.refs_2_ = f32[40,128]{1,0:T(8,128)S(1)} collective-permute-done((f32[40,128]{1,0:T(8,128)S(1)}, f32[40,128]{1,0:T(8,128)S(1)}, u32[]{:S(2)}, u32[]{:S(2)}) %collective-permute-start) | collective-permute-done | bytes 20512 | tf_op jit(solution)/shard_map/ppermute | solution.py:570
  13.0 1.0 %collective-permute-done.1.refs_3_ = f32[40,128]{1,0:T(8,128)S(1)} collective-permute-done((f32[40,128]{1,0:T(8,128)S(1)}, f32[40,128]{1,0:T(8,128)S(1)}, u32[]{:S(2)}, u32[]{:S(2)}) %collective-permute-start.1) | collective-permute-done | bytes 20512 | tf_op jit(solution)/shard_map/ppermute | solution.py:571
  14.0 0.0 copy-start
  14.0 0.2 shard_map.69
  14.2 0.0 copy-start.1
  14.2 0.8 %collective-permute-start.2 = (f32[80,128]{1,0:T(8,128)S(1)}, f32[80,128]{1,0:T(8,128)S(1)}, u32[]{:S(2)}, u32[]{:S(2)}) collective-permute-start(f32[80,128]{1,0:T(8,128)S(1)} %get-tuple-element.29), channel_id=1, source_target_pairs={{0,16},{16,0},{1,17},{17,1},{2,18},{18,2},{3,19},{19,3},{4,20},{20... | collective-permute-start | bytes 122888 | tf_op jit(solution)/shard_map/ppermute | solution.py:606
  15.0 4.6 %collective-permute-start.3 = (f32[80,128]{1,0:T(8,128)S(1)}, f32[80,128]{1,0:T(8,128)S(1)}, u32[]{:S(2)}, u32[]{:S(2)}) collective-permute-start(f32[80,128]{1,0:T(8,128)S(1)} %get-tuple-element.30), channel_id=1, source_target_pairs={{16,32},{32,16},{17,33},{33,17},{18,34},{34,18},{19,35},{35,19},{2... | collective-permute-start | bytes 122888 | tf_op jit(solution)/shard_map/ppermute | solution.py:606
  19.6 1.9 %collective-permute-start.4 = (f32[80,128]{1,0:T(8,128)S(1)}, f32[80,128]{1,0:T(8,128)S(1)}, u32[]{:S(2)}, u32[]{:S(2)}) collective-permute-start(f32[80,128]{1,0:T(8,128)S(1)} %get-tuple-element.31), channel_id=1, source_target_pairs={{32,48},{48,32},{33,49},{49,33},{34,50},{50,34},{35,51},{51,35},{3... | collective-permute-start | bytes 122888 | tf_op jit(solution)/shard_map/ppermute | solution.py:606
  21.5 0.0 collective-permute-done.2.refs_2_
  21.5 3.2 %collective-permute-done.3.refs_3_ = f32[80,128]{1,0:T(8,128)S(1)} collective-permute-done((f32[80,128]{1,0:T(8,128)S(1)}, f32[80,128]{1,0:T(8,128)S(1)}, u32[]{:S(2)}, u32[]{:S(2)}) %collective-permute-start.3) | collective-permute-done | bytes 40992 | tf_op jit(solution)/shard_map/ppermute | solution.py:606
  24.8 4.6 %collective-permute-done.4.refs_4_ = f32[80,128]{1,0:T(8,128)S(1)} collective-permute-done((f32[80,128]{1,0:T(8,128)S(1)}, f32[80,128]{1,0:T(8,128)S(1)}, u32[]{:S(2)}, u32[]{:S(2)}) %collective-permute-start.4) | collective-permute-done | bytes 40992 | tf_op jit(solution)/shard_map/ppermute | solution.py:606
  29.4 0.0 copy-start.2
  29.4 0.1 shard_map.70
  29.5 1.9 %collective-permute-start.5 = (f32[192,128]{1,0:T(8,128)S(1)}, f32[192,128]{1,0:T(8,128)S(1)}, u32[]{:S(2)}, u32[]{:S(2)}) collective-permute-start(f32[192,128]{1,0:T(8,128)S(1)} %get-tuple-element.34), channel_id=1, source_target_pairs={{64,128},{192,256},{320,384},{128,64},{256,192},{384,320},{65,129}... | collective-permute-start | bytes 294920 | tf_op jit(solution)/shard_map/ppermute | solution.py:570
  31.4 1.9 %collective-permute-start.6 = (f32[192,128]{1,0:T(8,128)S(1)}, f32[192,128]{1,0:T(8,128)S(1)}, u32[]{:S(2)}, u32[]{:S(2)}) collective-permute-start(f32[192,128]{1,0:T(8,128)S(1)} %get-tuple-element.35), channel_id=1, source_target_pairs={{0,64},{128,192},{256,320},{384,448},{64,0},{192,128},{320,256},{4... | collective-permute-start | bytes 294920 | tf_op jit(solution)/shard_map/ppermute | solution.py:571
  33.4 2.1 %collective-permute-done.5.refs_2_ = f32[192,128]{1,0:T(8,128)S(1)} collective-permute-done((f32[192,128]{1,0:T(8,128)S(1)}, f32[192,128]{1,0:T(8,128)S(1)}, u32[]{:S(2)}, u32[]{:S(2)}) %collective-permute-start.5) | collective-permute-done | bytes 98336 | tf_op jit(solution)/shard_map/ppermute | solution.py:570
  35.4 0.0 collective-permute-done.6.refs_3_
  35.4 0.0 copy-done
  35.4 0.0 copy-done.1
  35.4 0.0 copy-done.2
  35.5 0.0 copy-done.3
  35.5 2.1 %shard_map.71 = (f32[8,16,32]{2,1,0:T(8,128)}, bf16[1280,256]{1,0:T(8,128)(2,1)S(1)}, f32[152,128]{1,0:T(8,128)S(1)}) custom-call(f32[10,32,128]{2,1,0:T(8,128)S(1)} %get-tuple-element.32.refs_0_, f32[10,32,128]{2,1,0:T(8,128)S(1)} %get-tuple-element.33.refs_1_, f32[192,128]{1,0:T(8,128)S(1)} %collective-permute-done.5.refs_2_, ...), custom_call_target="tpu_custom_call" | custom-call | bytes 2000000 | tf_op jit(solution)/shard_map/pallas_call | solution.py:554
  37.6 2.8 %collective-permute-start.8 = (f32[152,128]{1,0:T(8,128)S(1)}, f32[152,128]{1,0:T(8,128)S(1)}, u32[]{:S(2)}, u32[]{:S(2)}) collective-permute-start(f32[152,128]{1,0:T(8,128)S(1)} %get-tuple-element.38.refs_10_), channel_id=1, source_target_pairs={{3,4},{7,8},{11,12},{15,0},{19,20},{23,24},{27,28},{31,16},{35,36}... | collective-permute-start | bytes 233480 | tf_op jit(solution)/shard_map/ppermute | solution.py:637
  40.4 1.3 %collective-permute-start.7 = (f32[152,128]{1,0:T(8,128)S(1)}, f32[152,128]{1,0:T(8,128)S(1)}, u32[]{:S(2)}, u32[]{:S(2)}) collective-permute-start(f32[152,128]{1,0:T(8,128)S(1)} %get-tuple-element.39.tail_ref), channel_id=1, source_target_pairs={{0,1},{1,2},{2,3},{4,5},{5,6},{6,7},{8,9},{9,10},{10,11},{12,13},{... | collective-permute-start | bytes 233480 | tf_op jit(solution)/shard_map/ppermute | solution.py:639
  41.7 2.2 %shard_map.73.refs_2_ = f32[28,3072]{1,0:T(8,128)} custom-call(s32[1]{0:T(128)S(6)} %copy.15.counts_ref, f32[8,128]{1,0:T(8,128)S(1)} %get-tuple-element.26.prior_ref.refs_0_, bf16[1280,256]{1,0:T(8,128)(2,1)S(1)} %get-tuple-element.40.nodes_ref, f32[152,128]{1,0:T(8,128)S(1)} %get-tuple-element.39.tail_ref, f32[28,2048]{1,0:T(8,128)S(1)} %copy-done, ...), custom_call_target="tpu_custom_call" | custom-call | flops 671088640 | bytes 2000000 | tf_op jit(solution)/shard_map/pallas_call | solution.py:554
  43.9 0.0 collective-permute-done.8.refs_1_
  43.9 0.1 shard_map.74.refs_2_
  44.0 2.7 %collective-permute-done.7.refs_1_ = f32[152,128]{1,0:T(8,128)S(1)} collective-permute-done((f32[152,128]{1,0:T(8,128)S(1)}, f32[152,128]{1,0:T(8,128)S(1)}, u32[]{:S(2)}, u32[]{:S(2)}) %collective-permute-start.7) | collective-permute-done | bytes 77856 | tf_op jit(solution)/shard_map/ppermute | solution.py:639
  46.7 0.8 %shard_map.75 = f32[28,3072]{1,0:T(8,128)} custom-call(f32[8,128]{1,0:T(8,128)S(1)} %get-tuple-element.26.prior_ref.refs_0_, f32[152,128]{1,0:T(8,128)S(1)} %collective-permute-done.7.refs_1_, f32[28,3072]{1,0:T(8,128)} %shard_map.74.refs_2_), custom_call_target="tpu_custom_call", output_to_operand_aliasing={{}: (2, {})} | custom-call | bytes 2000000 | tf_op jit(solution)/shard_map/pallas_call | solution.py:554
  (2 shorter events, 0.0 us)
Async XLA Ops:
  5.2 7.8 %collective-permute-start = (f32[40,128]{1,0:T(8,128)S(1)}, f32[40,128]{1,0:T(8,128)S(1)}, u32[]{:S(2)}, u32[]{:S(2)}) collective-permute-start(f32[40,128]{1,0:T(8,128)S(1)} %get-tuple-element.24), channel_id=1, source_target_pairs={{1,2},{3,4},{5,6},{7,8},{9,10},{11,12},{13,14},{2,1},{4,3},{6,5},{... | collective-permute-start | bytes 61448 | tf_op jit(solution)/shard_map/ppermute | solution.py:570
  8.3 5.7 %collective-permute-start.1 = (f32[40,128]{1,0:T(8,128)S(1)}, f32[40,128]{1,0:T(8,128)S(1)}, u32[]{:S(2)}, u32[]{:S(2)}) collective-permute-start(f32[40,128]{1,0:T(8,128)S(1)} %get-tuple-element.25), channel_id=1, source_target_pairs={{0,1},{2,3},{4,5},{6,7},{8,9},{10,11},{12,13},{14,15},{1,0},{3,2},... | collective-permute-start | bytes 61448 | tf_op jit(solution)/shard_map/ppermute | solution.py:571
  14.0 21.5 %copy-start = (f32[28,2048]{1,0:T(8,128)S(1)}, f32[28,2048]{1,0:T(8,128)}, u32[]{:S(2)}) copy-start(f32[28,2048]{1,0:T(8,128)} %part_ref.1) | copy-start | bytes 688132
  14.2 21.3 %copy-start.1 = (f32[3,8,2048]{2,1,0:T(8,128)S(1)}, f32[3,8,2048]{2,1,0:T(8,128)}, u32[]{:S(2)}) copy-start(f32[3,8,2048]{2,1,0:T(8,128)} %g_ref.1) | copy-start | bytes 589828
  14.2 7.3 %collective-permute-start.2 = (f32[80,128]{1,0:T(8,128)S(1)}, f32[80,128]{1,0:T(8,128)S(1)}, u32[]{:S(2)}, u32[]{:S(2)}) collective-permute-start(f32[80,128]{1,0:T(8,128)S(1)} %get-tuple-element.29), channel_id=1, source_target_pairs={{0,16},{16,0},{1,17},{17,1},{2,18},{18,2},{3,19},{19,3},{4,20},{20... | collective-permute-start | bytes 122888 | tf_op jit(solution)/shard_map/ppermute | solution.py:606
  15.0 9.8 %collective-permute-start.3 = (f32[80,128]{1,0:T(8,128)S(1)}, f32[80,128]{1,0:T(8,128)S(1)}, u32[]{:S(2)}, u32[]{:S(2)}) collective-permute-start(f32[80,128]{1,0:T(8,128)S(1)} %get-tuple-element.30), channel_id=1, source_target_pairs={{16,32},{32,16},{17,33},{33,17},{18,34},{34,18},{19,35},{35,19},{2... | collective-permute-start | bytes 122888 | tf_op jit(solution)/shard_map/ppermute | solution.py:606
  19.6 9.8 %collective-permute-start.4 = (f32[80,128]{1,0:T(8,128)S(1)}, f32[80,128]{1,0:T(8,128)S(1)}, u32[]{:S(2)}, u32[]{:S(2)}) collective-permute-start(f32[80,128]{1,0:T(8,128)S(1)} %get-tuple-element.31), channel_id=1, source_target_pairs={{32,48},{48,32},{33,49},{49,33},{34,50},{50,34},{35,51},{51,35},{3... | collective-permute-start | bytes 122888 | tf_op jit(solution)/shard_map/ppermute | solution.py:606
  29.4 6.0 %copy-start.2 = (f32[8,2048]{1,0:T(8,128)S(1)}, f32[8,2048]{1,0:T(8,128)}, u32[]{:S(2)}) copy-start(f32[8,2048]{1,0:T(8,128)} %w_ref.1) | copy-start | bytes 196612
  29.4 6.0 %copy-start.3 = (s32[3,2048]{1,0:T(4,128)S(1)}, s32[3,2048]{1,0:T(4,128)}, u32[]{:S(2)}) copy-start(s32[3,2048]{1,0:T(4,128)} %base_ref.1) | copy-start | bytes 73732
  29.5 5.9 %collective-permute-start.5 = (f32[192,128]{1,0:T(8,128)S(1)}, f32[192,128]{1,0:T(8,128)S(1)}, u32[]{:S(2)}, u32[]{:S(2)}) collective-permute-start(f32[192,128]{1,0:T(8,128)S(1)} %get-tuple-element.34), channel_id=1, source_target_pairs={{64,128},{192,256},{320,384},{128,64},{256,192},{384,320},{65,129}... | collective-permute-start | bytes 294920 | tf_op jit(solution)/shard_map/ppermute | solution.py:570
  31.4 4.0 %collective-permute-start.6 = (f32[192,128]{1,0:T(8,128)S(1)}, f32[192,128]{1,0:T(8,128)S(1)}, u32[]{:S(2)}, u32[]{:S(2)}) collective-permute-start(f32[192,128]{1,0:T(8,128)S(1)} %get-tuple-element.35), channel_id=1, source_target_pairs={{0,64},{128,192},{256,320},{384,448},{64,0},{192,128},{320,256},{4... | collective-permute-start | bytes 294920 | tf_op jit(solution)/shard_map/ppermute | solution.py:571
  37.6 6.3 %collective-permute-start.8 = (f32[152,128]{1,0:T(8,128)S(1)}, f32[152,128]{1,0:T(8,128)S(1)}, u32[]{:S(2)}, u32[]{:S(2)}) collective-permute-start(f32[152,128]{1,0:T(8,128)S(1)} %get-tuple-element.38.refs_10_), channel_id=1, source_target_pairs={{3,4},{7,8},{11,12},{15,0},{19,20},{23,24},{27,28},{31,16},{35,36}... | collective-permute-start | bytes 233480 | tf_op jit(solution)/shard_map/ppermute | solution.py:637
  40.4 6.3 %collective-permute-start.7 = (f32[152,128]{1,0:T(8,128)S(1)}, f32[152,128]{1,0:T(8,128)S(1)}, u32[]{:S(2)}, u32[]{:S(2)}) collective-permute-start(f32[152,128]{1,0:T(8,128)S(1)} %get-tuple-element.39.tail_ref), channel_id=1, source_target_pairs={{0,1},{1,2},{2,3},{4,5},{5,6},{6,7},{8,9},{9,10},{10,11},{12,13},{... | collective-permute-start | bytes 233480 | tf_op jit(solution)/shard_map/ppermute | solution.py:639

commit v7 on v6

--- a/solution.py
+++ b/solution.py
@@ -37,6 +37,8 @@
 AROWS = 176
 GROWS = 200
 GROUP = 40
+REACH = tuple(max(i - 1, 0) for i in range(LAYERS))
+ROWS_AT = tuple(sum(SY - 2 * r for r in REACH[:i]) for i in range(LAYERS + 1))
 HALF = 104
 PACK = SX // 3
 ZROWS = 40
@@ -248,9 +250,10 @@
         even_ref[rows, :] = jnp.where(is_even, high, low)
 
     for x in range(LAYERS):
-        put(slice(SY * x, SY * (x + 1)), deep_out[x, 0:SY, :], deep_out[EX - LAYERS + x, 0:SY, :])
+        rows = slice(REACH[x], SY - REACH[x])
+        put(slice(ROWS_AT[x], ROWS_AT[x + 1]), deep_out[x, rows, :], deep_out[EX - 1 - x, rows, :])
     for x in range(2):
-        at = SY * LAYERS + EY * x
+        at = ROWS_AT[LAYERS] + EY * x
         put(slice(at, at + EY), vel_out[x, OFF : OFF + EY, :], vel_out[EX - 2 + x, OFF : OFF + EY, :])
 
 
@@ -417,10 +420,11 @@
         if OFF <= xd < OFF + EX:
             sums_ref[xd] = deep_ref[xd - OFF]
         if xd < LAYERS:
-            sums_ref[xd, 0:SY, :] += before_ref[SY * xd : SY * (xd + 1), :]
+            i = LAYERS - 1 - xd
+            sums_ref[xd, REACH[i] : SY - REACH[i], :] += before_ref[ROWS_AT[i] : ROWS_AT[i + 1], :]
         if xd >= SX - LAYERS:
-            at = SY * (xd - SX + LAYERS)
-            sums_ref[xd, 0:SY, :] += after_ref[at : at + SY, :]
+            i = xd - SX + LAYERS
+            sums_ref[xd, REACH[i] : SY - REACH[i], :] += after_ref[ROWS_AT[i] : ROWS_AT[i + 1], :]
     lane = lane_index(PITCH)
     pos_x = lax.axis_index(AXES[0]) * CX - WIDE + three(lane, SZ, 0, PACK, 2 * PACK)
     pos_y = lax.axis_index(AXES[1]) * CY - WIDE + lax.broadcasted_iota(jnp.int32, (PITCH, 128), 0)
@@ -462,7 +466,7 @@
     move.start()
     fv_ref[...] = jnp.zeros_like(fv_ref)
     fd_ref[...] = jnp.zeros_like(fd_ref)
-    vel_at = SY * LAYERS
+    vel_at = ROWS_AT[LAYERS]
     lane = lane_index(EY)
     for x in range(EX):
         vel = vel_ref[x, OFF : OFF + EY, :]
@@ -604,7 +608,7 @@
         (deep, vel, from_odd, from_even),
     )
     received = [lax.ppermute(messages[i], "gy", [(i, i + 1), (i + 1, i)]) for i in range(pairs)]
-    wide_message = LAYERS * SY + 2 * EY
+    wide_message = ROWS_AT[LAYERS] + 2 * EY
     deep, vel, odd, even = call(
         lambda *refs: join_y_kernel(pairs, *refs),
         (shape(EX, PITCH, 128), shape(EX, PITCH, 128), shape(wide_message, 128), shape(wide_message, 128)),

time: 47.9 us -> 47.9 us (level)
  the two profiles are of different devices: /device:TPU:378 before, /device:TPU:348 now
where the time goes in v7:
time: 47.9 us; the launch traced here: 47.5 us
  starting transfers between devices  21.7 us (45%)
  waiting for transfers between devices  14.9 us (31%)
  Pallas kernels  9.47 us (20%)
  between operations  1.44 us (3%)
    pallas_call x8, Pallas kernels, call(): pl.pallas_call(kernel, out_shape=out_shape, in_specs=[pl.BlockSpec(memory...  9.47 us
    ppermute x3, waiting for transfers between devices, per_device(): lax.ppermute(messages[i], 'gy', [(i, i + 1), (i + 1, i)])  7.87 us
    ppermute x3, starting transfers between devices, per_device(): lax.ppermute(messages[i], 'gy', [(i, i + 1), (i + 1, i)])  6.43 us
    ppermute x2, starting transfers between devices, swap_pairs(): lax.ppermute(even, axis, even_pairs + [(j, i) for i, j in even_pairs])  6.18 us
    ppermute x2, starting transfers between devices, swap_pairs(): lax.ppermute(odd, axis, odd_pairs + [(j, i) for i, j in odd_pairs] + list...  4.68 us
    ppermute x1, starting transfers between devices, per_device(): recv_far = lax.ppermute(results[2], 'gz', far)  3.09 us
    ppermute x2, waiting for transfers between devices, swap_pairs(): lax.ppermute(odd, axis, odd_pairs + [(j, i) for i, j in odd_pairs] + list...  2.76 us
    ppermute x1, waiting for transfers between devices, per_device(): recv_near = lax.ppermute(tail, 'gz', near)  2.72 us
  transfers between devices with their start and end apart: 9, of which 6 were waited for; matrix products, arithmetic and copies ran while one was open for 0% of the time, Pallas kernels for 5%

profile of v7, /device:TPU:348, one launch (start us, length us, event | category | flops | bytes accessed | tf_op | source)
XLA Modules:
  0.0 47.5 jit_solution(8917288106424724757)
XLA Ops:
  1.3 3.9 %shard_map.68 = (f32[200,128]{1,0:T(8,128)S(1)}, f32[200,128]{1,0:T(8,128)S(1)}, f32[40,128]{1,0:T(8,128)S(1)}, f32[40,128]{1,0:T(8,128)S(1)}) custom-call(s32[1]{0:T(128)S(6)} %copy.15.counts_ref, f32[28,2048]{1,0:T(8,128)} %part_ref.1, s32[3,2048]{1,0:T(4,128)} %base_ref.1, f32[8,2048]{1,0:T(8,128)} %w_ref.1, f32[3,8,2048]{2,1,0:T(8,128)} %g_ref.1), custom_call_target="tpu_custom_call" | custom-call | bytes 2000000 | tf_op jit(solution)/shard_map/pallas_call | solution.py:558
  5.2 2.8 %collective-permute-start = (f32[40,128]{1,0:T(8,128)S(1)}, f32[40,128]{1,0:T(8,128)S(1)}, u32[]{:S(2)}, u32[]{:S(2)}) collective-permute-start(f32[40,128]{1,0:T(8,128)S(1)} %get-tuple-element.24), channel_id=1, source_target_pairs={{1,2},{3,4},{5,6},{7,8},{9,10},{11,12},{13,14},{2,1},{4,3},{6,5},{... | collective-permute-start | bytes 61448 | tf_op jit(solution)/shard_map/ppermute | solution.py:574
  8.0 2.2 %collective-permute-start.1 = (f32[40,128]{1,0:T(8,128)S(1)}, f32[40,128]{1,0:T(8,128)S(1)}, u32[]{:S(2)}, u32[]{:S(2)}) collective-permute-start(f32[40,128]{1,0:T(8,128)S(1)} %get-tuple-element.25), channel_id=1, source_target_pairs={{0,1},{2,3},{4,5},{6,7},{8,9},{10,11},{12,13},{14,15},{1,0},{3,2},... | collective-permute-start | bytes 61448 | tf_op jit(solution)/shard_map/ppermute | solution.py:575
  10.3 2.8 %collective-permute-done.refs_2_ = f32[40,128]{1,0:T(8,128)S(1)} collective-permute-done((f32[40,128]{1,0:T(8,128)S(1)}, f32[40,128]{1,0:T(8,128)S(1)}, u32[]{:S(2)}, u32[]{:S(2)}) %collective-permute-start) | collective-permute-done | bytes 20512 | tf_op jit(solution)/shard_map/ppermute | solution.py:574
  13.0 0.7 %collective-permute-done.1.refs_3_ = f32[40,128]{1,0:T(8,128)S(1)} collective-permute-done((f32[40,128]{1,0:T(8,128)S(1)}, f32[40,128]{1,0:T(8,128)S(1)}, u32[]{:S(2)}, u32[]{:S(2)}) %collective-permute-start.1) | collective-permute-done | bytes 20512 | tf_op jit(solution)/shard_map/ppermute | solution.py:575
  13.7 0.2 shard_map.69
  13.9 0.0 copy-start.1
  13.9 0.8 %collective-permute-start.2 = (f32[80,128]{1,0:T(8,128)S(1)}, f32[80,128]{1,0:T(8,128)S(1)}, u32[]{:S(2)}, u32[]{:S(2)}) collective-permute-start(f32[80,128]{1,0:T(8,128)S(1)} %get-tuple-element.29), channel_id=1, source_target_pairs={{0,16},{16,0},{1,17},{17,1},{2,18},{18,2},{3,19},{19,3},{4,20},{20... | collective-permute-start | bytes 122888 | tf_op jit(solution)/shard_map/ppermute | solution.py:610
  14.7 3.7 %collective-permute-start.3 = (f32[80,128]{1,0:T(8,128)S(1)}, f32[80,128]{1,0:T(8,128)S(1)}, u32[]{:S(2)}, u32[]{:S(2)}) collective-permute-start(f32[80,128]{1,0:T(8,128)S(1)} %get-tuple-element.30), channel_id=1, source_target_pairs={{16,32},{32,16},{17,33},{33,17},{18,34},{34,18},{19,35},{35,19},{2... | collective-permute-start | bytes 122888 | tf_op jit(solution)/shard_map/ppermute | solution.py:610
  18.4 1.9 %collective-permute-start.4 = (f32[80,128]{1,0:T(8,128)S(1)}, f32[80,128]{1,0:T(8,128)S(1)}, u32[]{:S(2)}, u32[]{:S(2)}) collective-permute-start(f32[80,128]{1,0:T(8,128)S(1)} %get-tuple-element.31), channel_id=1, source_target_pairs={{32,48},{48,32},{33,49},{49,33},{34,50},{50,34},{35,51},{51,35},{3... | collective-permute-start | bytes 122888 | tf_op jit(solution)/shard_map/ppermute | solution.py:610
  20.3 0.0 collective-permute-done.2.refs_2_
  20.3 5.4 %collective-permute-done.3.refs_3_ = f32[80,128]{1,0:T(8,128)S(1)} collective-permute-done((f32[80,128]{1,0:T(8,128)S(1)}, f32[80,128]{1,0:T(8,128)S(1)}, u32[]{:S(2)}, u32[]{:S(2)}) %collective-permute-start.3) | collective-permute-done | bytes 40992 | tf_op jit(solution)/shard_map/ppermute | solution.py:610
  25.7 2.5 %collective-permute-done.4.refs_4_ = f32[80,128]{1,0:T(8,128)S(1)} collective-permute-done((f32[80,128]{1,0:T(8,128)S(1)}, f32[80,128]{1,0:T(8,128)S(1)}, u32[]{:S(2)}, u32[]{:S(2)}) %collective-permute-start.4) | collective-permute-done | bytes 40992 | tf_op jit(solution)/shard_map/ppermute | solution.py:610
  28.2 0.0 copy-start.2
  28.2 0.0 copy-start.3
  28.2 0.1 shard_map.70
  28.3 1.9 %collective-permute-start.5 = (f32[172,128]{1,0:T(8,128)S(1)}, f32[172,128]{1,0:T(8,128)S(1)}, u32[]{:S(2)}, u32[]{:S(2)}) collective-permute-start(f32[172,128]{1,0:T(8,128)S(1)} %get-tuple-element.34), channel_id=1, source_target_pairs={{64,128},{192,256},{320,384},{128,64},{256,192},{384,320},{65,129}... | collective-permute-start | bytes 264200 | tf_op jit(solution)/shard_map/ppermute | solution.py:574
  30.2 3.9 %collective-permute-start.6 = (f32[172,128]{1,0:T(8,128)S(1)}, f32[172,128]{1,0:T(8,128)S(1)}, u32[]{:S(2)}, u32[]{:S(2)}) collective-permute-start(f32[172,128]{1,0:T(8,128)S(1)} %get-tuple-element.35), channel_id=1, source_target_pairs={{0,64},{128,192},{256,320},{384,448},{64,0},{192,128},{320,256},{4... | collective-permute-start | bytes 264200 | tf_op jit(solution)/shard_map/ppermute | solution.py:575
  34.2 0.0 collective-permute-done.5.refs_2_
  34.2 0.9 %collective-permute-done.6.refs_3_ = f32[172,128]{1,0:T(8,128)S(1)} collective-permute-done((f32[172,128]{1,0:T(8,128)S(1)}, f32[172,128]{1,0:T(8,128)S(1)}, u32[]{:S(2)}, u32[]{:S(2)}) %collective-permute-start.6) | collective-permute-done | bytes 88096 | tf_op jit(solution)/shard_map/ppermute | solution.py:575
  35.1 0.0 copy-done
  35.1 0.0 copy-done.1
  35.1 0.0 copy-done.2
  35.1 0.0 copy-done.3
  35.1 2.1 %shard_map.71 = (f32[8,16,32]{2,1,0:T(8,128)}, bf16[1280,256]{1,0:T(8,128)(2,1)S(1)}, f32[152,128]{1,0:T(8,128)S(1)}) custom-call(f32[10,32,128]{2,1,0:T(8,128)S(1)} %get-tuple-element.32.refs_0_, f32[10,32,128]{2,1,0:T(8,128)S(1)} %get-tuple-element.33.refs_1_, f32[172,128]{1,0:T(8,128)S(1)} %collective-permute-done.5.refs_2_, ...), custom_call_target="tpu_custom_call" | custom-call | bytes 2000000 | tf_op jit(solution)/shard_map/pallas_call | solution.py:558
  37.2 3.1 %collective-permute-start.8 = (f32[152,128]{1,0:T(8,128)S(1)}, f32[152,128]{1,0:T(8,128)S(1)}, u32[]{:S(2)}, u32[]{:S(2)}) collective-permute-start(f32[152,128]{1,0:T(8,128)S(1)} %get-tuple-element.38.refs_10_), channel_id=1, source_target_pairs={{3,4},{7,8},{11,12},{15,0},{19,20},{23,24},{27,28},{31,16},{35,36}... | collective-permute-start | bytes 233480 | tf_op jit(solution)/shard_map/ppermute | solution.py:641
  40.4 1.3 %collective-permute-start.7 = (f32[152,128]{1,0:T(8,128)S(1)}, f32[152,128]{1,0:T(8,128)S(1)}, u32[]{:S(2)}, u32[]{:S(2)}) collective-permute-start(f32[152,128]{1,0:T(8,128)S(1)} %get-tuple-element.39.tail_ref), channel_id=1, source_target_pairs={{0,1},{1,2},{2,3},{4,5},{5,6},{6,7},{8,9},{9,10},{10,11},{12,13},{... | collective-permute-start | bytes 233480 | tf_op jit(solution)/shard_map/ppermute | solution.py:643
  41.7 2.2 %shard_map.73.refs_2_ = f32[28,3072]{1,0:T(8,128)} custom-call(s32[1]{0:T(128)S(6)} %copy.15.counts_ref, f32[8,128]{1,0:T(8,128)S(1)} %get-tuple-element.26.prior_ref.refs_0_, bf16[1280,256]{1,0:T(8,128)(2,1)S(1)} %get-tuple-element.40.nodes_ref, f32[152,128]{1,0:T(8,128)S(1)} %get-tuple-element.39.tail_ref, f32[28,2048]{1,0:T(8,128)S(1)} %copy-done, ...), custom_call_target="tpu_custom_call" | custom-call | flops 671088640 | bytes 2000000 | tf_op jit(solution)/shard_map/pallas_call | solution.py:558
  43.8 0.0 collective-permute-done.8.refs_1_
  43.9 0.1 shard_map.74.refs_2_
  44.0 2.7 %collective-permute-done.7.refs_1_ = f32[152,128]{1,0:T(8,128)S(1)} collective-permute-done((f32[152,128]{1,0:T(8,128)S(1)}, f32[152,128]{1,0:T(8,128)S(1)}, u32[]{:S(2)}, u32[]{:S(2)}) %collective-permute-start.7) | collective-permute-done | bytes 77856 | tf_op jit(solution)/shard_map/ppermute | solution.py:643
  46.7 0.8 %shard_map.75 = f32[28,3072]{1,0:T(8,128)} custom-call(f32[8,128]{1,0:T(8,128)S(1)} %get-tuple-element.26.prior_ref.refs_0_, f32[152,128]{1,0:T(8,128)S(1)} %collective-permute-done.7.refs_1_, f32[28,3072]{1,0:T(8,128)} %shard_map.74.refs_2_), custom_call_target="tpu_custom_call", output_to_operand_aliasing={{}: (2, {})} | custom-call | bytes 2000000 | tf_op jit(solution)/shard_map/pallas_call | solution.py:558
  (2 shorter events, 0.0 us)
Async XLA Ops:
  5.2 7.8 %collective-permute-start = (f32[40,128]{1,0:T(8,128)S(1)}, f32[40,128]{1,0:T(8,128)S(1)}, u32[]{:S(2)}, u32[]{:S(2)}) collective-permute-start(f32[40,128]{1,0:T(8,128)S(1)} %get-tuple-element.24), channel_id=1, source_target_pairs={{1,2},{3,4},{5,6},{7,8},{9,10},{11,12},{13,14},{2,1},{4,3},{6,5},{... | collective-permute-start | bytes 61448 | tf_op jit(solution)/shard_map/ppermute | solution.py:574
  8.0 5.7 %collective-permute-start.1 = (f32[40,128]{1,0:T(8,128)S(1)}, f32[40,128]{1,0:T(8,128)S(1)}, u32[]{:S(2)}, u32[]{:S(2)}) collective-permute-start(f32[40,128]{1,0:T(8,128)S(1)} %get-tuple-element.25), channel_id=1, source_target_pairs={{0,1},{2,3},{4,5},{6,7},{8,9},{10,11},{12,13},{14,15},{1,0},{3,2},... | collective-permute-start | bytes 61448 | tf_op jit(solution)/shard_map/ppermute | solution.py:575
  13.7 21.4 %copy-start = (f32[28,2048]{1,0:T(8,128)S(1)}, f32[28,2048]{1,0:T(8,128)}, u32[]{:S(2)}) copy-start(f32[28,2048]{1,0:T(8,128)} %part_ref.1) | copy-start | bytes 688132
  13.9 21.2 %copy-start.1 = (f32[3,8,2048]{2,1,0:T(8,128)S(1)}, f32[3,8,2048]{2,1,0:T(8,128)}, u32[]{:S(2)}) copy-start(f32[3,8,2048]{2,1,0:T(8,128)} %g_ref.1) | copy-start | bytes 589828
  13.9 6.5 %collective-permute-start.2 = (f32[80,128]{1,0:T(8,128)S(1)}, f32[80,128]{1,0:T(8,128)S(1)}, u32[]{:S(2)}, u32[]{:S(2)}) collective-permute-start(f32[80,128]{1,0:T(8,128)S(1)} %get-tuple-element.29), channel_id=1, source_target_pairs={{0,16},{16,0},{1,17},{17,1},{2,18},{18,2},{3,19},{19,3},{4,20},{20... | collective-permute-start | bytes 122888 | tf_op jit(solution)/shard_map/ppermute | solution.py:610
  14.7 11.1 %collective-permute-start.3 = (f32[80,128]{1,0:T(8,128)S(1)}, f32[80,128]{1,0:T(8,128)S(1)}, u32[]{:S(2)}, u32[]{:S(2)}) collective-permute-start(f32[80,128]{1,0:T(8,128)S(1)} %get-tuple-element.30), channel_id=1, source_target_pairs={{16,32},{32,16},{17,33},{33,17},{18,34},{34,18},{19,35},{35,19},{2... | collective-permute-start | bytes 122888 | tf_op jit(solution)/shard_map/ppermute | solution.py:610
  18.4 9.8 %collective-permute-start.4 = (f32[80,128]{1,0:T(8,128)S(1)}, f32[80,128]{1,0:T(8,128)S(1)}, u32[]{:S(2)}, u32[]{:S(2)}) collective-permute-start(f32[80,128]{1,0:T(8,128)S(1)} %get-tuple-element.31), channel_id=1, source_target_pairs={{32,48},{48,32},{33,49},{49,33},{34,50},{50,34},{35,51},{51,35},{3... | collective-permute-start | bytes 122888 | tf_op jit(solution)/shard_map/ppermute | solution.py:610
  28.2 6.9 %copy-start.2 = (f32[8,2048]{1,0:T(8,128)S(1)}, f32[8,2048]{1,0:T(8,128)}, u32[]{:S(2)}) copy-start(f32[8,2048]{1,0:T(8,128)} %w_ref.1) | copy-start | bytes 196612
  28.2 6.9 %copy-start.3 = (s32[3,2048]{1,0:T(4,128)S(1)}, s32[3,2048]{1,0:T(4,128)}, u32[]{:S(2)}) copy-start(s32[3,2048]{1,0:T(4,128)} %base_ref.1) | copy-start | bytes 73732
  28.3 5.9 %collective-permute-start.5 = (f32[172,128]{1,0:T(8,128)S(1)}, f32[172,128]{1,0:T(8,128)S(1)}, u32[]{:S(2)}, u32[]{:S(2)}) collective-permute-start(f32[172,128]{1,0:T(8,128)S(1)} %get-tuple-element.34), channel_id=1, source_target_pairs={{64,128},{192,256},{320,384},{128,64},{256,192},{384,320},{65,129}... | collective-permute-start | bytes 264200 | tf_op jit(solution)/shard_map/ppermute | solution.py:574
  30.2 4.8 %collective-permute-start.6 = (f32[172,128]{1,0:T(8,128)S(1)}, f32[172,128]{1,0:T(8,128)S(1)}, u32[]{:S(2)}, u32[]{:S(2)}) collective-permute-start(f32[172,128]{1,0:T(8,128)S(1)} %get-tuple-element.35), channel_id=1, source_target_pairs={{0,64},{128,192},{256,320},{384,448},{64,0},{192,128},{320,256},{4... | collective-permute-start | bytes 264200 | tf_op jit(solution)/shard_map/ppermute | solution.py:575
  37.2 6.6 %collective-permute-start.8 = (f32[152,128]{1,0:T(8,128)S(1)}, f32[152,128]{1,0:T(8,128)S(1)}, u32[]{:S(2)}, u32[]{:S(2)}) collective-permute-start(f32[152,128]{1,0:T(8,128)S(1)} %get-tuple-element.38.refs_10_), channel_id=1, source_target_pairs={{3,4},{7,8},{11,12},{15,0},{19,20},{23,24},{27,28},{31,16},{35,36}... | collective-permute-start | bytes 233480 | tf_op jit(solution)/shard_map/ppermute | solution.py:641
  40.4 6.3 %collective-permute-start.7 = (f32[152,128]{1,0:T(8,128)S(1)}, f32[152,128]{1,0:T(8,128)S(1)}, u32[]{:S(2)}, u32[]{:S(2)}) collective-permute-start(f32[152,128]{1,0:T(8,128)S(1)} %get-tuple-element.39.tail_ref), channel_id=1, source_target_pairs={{0,1},{1,2},{2,3},{4,5},{5,6},{6,7},{8,9},{9,10},{10,11},{12,13},{... | collective-permute-start | bytes 233480 | tf_op jit(solution)/shard_map/ppermute | solution.py:643
